TPU v7x, 512 devices: a whole 4x4x16 slice. The times are simulated.
512 devices in a mesh: dom: 128 (over y, z, core), ply: 4 (over x).
Axes of the slice: x: 4, y: 4, z: 16, core: 2. Of those that a mesh axis runs over, the one named last changes fastest.
Arguments:
- state_dofs: float32 [9, 35, 65536], P(None, None, ('dom', 'ply')), may hold values from -6 to 6
- star_matrices: bfloat16 [3, 9, 9, 65536], P(None, None, None, ('dom', 'ply')), may hold values from -0.359375 to 0.359375
- flux_solvers: bfloat16 [2, 4, 9, 9, 65536], P(None, None, None, None, ('dom', 'ply')), may hold values from -0.8984375 to 0.8984375
- cluster_ids: int32 [65536], P(('dom', 'ply')), may hold values from 0 to 1, as said below
- neighbour_faces: int32 [4, 65536], P(None, ('dom', 'ply')), may hold values from -1 to 511, as said below
- face_orient: int32 [4, 65536], P(None, ('dom', 'ply')), may hold values from 0 to 2
- plane_cut_faces: int32 [512, 1024], P(('dom', 'ply')), may hold values from -1 to 511, as said below
- thickness_faces: int32 [1024, 16], P(('dom', 'ply')), may hold values from 0 to 511, as said below
- stiffness: float32 [3, 35, 35], replicated, may hold values from -6 to 6, as said below
- trace_maps: float32 [4, 15, 35], replicated, may hold values from -1 to 1
- lift_maps: float32 [4, 35, 15], replicated, may hold values from -0.75 to 0.75
- face_rotations: float32 [3, 15, 15], replicated, may hold values from -1.5 to 1.5
Outputs:
- updated_dofs: float32 [9, 35, 65536], P(None, None, ('dom', 'ply'))
Inputs may be any that keep to these rules, and one draw needn't show every extreme that they name: `cluster_ids`: 1 marks an element of the fine cluster, 0 one of the coarse cluster; at most 32 of one device's 128 elements are fine, and some device has exactly 32. `neighbour_faces`: row f, column e of device g's block is face n = f * 128 + e; its entry is the face number m of the same device that shares the face, and the entry of m names n back; -1 where the face is cut between devices or on the boundary. Column b * 8 + s of device g's row names a face number shared with the face at column a * 8 + s of the row of the device with dom index b and the same ply index (a being g's dom index), or -1 where both are unused; the used columns of a block come first; blocks are used only toward dom indices a + 1, a - 1, a + 3, a - 3 and a + 128 / 2 (modulo 128), each of these with one face or more; some blocks are full. A face number appears at most once among a device's plane_cut_faces, thickness_faces and nonnegative neighbour_faces entries. `thickness_faces`: all entries of one device are distinct face numbers; position k of the first row of a device is shared with position k of the second row of the device one ply index lower, position k of the second row with position k of the first row of the device one ply index higher; at the ends of the ply axis those faces are on the boundary. `stiffness`: entry [d, i, j] is zero unless basis function j has a higher polynomial degree than basis function i; the basis functions are ordered by degree, in groups of 1, 3, 6, 10 and 15.
All inputs are finite; a program needn't handle non-finite values.
Results may differ from a plain program's by a relative error of at most 0.00035.
Values sent between devices are 32-bit elements; how exact they have to be, the bound alone decides.
No kernel may reach another device: no remote copies, remote signals or barrier semaphores. Data moves between devices by JAX's collectives and lax.ppermute only.
A program may use at most 128 MiB of HBM per device.

v0:
```python
import jax
import jax.numpy as jnp
from jax import lax
from jax.experimental import pallas as pl
from jax.experimental.pallas import tpu as pltpu
from jax.sharding import PartitionSpec as P

F32, BF16 = jnp.float32, jnp.bfloat16
Q, B, A, ORDER = 9, 35, 15, 5
E = 128
PAD = 48
AP = 16
SLOT, LAY = 8, 16
CUTS = 5 * SLOT + 2 * LAY
CP = 80
WIDE = Q * E
ALL = 4 * E

EARLY = [0.5 ** (k + 1) for k in range(ORDER)]
LATE = [1.0 - 0.5 ** (k + 1) for k in range(ORDER)]
FACT = [1.0, 2.0, 6.0, 24.0, 120.0]
STEPS = [(24, 48), (16, 32), (8, 16), (8, 16)]


def dot(a, b):
    return jnp.dot(a, b, preferred_element_type=F32)


def halves(x):
    top = x.astype(BF16)
    return top, (x - top.astype(F32)).astype(BF16)


def tripled(a):
    top = a.astype(BF16).astype(F32)
    return jnp.concatenate([top, top, a - top], axis=1).astype(BF16)


def padded(a, rows, cols):
    r, c = a.shape
    if c < cols:
        a = jnp.concatenate([a, jnp.zeros((r, cols - c), a.dtype)], axis=1)
    if r < rows:
        a = jnp.concatenate([a, jnp.zeros((rows - r, cols), a.dtype)], axis=0)
    return a


def lanes(p):
    return slice(p * E, (p + 1) * E)


def put_stack(ref, rows, p, value):
    top, rest = halves(value)
    ref[0:rows, lanes(p)] = top
    ref[rows : 2 * rows, lanes(p)] = rest
    ref[2 * rows : 3 * rows, lanes(p)] = top


def stiff_rows(stiffness, rows, cols):
    blocks = [
        tripled(padded(stiffness[d], PAD, PAD)[:rows, :cols]).astype(F32) for d in range(3)
    ]
    return jnp.concatenate(blocks, axis=0).astype(BF16)


def trace_rows(trace_maps):
    blocks = [tripled(padded(trace_maps[:, f, :], AP, PAD)).astype(F32) for f in range(4)]
    return jnp.concatenate(blocks, axis=0).astype(BF16)


def volume_rows(stiffness):
    blocks = [tripled(padded(stiffness[d].T, 40, PAD)).astype(F32) for d in range(3)]
    return jnp.concatenate(blocks, axis=0).astype(BF16)


def lift_rows(lift_maps):
    return tripled(jnp.concatenate([padded(lift_maps[:, f, :].T, 40, AP) for f in range(4)], axis=1))


def turn_rows(face_rotations):
    blocks = [tripled(padded(face_rotations[h], AP, AP)).astype(F32) for h in range(3)]
    return jnp.concatenate(blocks, axis=0).astype(BF16)


def widen(source, target, blocks):
    for n in range(blocks):
        target[n] = source[n].astype(F32)


def star_apply(y, stars, rows):
    def one(p, total):
        total = list(total)
        at = pl.ds(pl.multiple_of(p * E, E), E)
        for d in range(3):
            value = y[d * rows : (d + 1) * rows, at]
            for q in range(Q):
                total[q] = total[q] + stars[q * Q + p, d : d + 1, :] * value
        return tuple(total)

    return lax.fori_loop(0, Q, one, tuple(jnp.zeros((rows, E), F32) for _ in range(Q)))


def taylor(first, steps, stars, x, y, add):
    values = [first[q] for q in range(Q)]
    for k, (rows, reads) in enumerate(STEPS):
        for p in range(Q):
            put_stack(x, reads, p, padded(values[p], reads, E))
        y[0 : 3 * rows, :] = dot(steps[k][...], x[0 : 3 * reads, :])
        values = star_apply(y, stars, rows)
        for q in range(Q):
            add(k + 1, q, rows, values[q])


def far_first(count):
    return (count // 2, count - 3, count - 1, 3, 1)


def shared_faces(plane, thick):
    dom, ply = lax.axis_index("dom"), lax.axis_index("ply")
    count = lax.axis_size("dom")
    odd, high = lax.rem(dom, 2), lax.rem(ply, 2)
    sub = lax.broadcasted_iota(jnp.int32, (SLOT, E), 0)
    groups = []
    for step in far_first(count):
        peer = lax.rem(dom + jnp.where(odd == 0, step, count - step), count)
        groups.append(lambda s, at=peer * SLOT: plane[0, at + s])
    for row in (1 - high, high):
        for half in (0, SLOT):
            groups.append(lambda s, row=row, half=half: thick[row, half + s])
    columns = []
    for face in groups:
        column = jnp.full((SLOT, E), -1, jnp.int32)
        for s in range(SLOT):
            column = jnp.where(sub == s, face(s), column)
        columns.append(column)
    columns.append(jnp.full((SLOT, E), -1, jnp.int32))
    return jnp.concatenate(columns, axis=0)


def pick_shared(plane, thick, hot):
    column = shared_faces(plane, thick)
    lane = lax.broadcasted_iota(jnp.int32, (CP, E), 1)
    for f in range(4):
        hot[:, lanes(f)] = jnp.where(column == lane + f * E, 1.0, 0.0).astype(BF16)


def send_traces(s, hot, l, outs):
    for q in range(Q):
        for f in range(4):
            value = s[f * AP : (f + 1) * AP, lanes(q)]
            for part in range(3):
                piece = value.astype(BF16)
                value = value - piece.astype(F32)
                l[part * Q * AP + q * AP : part * Q * AP + (q + 1) * AP, lanes(f)] = piece
    total = None
    for part in (2, 1, 0):
        piece = lax.dot_general(
            hot[...],
            l[part * Q * AP : (part + 1) * Q * AP, :],
            (((1,), (1,)), ((), ())),
            preferred_element_type=F32,
        )
        total = piece if total is None else total + piece
    at = 0
    for out in outs:
        out[...] = total[at : at + out.shape[0]]
        at += out.shape[0]


def first_kernel(state, star, stiffness, trace_maps, plane, thick,
                 x_out, s_out, coarse, hot, stars, step1, step2, step3, step4, traces, *rest):
    sends = rest[:7]
    (stiff_here, trace_here, star_here, state_here, plane_here, thick_here, sems,
     first, early, x, y, l) = rest[7:]
    here = (stiff_here, trace_here, star_here, state_here, plane_here, thick_here)
    there = (stiffness, trace_maps, star, state, plane, thick)
    copies = [
        pltpu.make_async_copy(source, target, sems.at[n])
        for n, (source, target) in enumerate(zip(there, here))
    ]
    for copy in copies:
        copy.start()
    first[...] = jnp.zeros_like(first)
    copies[0].wait()
    steps = (step1, step2, step3, step4)
    for step, (rows, reads) in zip(steps, STEPS):
        step[...] = stiff_rows(stiff_here, rows, reads)
    copies[1].wait()
    traces[...] = trace_rows(trace_here)
    for copy in copies[2:]:
        copy.wait()
    pick_shared(plane_here, thick_here, hot)
    widen(star_here, stars, Q * Q)
    first[:, 0:B, :] = state_here[...]
    early[...] = first[...] * EARLY[0]
    coarse[...] = first[:, 0:40, :] * LATE[0]

    def add(k, q, rows, value):
        sign = -1.0 if k % 2 else 1.0
        early[q, 0:rows, :] = early[q, 0:rows, :] + value * (sign * EARLY[k] / FACT[k])
        coarse[q, 0:rows, :] = coarse[q, 0:rows, :] + value * (sign * LATE[k] / FACT[k])

    taylor(first, steps, stars, x, y, add)
    for p in range(Q):
        put_stack(x_out, PAD, p, early[p])
    s_out[...] = dot(traces[...], x_out[...])
    send_traces(s_out, hot, l, sends)


def own_part(base, x, s, stars, solvers, volumes, same, held, own, picked, y, l):
    for q in range(Q):
        for f in range(4):
            top, rest = halves(s[f * AP : (f + 1) * AP, lanes(q)])
            l[q * AP : (q + 1) * AP, lanes(f)] = top
            l[Q * AP + q * AP : Q * AP + (q + 1) * AP, lanes(f)] = rest
    picked[...] = dot(l[...], same[...])
    y[...] = dot(volumes[...], x[...])
    sums = star_apply(y, stars, 40)
    for q in range(Q):
        held[q] = base(q) + sums[q]
    fluxes(solvers, 0, s, own, None)


def fluxes(solvers, side, values, g, before):
    for f in range(4):
        rows = slice(f * AP, (f + 1) * AP)

        def face(p, total):
            total = list(total)
            at = pl.ds(pl.multiple_of(p * E, E), E)
            value = values[rows, at]
            for q in range(Q):
                total[q] = total[q] + solvers[(side * Q + q) * Q + p, f : f + 1, :] * value
            return tuple(total)

        start = [jnp.zeros((AP, E), F32) if before is None else before[rows, lanes(q)] for q in range(Q)]
        total = lax.fori_loop(0, Q, face, tuple(start))
        for q in range(Q):
            g[rows, lanes(q)] = total[q]


def early_own_kernel(state, x, s, stars, flux, neighbour, stiffness, lift_maps, rotations,
                     held, own, picked, solvers, same, volumes, lifts, turns, padded_state, y, l):
    widen(flux, solvers, 2 * Q * Q)
    sub = lax.broadcasted_iota(jnp.int32, (ALL, E), 0)
    for f in range(4):
        same[:, lanes(f)] = jnp.where(sub == neighbour[f : f + 1, :], 1.0, 0.0).astype(BF16)
    volumes[...] = volume_rows(stiffness)
    lifts[...] = lift_rows(lift_maps)
    turns[...] = turn_rows(rotations)
    padded_state[...] = jnp.zeros_like(padded_state)
    padded_state[:, 0:B, :] = state[...]
    own_part(lambda q: padded_state[q], x, s, stars, solvers, volumes, same, held, own, picked, y, l)


def late_own_kernel(middle, x, s, stars, solvers, volumes, same, held, own, picked, y, l):
    own_part(lambda q: middle[q], x, s, stars, solvers, volumes, same, held, own, picked, y, l)


def finished(held, own, picked, arrived, hot, orient, solvers, lifts, turns, turned_in, o, g):
    landed = jnp.concatenate(
        [ref[...] for ref in arrived] + [jnp.zeros((CP - CUTS, Q * AP), F32)], axis=0
    )
    both = [
        picked[part * Q * AP : (part + 1) * Q * AP, :]
        + lax.dot_general(
            piece, hot[...], (((0,), (0,)), ((), ())), preferred_element_type=F32
        )
        for part, piece in enumerate(halves(landed))
    ]
    for q in range(Q):
        cols = slice(q * ALL, (q + 1) * ALL)
        top = both[0][q * AP : (q + 1) * AP].astype(BF16)
        turned_in[0:AP, cols] = top
        turned_in[AP : 2 * AP, cols] = both[1][q * AP : (q + 1) * AP].astype(BF16)
        turned_in[2 * AP : 3 * AP, cols] = top
    for q in range(Q):
        turned = dot(turns[...], turned_in[:, q * ALL : (q + 1) * ALL])
        for f in range(4):
            way = orient[f : f + 1, :]
            o[f * AP : (f + 1) * AP, lanes(q)] = jnp.where(
                way == 0,
                turned[0:AP, lanes(f)],
                jnp.where(way == 1, turned[AP : 2 * AP, lanes(f)], turned[2 * AP : 3 * AP, lanes(f)]),
            )
    fluxes(solvers, 1, o, g, own)
    results = []
    for q in range(Q):
        top, rest = halves(g[:, lanes(q)])
        results.append(held[q] - dot(lifts[...], jnp.concatenate([top, rest, top], axis=0)))
    return results


def middle_kernel(held, own, picked, coarse, hot, orient, cluster, stars, solvers, lifts, turns,
                  step1, step2, step3, step4, traces, *rest):
    arrived, (middle, x_out, s_out), sends = rest[:7], rest[7:10], rest[10:17]
    first, late, x, y, l, turned_in, o, g = rest[17:]
    values = finished(held, own, picked, arrived, hot, orient, solvers, lifts, turns, turned_in, o, g)
    for q in range(Q):
        first[q] = padded(values[q], PAD, E)
        middle[q] = values[q]
        late[q] = first[q] * EARLY[0]

    def add(k, q, rows, value):
        sign = -1.0 if k % 2 else 1.0
        late[q, 0:rows, :] = late[q, 0:rows, :] + value * (sign * EARLY[k] / FACT[k])

    taylor(first, (step1, step2, step3, step4), stars, x, y, add)
    fine = cluster[...] == 1
    for q in range(Q):
        late[q, 0:40, :] = jnp.where(fine, late[q, 0:40, :], coarse[q])
        put_stack(x_out, PAD, q, late[q])
    s_out[...] = dot(traces[...], x_out[...])
    send_traces(s_out, hot, l, sends)


def last_kernel(held, own, picked, hot, orient, solvers, lifts, turns, *rest):
    arrived, out, (turned_in, o, g) = rest[:7], rest[7], rest[8:]
    values = finished(held, own, picked, arrived, hot, orient, solvers, lifts, turns, turned_in, o, g)
    for q in range(Q):
        out[q] = values[q][0:B]


def shape(dims, kind=F32):
    return jax.ShapeDtypeStruct(dims, kind)


SENDS = [(SLOT, Q * AP)] * 5 + [(LAY, Q * AP)] * 2
PADDED = pltpu.VMEM((Q, PAD, E), F32)
X = pltpu.VMEM((3 * PAD, WIDE), BF16)
Y = pltpu.VMEM((120, WIDE), F32)
TWO = pltpu.VMEM((2 * Q * AP, ALL), BF16)
THREE = pltpu.VMEM((3 * Q * AP, ALL), BF16)
TURNED = pltpu.VMEM((3 * AP, Q * ALL), BF16)
SIDE = pltpu.VMEM((4 * AP, WIDE), F32)


def call(kernel, operands, outs, scratch, flops, memory=pltpu.VMEM, limit=40):
    vmem, source = pl.BlockSpec(memory_space=pltpu.VMEM), pl.BlockSpec(memory_space=memory)
    return pl.pallas_call(
        kernel,
        out_shape=outs,
        in_specs=[source] * len(operands),
        out_specs=jax.tree.map(lambda _: vmem, outs),
        scratch_shapes=scratch,
        compiler_params=pltpu.CompilerParams(vmem_limit_bytes=limit * 1024 * 1024),
        cost_estimate=pl.CostEstimate(flops=flops, bytes_accessed=2_000_000, transcendentals=0),
    )(*operands)


def exchange(blocks):
    count, layers = lax.axis_size("dom"), lax.axis_size("ply")
    landed = []
    for step, block in zip(far_first(count), blocks):
        pairs = []
        for even in range(0, count, 2):
            other = (even + step) % count
            pairs += [(even, other)] + ([(other, even)] if step % 2 else [])
        if step % 2 == 0:
            pairs = [(i, (i + step) % count) for i in range(count)]
        landed.append(lax.ppermute(block, "dom", pairs))
    for start, block in zip((0, 1), blocks[5:]):
        pairs = []
        for low in range(start, layers - 1, 2):
            pairs += [(low, low + 1), (low + 1, low)]
        landed.append(lax.ppermute(block, "ply", pairs))
    return landed


def body(state, star, flux, cluster, neighbour, orient, plane, thick,
         stiffness, trace_maps, lift_maps, rotations):
    star = star.transpose(1, 2, 0, 3).reshape(Q * Q, 3, E)
    flux = flux.transpose(0, 2, 3, 1, 4).reshape(2 * Q * Q, 4, E)
    trace_maps = trace_maps.transpose(1, 0, 2)
    lift_maps = lift_maps.transpose(2, 0, 1)
    cluster = cluster.reshape(1, E)
    kept = [shape((3 * PAD, WIDE), BF16), shape((4 * AP, WIDE)), shape((Q, 40, E))]
    sends = [shape(dims) for dims in SENDS]
    wide = shape((Q * Q, 3, E))
    products = [shape((3 * rows, 3 * reads), BF16) for rows, reads in STEPS]
    products.append(shape((4 * AP, 3 * PAD), BF16))
    own_outs = [kept[2], kept[1], shape((2 * Q * AP, ALL))]
    x_early, s_early, coarse, hot, stars, *rest = call(
        first_kernel, (state, star, stiffness, trace_maps, plane, thick),
        kept + [shape((CP, ALL), BF16), wide] + products + sends,
        [
            pltpu.VMEM(stiffness.shape, F32),
            pltpu.VMEM(trace_maps.shape, F32),
            pltpu.VMEM(star.shape, BF16),
            pltpu.VMEM(state.shape, F32),
            pltpu.SMEM(plane.shape, jnp.int32),
            pltpu.SMEM(thick.shape, jnp.int32),
            pltpu.SemaphoreType.DMA((6,)),
            PADDED, PADDED, X, Y, THREE,
        ],
        100_000_000, pltpu.HBM, 60,
    )
    steps, out_early = rest[:5], rest[5:]
    in_early = exchange(out_early)
    held, own, picked, solvers, same, volumes, lifts, turns = call(
        early_own_kernel,
        (state, x_early, s_early, stars, flux, neighbour, stiffness, lift_maps, rotations),
        own_outs + [
            shape((2 * Q * Q, 4, E)), shape((ALL, ALL), BF16), shape((120, 3 * PAD), BF16),
            shape((40, 12 * AP), BF16), shape((3 * AP, 3 * AP), BF16),
        ],
        [pltpu.VMEM((Q, 40, E), F32), Y, TWO], 200_000_000,
    )
    middle, x_late, s_late, *out_late = call(
        middle_kernel,
        (held, own, picked, coarse, hot, orient, cluster, stars, solvers, lifts, turns, *steps,
         *in_early),
        [kept[2], kept[0], kept[1]] + sends,
        [PADDED, PADDED, X, Y, THREE, TURNED, SIDE, SIDE], 200_000_000,
    )
    in_late = exchange(out_late)
    held, own, picked = call(
        late_own_kernel, (middle, x_late, s_late, stars, solvers, volumes, same), own_outs,
        [Y, TWO], 200_000_000,
    )
    return call(
        last_kernel, (held, own, picked, hot, orient, solvers, lifts, turns, *in_late),
        shape((Q, B, E)), [TURNED, SIDE, SIDE], 100_000_000,
    )


def solution(mesh):
    both = ("dom", "ply")
    in_specs = (
        P(None, None, both),
        P(None, None, None, both),
        P(None, None, None, None, both),
        P(both),
        P(None, both),
        P(None, both),
        P(both, None),
        P(both, None),
        P(),
        P(),
        P(),
        P(),
    )
    return jax.shard_map(
        body, mesh=mesh, in_specs=in_specs, out_specs=P(None, None, both), check_vma=False
    )
```

profile of v0, /device:TPU:2, one launch (start us, length us, event | category | flops | bytes accessed | tf_op | source)
XLA Modules:
  0.0 71.9 jit_solution(11067163229571871026)
XLA Ops:
  0.0 3.9 %shard_map.118 = (bf16[144,1152]{1,0:T(8,128)(2,1)}, f32[64,1152]{1,0:T(8,128)}, f32[9,40,128]{2,1,0:T(8,128)}, bf16[80,512]{1,0:T(8,128)(2,1)}, f32[81,3,128]{2...) custom-call(f32[9,35,128]{2,1,0:T(8,128)} %state.3, ...), custom_call_target="tpu_custom_call" | custom-call | flops 100000000 | bytes 2000000 | tf_op jit(solution)/shard_map/pallas_call | solution.py:340
  4.0 5.1 %collective-permute-start = (f32[8,144]{1,0:T(8,128)}, f32[8,144]{1,0:T(8,128)S(1)}, u32[]{:S(2)}, u32[]{:S(2)}) collective-permute-start(f32[8,144]{1,0:T(8,128)} %get-tuple-element.59), channel_id=1, source_target_pairs={{0,256},{4,260},{8,264},{12,268},{16,272},{20,276},{24,280},{28,28... | collective-permute-start | bytes 13832 | tf_op jit(solution)/shard_map/ppermute | solution.py:361
  9.1 11.5 %collective-permute-start.1 = (f32[8,144]{1,0:T(8,128)}, f32[8,144]{1,0:T(8,128)S(1)}, u32[]{:S(2)}, u32[]{:S(2)}) collective-permute-start(f32[8,144]{1,0:T(8,128)} %get-tuple-element.60), channel_id=1, source_target_pairs={{0,500},{500,0},{8,508},{508,8},{16,4},{4,16},{24,12},{12,24},{32,... | collective-permute-start | bytes 13832 | tf_op jit(solution)/shard_map/ppermute | solution.py:361
  20.6 1.9 %collective-permute-start.2 = (f32[8,144]{1,0:T(8,128)}, f32[8,144]{1,0:T(8,128)S(1)}, u32[]{:S(2)}, u32[]{:S(2)}) collective-permute-start(f32[8,144]{1,0:T(8,128)} %get-tuple-element.61), channel_id=1, source_target_pairs={{0,508},{508,0},{8,4},{4,8},{16,12},{12,16},{24,20},{20,24},{32,28... | collective-permute-start | bytes 13832 | tf_op jit(solution)/shard_map/ppermute | solution.py:361
  22.5 1.9 %collective-permute-start.3 = (f32[8,144]{1,0:T(8,128)}, f32[8,144]{1,0:T(8,128)S(1)}, u32[]{:S(2)}, u32[]{:S(2)}) collective-permute-start(f32[8,144]{1,0:T(8,128)} %get-tuple-element.62), channel_id=1, source_target_pairs={{0,12},{12,0},{8,20},{20,8},{16,28},{28,16},{24,36},{36,24},{32,44... | collective-permute-start | bytes 13832 | tf_op jit(solution)/shard_map/ppermute | solution.py:361
  24.4 3.0 %collective-permute-start.4 = (f32[8,144]{1,0:T(8,128)}, f32[8,144]{1,0:T(8,128)S(1)}, u32[]{:S(2)}, u32[]{:S(2)}) collective-permute-start(f32[8,144]{1,0:T(8,128)} %get-tuple-element.63), channel_id=1, source_target_pairs={{0,4},{4,0},{8,12},{12,8},{16,20},{20,16},{24,28},{28,24},{32,36},... | collective-permute-start | bytes 13832 | tf_op jit(solution)/shard_map/ppermute | solution.py:361
  27.5 2.4 %collective-permute-start.5 = (f32[16,144]{1,0:T(8,128)}, f32[16,144]{1,0:T(8,128)S(1)}, u32[]{:S(2)}, u32[]{:S(2)}) collective-permute-start(f32[16,144]{1,0:T(8,128)} %get-tuple-element.64), channel_id=1, source_target_pairs={{0,1},{1,0},{2,3},{3,2},{4,5},{5,4},{6,7},{7,6},{8,9},{9,8},{10,11... | collective-permute-start | bytes 27656 | tf_op jit(solution)/shard_map/ppermute | solution.py:366
  29.9 4.1 %collective-permute-start.6 = (f32[16,144]{1,0:T(8,128)}, f32[16,144]{1,0:T(8,128)S(1)}, u32[]{:S(2)}, u32[]{:S(2)}) collective-permute-start(f32[16,144]{1,0:T(8,128)} %get-tuple-element.65), channel_id=1, source_target_pairs={{1,2},{2,1},{5,6},{6,5},{9,10},{10,9},{13,14},{14,13},{17,18},{18,... | collective-permute-start | bytes 27656 | tf_op jit(solution)/shard_map/ppermute | solution.py:366
  34.7 0.9 %copy-done = f32[81,3,128]{2,1,0:T(4,128)S(1)} copy-done((f32[81,3,128]{2,1,0:T(4,128)S(1)}, f32[81,3,128]{2,1,0:T(4,128)}, u32[]{:S(2)}) %copy-start) | copy-done | bytes 124440
  35.6 1.0 %copy-done.2 = bf16[144,1152]{1,0:T(8,128)(2,1)S(1)} copy-done((bf16[144,1152]{1,0:T(8,128)(2,1)S(1)}, bf16[144,1152]{1,0:T(8,128)(2,1)}, u32[]{:S(2)}) %copy-start.2) | copy-done | bytes 331800
  36.6 1.0 %copy-done.4 = f32[64,1152]{1,0:T(8,128)S(1)} copy-done((f32[64,1152]{1,0:T(8,128)S(1)}, f32[64,1152]{1,0:T(8,128)}, u32[]{:S(2)}) %copy-start.4) | copy-done | bytes 294936
  37.6 0.8 %copy-done.8 = f32[3,35,35]{2,1,0:T(8,128)S(1)} copy-done((f32[3,35,35]{2,1,0:T(8,128)S(1)}, f32[3,35,35]{2,1,0:T(8,128)}, u32[]{:S(2)}) %copy-start.8) | copy-done | bytes 14724
  39.2 1.4 %shard_map.119 = (f32[9,40,128]{2,1,0:T(8,128)S(1)}, f32[64,1152]{1,0:T(8,128)S(1)}, f32[288,512]{1,0:T(8,128)S(1)}, f32[162,4,128]{2,1,0:T(4,128)S(1)}, bf16[51...) custom-call(f32[9,35,128]{2,1,0:T(8,128)S(1)} %copy-done.5, ...), custom_call_target="tpu_custom_call" | custom-call | flops 200000000 | bytes 2000000 | tf_op jit(solution)/shard_map/pallas_call | solution.py:340
  41.3 3.3 %shard_map.120 = (f32[9,40,128]{2,1,0:T(8,128)S(1)}, bf16[144,1152]{1,0:T(8,128)(2,1)S(1)}, f32[64,1152]{1,0:T(8,128)S(1)}, f32[8,144]{1,0:T(8,128)S(1)}, f32[8,...) custom-call(f32[9,40,128]{2,1,0:T(8,128)S(1)} %get-tuple-element.46., ...), custom_call_target="tpu_custom_call" | custom-call | flops 200000000 | bytes 2000000 | tf_op jit(solution)/shard_map/pallas_call | solution.py:340
  44.6 3.6 %collective-permute-start.7 = (f32[8,144]{1,0:T(8,128)S(1)}, f32[8,144]{1,0:T(8,128)S(1)}, u32[]{:S(2)}, u32[]{:S(2)}) collective-permute-start(f32[8,144]{1,0:T(8,128)S(1)} %get-tuple-element.74), channel_id=1, source_target_pairs={{0,256},{4,260},{8,264},{12,268},{16,272},{20,276},{24,280},{28,28... | collective-permute-start | bytes 13832 | tf_op jit(solution)/shard_map/ppermute | solution.py:361
  48.2 6.0 %collective-permute-start.8 = (f32[8,144]{1,0:T(8,128)S(1)}, f32[8,144]{1,0:T(8,128)S(1)}, u32[]{:S(2)}, u32[]{:S(2)}) collective-permute-start(f32[8,144]{1,0:T(8,128)S(1)} %get-tuple-element.75), channel_id=1, source_target_pairs={{0,500},{500,0},{8,508},{508,8},{16,4},{4,16},{24,12},{12,24},{32,... | collective-permute-start | bytes 13832 | tf_op jit(solution)/shard_map/ppermute | solution.py:361
  54.2 3.4 %collective-permute-start.9 = (f32[8,144]{1,0:T(8,128)S(1)}, f32[8,144]{1,0:T(8,128)S(1)}, u32[]{:S(2)}, u32[]{:S(2)}) collective-permute-start(f32[8,144]{1,0:T(8,128)S(1)} %get-tuple-element.76), channel_id=1, source_target_pairs={{0,508},{508,0},{8,4},{4,8},{16,12},{12,16},{24,20},{20,24},{32,28... | collective-permute-start | bytes 13832 | tf_op jit(solution)/shard_map/ppermute | solution.py:361
  57.5 1.9 %collective-permute-start.10 = (f32[8,144]{1,0:T(8,128)S(1)}, f32[8,144]{1,0:T(8,128)S(1)}, u32[]{:S(2)}, u32[]{:S(2)}) collective-permute-start(f32[8,144]{1,0:T(8,128)S(1)} %get-tuple-element.77), channel_id=1, source_target_pairs={{0,12},{12,0},{8,20},{20,8},{16,28},{28,16},{24,36},{36,24},{32,44... | collective-permute-start | bytes 13832 | tf_op jit(solution)/shard_map/ppermute | solution.py:361
  59.5 3.0 %collective-permute-start.11 = (f32[8,144]{1,0:T(8,128)S(1)}, f32[8,144]{1,0:T(8,128)S(1)}, u32[]{:S(2)}, u32[]{:S(2)}) collective-permute-start(f32[8,144]{1,0:T(8,128)S(1)} %get-tuple-element.78), channel_id=1, source_target_pairs={{0,4},{4,0},{8,12},{12,8},{16,20},{20,16},{24,28},{28,24},{32,36},... | collective-permute-start | bytes 13832 | tf_op jit(solution)/shard_map/ppermute | solution.py:361
  62.5 1.9 %collective-permute-start.12 = (f32[16,144]{1,0:T(8,128)S(1)}, f32[16,144]{1,0:T(8,128)S(1)}, u32[]{:S(2)}, u32[]{:S(2)}) collective-permute-start(f32[16,144]{1,0:T(8,128)S(1)} %get-tuple-element.79), channel_id=1, source_target_pairs={{0,1},{1,0},{2,3},{3,2},{4,5},{5,4},{6,7},{7,6},{8,9},{9,8},{10,11... | collective-permute-start | bytes 27656 | tf_op jit(solution)/shard_map/ppermute | solution.py:366
  64.5 1.9 %collective-permute-start.13 = (f32[16,144]{1,0:T(8,128)S(1)}, f32[16,144]{1,0:T(8,128)S(1)}, u32[]{:S(2)}, u32[]{:S(2)}) collective-permute-start(f32[16,144]{1,0:T(8,128)S(1)} %get-tuple-element.80), channel_id=1, source_target_pairs={{1,2},{2,1},{5,6},{6,5},{9,10},{10,9},{13,14},{14,13},{17,18},{18,... | collective-permute-start | bytes 27656 | tf_op jit(solution)/shard_map/ppermute | solution.py:366
  66.4 1.2 %shard_map.121 = (f32[9,40,128]{2,1,0:T(8,128)S(1)}, f32[64,1152]{1,0:T(8,128)S(1)}, f32[288,512]{1,0:T(8,128)S(1)}) custom-call(f32[9,40,128]{2,1,0:T(8,128)S(1)} %get-tuple-element.66.middle, bf16[144,1152]{1,0:T(8,128)(2,1)S(1)} %get-tuple-element.67.x, f32[64,1152]{1,0:T(8,128)S(1)} %get-tuple-element.68.s, f32[81,3,128]{2,1,0:T(4,128)S(1)} %copy-done.1, ...), custom_call_target="tpu_custom_call" | custom-call | flops 200000000 | bytes 2000000 | tf_op jit(solution)/shard_map/pallas_call | solution.py:340
  68.2 1.9 %collective-permute-done.13.rest_6_ = f32[16,144]{1,0:T(8,128)S(1)} collective-permute-done((f32[16,144]{1,0:T(8,128)S(1)}, f32[16,144]{1,0:T(8,128)S(1)}, u32[]{:S(2)}, u32[]{:S(2)}) %collective-permute-start.13) | collective-permute-done | bytes 9248 | tf_op jit(solution)/shard_map/ppermute | solution.py:366
  70.1 1.9 %shard_map.122 = f32[9,35,128]{2,1,0:T(8,128)} custom-call(f32[9,40,128]{2,1,0:T(8,128)S(1)} %get-tuple-element.71.held, f32[64,1152]{1,0:T(8,128)S(1)} %get-tuple-element.72.own, f32[288,512]{1,0:T(8,128)S(1)} %get-tuple-element.73.picked, bf16[80,512]{1,0:T(8,128)(2,1)S(1)} %copy-done.3, s32[4,128]{1,0:T(4,128)S(1)} %copy-done.14, ...), custom_call_target="tpu_custom_call" | custom-call | flops 100000000 | bytes 2000000 | tf_op jit(solution)/shard_map/pallas_call | solution.py:340
  (47 shorter events, 2.6 us)
Async XLA Ops:
  0.0 34.0 %copy-start.5 = (f32[9,35,128]{2,1,0:T(8,128)S(1)}, f32[9,35,128]{2,1,0:T(8,128)}, u32[]{:S(2)}) copy-start(f32[9,35,128]{2,1,0:T(8,128)} %state.3) | copy-start | bytes 483844
  0.0 34.0 %copy-start.7 = (bf16[2,4,9,9,128]{4,1,3,2,0:T(4,128)(2,1)S(1)}, bf16[2,4,9,9,128]{4,1,3,2,0:T(4,128)(2,1)}, u32[]{:S(2)}) copy-start(bf16[2,4,9,9,128]{4,1,3,2,0:T(4,128)(2,1)} %param.14) | copy-start | bytes 497668
  0.0 34.0 %copy-start.11 = (f32[4,35,15]{1,0,2:T(4,128)S(1)}, f32[4,35,15]{1,0,2:T(4,128)}, u32[]{:S(2)}) copy-start(f32[4,35,15]{1,0,2:T(4,128)} %param.22) | copy-start | bytes 25204
  4.0 23.5 %collective-permute-start = (f32[8,144]{1,0:T(8,128)}, f32[8,144]{1,0:T(8,128)S(1)}, u32[]{:S(2)}, u32[]{:S(2)}) collective-permute-start(f32[8,144]{1,0:T(8,128)} %get-tuple-element.59), channel_id=1, source_target_pairs={{0,256},{4,260},{8,264},{12,268},{16,272},{20,276},{24,280},{28,28... | collective-permute-start | bytes 13832 | tf_op jit(solution)/shard_map/ppermute | solution.py:361
  9.1 20.9 %collective-permute-start.1 = (f32[8,144]{1,0:T(8,128)}, f32[8,144]{1,0:T(8,128)S(1)}, u32[]{:S(2)}, u32[]{:S(2)}) collective-permute-start(f32[8,144]{1,0:T(8,128)} %get-tuple-element.60), channel_id=1, source_target_pairs={{0,500},{500,0},{8,508},{508,8},{16,4},{4,16},{24,12},{12,24},{32,... | collective-permute-start | bytes 13832 | tf_op jit(solution)/shard_map/ppermute | solution.py:361
  20.6 20.0 %collective-permute-start.2 = (f32[8,144]{1,0:T(8,128)}, f32[8,144]{1,0:T(8,128)S(1)}, u32[]{:S(2)}, u32[]{:S(2)}) collective-permute-start(f32[8,144]{1,0:T(8,128)} %get-tuple-element.61), channel_id=1, source_target_pairs={{0,508},{508,0},{8,4},{4,8},{16,12},{12,16},{24,20},{20,24},{32,28... | collective-permute-start | bytes 13832 | tf_op jit(solution)/shard_map/ppermute | solution.py:361
  22.5 18.1 %collective-permute-start.3 = (f32[8,144]{1,0:T(8,128)}, f32[8,144]{1,0:T(8,128)S(1)}, u32[]{:S(2)}, u32[]{:S(2)}) collective-permute-start(f32[8,144]{1,0:T(8,128)} %get-tuple-element.62), channel_id=1, source_target_pairs={{0,12},{12,0},{8,20},{20,8},{16,28},{28,16},{24,36},{36,24},{32,44... | collective-permute-start | bytes 13832 | tf_op jit(solution)/shard_map/ppermute | solution.py:361
  24.4 16.1 %collective-permute-start.4 = (f32[8,144]{1,0:T(8,128)}, f32[8,144]{1,0:T(8,128)S(1)}, u32[]{:S(2)}, u32[]{:S(2)}) collective-permute-start(f32[8,144]{1,0:T(8,128)} %get-tuple-element.63), channel_id=1, source_target_pairs={{0,4},{4,0},{8,12},{12,8},{16,20},{20,16},{24,28},{28,24},{32,36},... | collective-permute-start | bytes 13832 | tf_op jit(solution)/shard_map/ppermute | solution.py:361
  27.5 13.1 %collective-permute-start.5 = (f32[16,144]{1,0:T(8,128)}, f32[16,144]{1,0:T(8,128)S(1)}, u32[]{:S(2)}, u32[]{:S(2)}) collective-permute-start(f32[16,144]{1,0:T(8,128)} %get-tuple-element.64), channel_id=1, source_target_pairs={{0,1},{1,0},{2,3},{3,2},{4,5},{5,4},{6,7},{7,6},{8,9},{9,8},{10,11... | collective-permute-start | bytes 27656 | tf_op jit(solution)/shard_map/ppermute | solution.py:366
  29.9 10.7 %collective-permute-start.6 = (f32[16,144]{1,0:T(8,128)}, f32[16,144]{1,0:T(8,128)S(1)}, u32[]{:S(2)}, u32[]{:S(2)}) collective-permute-start(f32[16,144]{1,0:T(8,128)} %get-tuple-element.65), channel_id=1, source_target_pairs={{1,2},{2,1},{5,6},{6,5},{9,10},{10,9},{13,14},{14,13},{17,18},{18,... | collective-permute-start | bytes 27656 | tf_op jit(solution)/shard_map/ppermute | solution.py:366
  35.6 1.0 %copy-start.2 = (bf16[144,1152]{1,0:T(8,128)(2,1)S(1)}, bf16[144,1152]{1,0:T(8,128)(2,1)}, u32[]{:S(2)}) copy-start(bf16[144,1152]{1,0:T(8,128)(2,1)} %get-tuple-element.43.x) | copy-start | bytes 995332
  39.1 1.5 %copy-start.1 = (f32[81,3,128]{2,1,0:T(4,128)S(1)}, f32[81,3,128]{2,1,0:T(4,128)}, u32[]{:S(2)}) copy-start(f32[81,3,128]{2,1,0:T(4,128)} %get-tuple-element.45.stars) | copy-start | bytes 373252
  39.1 1.5 %copy-start.3 = (bf16[80,512]{1,0:T(8,128)(2,1)S(1)}, bf16[80,512]{1,0:T(8,128)(2,1)}, u32[]{:S(2)}) copy-start(bf16[80,512]{1,0:T(8,128)(2,1)} %get-tuple-element.50.hot) | copy-start | bytes 245764
  39.1 1.5 %copy-start.6 = (f32[9,40,128]{2,1,0:T(8,128)S(1)}, f32[9,40,128]{2,1,0:T(8,128)}, u32[]{:S(2)}) copy-start(f32[9,40,128]{2,1,0:T(8,128)} %get-tuple-element.49.coarse) | copy-start | bytes 552964
  39.1 1.6 %copy-start.9 = (bf16[72,144]{1,0:T(8,128)(2,1)S(1)}, bf16[72,144]{1,0:T(8,128)(2,1)}, u32[]{:S(2)}) copy-start(bf16[72,144]{1,0:T(8,128)(2,1)} %get-tuple-element.54.step1) | copy-start | bytes 62212
  39.1 1.6 %copy-start.10 = (bf16[64,144]{1,0:T(8,128)(2,1)S(1)}, bf16[64,144]{1,0:T(8,128)(2,1)}, u32[]{:S(2)}) copy-start(bf16[64,144]{1,0:T(8,128)(2,1)} %get-tuple-element.58.traces) | copy-start | bytes 55300
  39.1 1.6 %copy-start.16 = (bf16[24,48]{1,0:T(8,128)(2,1)S(1)}, bf16[24,48]{1,0:T(8,128)(2,1)}, u32[]{:S(2)}) copy-start(bf16[24,48]{1,0:T(8,128)(2,1)} %get-tuple-element.57.step4) | copy-start | bytes 6916
  44.6 17.9 %collective-permute-start.7 = (f32[8,144]{1,0:T(8,128)S(1)}, f32[8,144]{1,0:T(8,128)S(1)}, u32[]{:S(2)}, u32[]{:S(2)}) collective-permute-start(f32[8,144]{1,0:T(8,128)S(1)} %get-tuple-element.74), channel_id=1, source_target_pairs={{0,256},{4,260},{8,264},{12,268},{16,272},{20,276},{24,280},{28,28... | collective-permute-start | bytes 13832 | tf_op jit(solution)/shard_map/ppermute | solution.py:361
  48.2 16.2 %collective-permute-start.8 = (f32[8,144]{1,0:T(8,128)S(1)}, f32[8,144]{1,0:T(8,128)S(1)}, u32[]{:S(2)}, u32[]{:S(2)}) collective-permute-start(f32[8,144]{1,0:T(8,128)S(1)} %get-tuple-element.75), channel_id=1, source_target_pairs={{0,500},{500,0},{8,508},{508,8},{16,4},{4,16},{24,12},{12,24},{32,... | collective-permute-start | bytes 13832 | tf_op jit(solution)/shard_map/ppermute | solution.py:361
  54.2 13.5 %collective-permute-start.9 = (f32[8,144]{1,0:T(8,128)S(1)}, f32[8,144]{1,0:T(8,128)S(1)}, u32[]{:S(2)}, u32[]{:S(2)}) collective-permute-start(f32[8,144]{1,0:T(8,128)S(1)} %get-tuple-element.76), channel_id=1, source_target_pairs={{0,508},{508,0},{8,4},{4,8},{16,12},{12,16},{24,20},{20,24},{32,28... | collective-permute-start | bytes 13832 | tf_op jit(solution)/shard_map/ppermute | solution.py:361
  57.5 10.1 %collective-permute-start.10 = (f32[8,144]{1,0:T(8,128)S(1)}, f32[8,144]{1,0:T(8,128)S(1)}, u32[]{:S(2)}, u32[]{:S(2)}) collective-permute-start(f32[8,144]{1,0:T(8,128)S(1)} %get-tuple-element.77), channel_id=1, source_target_pairs={{0,12},{12,0},{8,20},{20,8},{16,28},{28,16},{24,36},{36,24},{32,44... | collective-permute-start | bytes 13832 | tf_op jit(solution)/shard_map/ppermute | solution.py:361
  59.5 8.2 %collective-permute-start.11 = (f32[8,144]{1,0:T(8,128)S(1)}, f32[8,144]{1,0:T(8,128)S(1)}, u32[]{:S(2)}, u32[]{:S(2)}) collective-permute-start(f32[8,144]{1,0:T(8,128)S(1)} %get-tuple-element.78), channel_id=1, source_target_pairs={{0,4},{4,0},{8,12},{12,8},{16,20},{20,16},{24,28},{28,24},{32,36},... | collective-permute-start | bytes 13832 | tf_op jit(solution)/shard_map/ppermute | solution.py:361
  62.5 5.6 %collective-permute-start.12 = (f32[16,144]{1,0:T(8,128)S(1)}, f32[16,144]{1,0:T(8,128)S(1)}, u32[]{:S(2)}, u32[]{:S(2)}) collective-permute-start(f32[16,144]{1,0:T(8,128)S(1)} %get-tuple-element.79), channel_id=1, source_target_pairs={{0,1},{1,0},{2,3},{3,2},{4,5},{5,4},{6,7},{7,6},{8,9},{9,8},{10,11... | collective-permute-start | bytes 27656 | tf_op jit(solution)/shard_map/ppermute | solution.py:366
  64.5 5.6 %collective-permute-start.13 = (f32[16,144]{1,0:T(8,128)S(1)}, f32[16,144]{1,0:T(8,128)S(1)}, u32[]{:S(2)}, u32[]{:S(2)}) collective-permute-start(f32[16,144]{1,0:T(8,128)S(1)} %get-tuple-element.80), channel_id=1, source_target_pairs={{1,2},{2,1},{5,6},{6,5},{9,10},{10,9},{13,14},{14,13},{17,18},{18,... | collective-permute-start | bytes 27656 | tf_op jit(solution)/shard_map/ppermute | solution.py:366
  (9 other events, 6.9 us)
where the time goes:
time: 72.7 us; the launch traced here: 71.9 us
  starting transfers between devices  51.7 us (71%)
  Pallas kernels  11.7 us (16%)
  local copies, waits for them, and re-layouts  5.72 us (8%)
  waiting for transfers between devices  2.45 us (3%)
    ppermute x10, starting transfers between devices, exchange(): landed.append(lax.ppermute(block, 'dom', pairs))  41.4 us
    pallas_call x5, Pallas kernels, call(): pl.pallas_call(kernel, out_shape=outs, in_specs=[source] * len(operands),...  11.7 us
    ppermute x4, starting transfers between devices, exchange(): landed.append(lax.ppermute(block, 'ply', pairs))  10.3 us
    unnamed x38, local copies, waits for them, and re-layouts  5.72 us
    ppermute x4, waiting for transfers between devices, exchange(): landed.append(lax.ppermute(block, 'ply', pairs))  2.43 us
  transfers between devices with their start and end apart: 14, of which 2 were waited for; matrix products, arithmetic and copies ran while one was open for 0% of the time, Pallas kernels for 4%

commit v1 on v0

v1 whole, which is shorter than its diff:
```python
import jax
import jax.numpy as jnp
from jax import lax
from jax.experimental import pallas as pl
from jax.experimental.pallas import tpu as pltpu
from jax.sharding import PartitionSpec as P

F32, BF16 = jnp.float32, jnp.bfloat16
Q, B, A, ORDER = 9, 35, 15, 5
E = 128
PAD = 48
AP = 16
SLOT, LAY = 8, 16
CUTS = 5 * SLOT + 2 * LAY
CP = 80
WIDE = Q * E
ALL = 4 * E

EARLY = [0.5 ** (k + 1) for k in range(ORDER)]
LATE = [1.0 - 0.5 ** (k + 1) for k in range(ORDER)]
FACT = [1.0, 2.0, 6.0, 24.0, 120.0]
STEPS = [(24, 48), (16, 32), (8, 16), (8, 16)]


def dot(a, b):
    return jnp.dot(a, b, preferred_element_type=F32)


def halves(x):
    top = x.astype(BF16)
    return top, (x - top.astype(F32)).astype(BF16)


def tripled(a):
    top = a.astype(BF16).astype(F32)
    return jnp.concatenate([top, top, a - top], axis=1).astype(BF16)


def padded(a, rows, cols):
    r, c = a.shape
    if c < cols:
        a = jnp.concatenate([a, jnp.zeros((r, cols - c), a.dtype)], axis=1)
    if r < rows:
        a = jnp.concatenate([a, jnp.zeros((rows - r, cols), a.dtype)], axis=0)
    return a


def lanes(p):
    return slice(p * E, (p + 1) * E)


def put_stack(ref, rows, p, value):
    top, rest = halves(value)
    ref[0:rows, lanes(p)] = top
    ref[rows : 2 * rows, lanes(p)] = rest
    ref[2 * rows : 3 * rows, lanes(p)] = top


def stiff_rows(stiffness, rows, cols):
    blocks = [
        tripled(padded(stiffness[d], PAD, PAD)[:rows, :cols]).astype(F32) for d in range(3)
    ]
    return jnp.concatenate(blocks, axis=0).astype(BF16)


def trace_rows(trace_maps):
    blocks = [tripled(padded(trace_maps[f], AP, PAD)).astype(F32) for f in range(4)]
    return jnp.concatenate(blocks, axis=0).astype(BF16)


def volume_rows(stiffness):
    blocks = [tripled(padded(stiffness[d].T, 40, PAD)).astype(F32) for d in range(3)]
    return jnp.concatenate(blocks, axis=0).astype(BF16)


def lift_rows(lift_maps):
    return tripled(jnp.concatenate([padded(lift_maps[:, f, :].T, 40, AP) for f in range(4)], axis=1))


def turn_rows(face_rotations):
    blocks = [tripled(padded(face_rotations[h], AP, AP)).astype(F32) for h in range(3)]
    return jnp.concatenate(blocks, axis=0).astype(BF16)


def widen(source, target, blocks):
    for n in range(blocks):
        target[n] = source[n].astype(F32)


def star_apply(y, stars, rows):
    def one(p, total):
        total = list(total)
        at = pl.ds(pl.multiple_of(p * E, E), E)
        for d in range(3):
            value = y[d * rows : (d + 1) * rows, at]
            for q in range(Q):
                total[q] = total[q] + stars[q * Q + p, d : d + 1, :] * value
        return tuple(total)

    start = tuple(jnp.zeros((rows, E), F32) for _ in range(Q))
    return lax.fori_loop(0, Q, one, start, unroll=Q if rows < 40 else 3)


def taylor(first, steps, stars, x, y, add):
    values = [first[q] for q in range(Q)]
    for k, (rows, reads) in enumerate(STEPS):
        for p in range(Q):
            put_stack(x, reads, p, padded(values[p], reads, E))
        y[0 : 3 * rows, :] = dot(steps[k][...], x[0 : 3 * reads, :])
        values = star_apply(y, stars, rows)
        for q in range(Q):
            add(k + 1, q, rows, values[q])


def far_steps(count):
    return (count - 3, count // 2)


def near_steps(count):
    return (count - 1, 3, 1)


def shared_faces(plane, thick):
    dom, ply = lax.axis_index("dom"), lax.axis_index("ply")
    count = lax.axis_size("dom")
    odd, high = lax.rem(dom, 2), lax.rem(ply, 2)
    sub = lax.broadcasted_iota(jnp.int32, (SLOT, E), 0)
    def plane_group(step):
        peer = lax.rem(dom + jnp.where(odd == 0, step, count - step), count)
        return lambda s: plane[0, peer * SLOT + s]

    groups = [plane_group(step) for step in far_steps(count)]
    for row in (1 - high, high):
        for half in (0, SLOT):
            groups.append(lambda s, row=row, half=half: thick[row, half + s])
    groups += [plane_group(step) for step in near_steps(count)]
    columns = []
    for face in groups:
        column = jnp.full((SLOT, E), -1, jnp.int32)
        for s in range(SLOT):
            column = jnp.where(sub == s, face(s), column)
        columns.append(column)
    columns.append(jnp.full((SLOT, E), -1, jnp.int32))
    return jnp.concatenate(columns, axis=0)


def pick_shared(plane, thick, hot):
    column = shared_faces(plane, thick)
    lane = lax.broadcasted_iota(jnp.int32, (CP, E), 1)
    for f in range(4):
        hot[:, lanes(f)] = jnp.where(column == lane + f * E, 1.0, 0.0).astype(BF16)


def send_traces(s, hot, l, outs):
    split_traces(s, l)
    total = None
    for part in (1, 0):
        piece = lax.dot_general(
            hot[...],
            l[part * Q * AP : (part + 1) * Q * AP, :],
            (((1,), (1,)), ((), ())),
            preferred_element_type=F32,
        )
        total = piece if total is None else total + piece
    at = 0
    for out in outs[:-1]:
        out[...] = total[at : at + out.shape[0]]
        at += out.shape[0]
    outs[-1][...] = jnp.zeros_like(outs[-1])
    outs[-1][0:SLOT] = total[at : at + SLOT]


def split_traces(s, l):
    for q in range(Q):
        for f in range(4):
            top, rest = halves(s[f * AP : (f + 1) * AP, lanes(q)])
            l[q * AP : (q + 1) * AP, lanes(f)] = top
            l[Q * AP + q * AP : Q * AP + (q + 1) * AP, lanes(f)] = rest


def first_kernel(state, stars, stiffness, trace_maps, plane, thick, neighbour, orient, cluster,
                 x_out, s_out, coarse, hot, marks, l, step1, step2, step3, step4, traces, *rest):
    sends, (first, early, x, y) = rest[:7], rest[7:]
    steps = (step1, step2, step3, step4)
    for step, (rows, reads) in zip(steps, STEPS):
        step[...] = stiff_rows(stiffness, rows, reads)
    traces[...] = trace_rows(trace_maps)
    pick_shared(plane, thick, hot)
    marks[0:4] = neighbour[...]
    marks[4:8] = orient[...]
    marks[8:9] = cluster[...]
    first[...] = jnp.zeros_like(first)
    first[:, 0:B, :] = state[...]
    early[...] = first[...] * EARLY[0]
    coarse[...] = first[:, 0:40, :] * LATE[0]

    def add(k, q, rows, value):
        sign = -1.0 if k % 2 else 1.0
        early[q, 0:rows, :] = early[q, 0:rows, :] + value * (sign * EARLY[k] / FACT[k])
        coarse[q, 0:rows, :] = coarse[q, 0:rows, :] + value * (sign * LATE[k] / FACT[k])

    taylor(first, steps, stars, x, y, add)
    for p in range(Q):
        put_stack(x_out, PAD, p, early[p])
    s_out[...] = dot(traces[...], x_out[...])
    send_traces(s_out, hot, l, sends)


def own_part(base, x, s, l, stars, solvers, volumes, same, held, own, picked, y):
    picked[...] = dot(l[...], same[...])
    y[...] = dot(volumes[...], x[...])
    sums = star_apply(y, stars, 40)
    for q in range(Q):
        held[q] = base(q) + sums[q]
    fluxes(solvers, 0, s, own, None)


def fluxes(solvers, side, values, g, before):
    for f in range(4):
        rows = slice(f * AP, (f + 1) * AP)

        def face(p, total):
            total = list(total)
            at = pl.ds(pl.multiple_of(p * E, E), E)
            value = values[rows, at]
            for q in range(Q):
                total[q] = total[q] + solvers[(side * Q + q) * Q + p, f : f + 1, :] * value
            return tuple(total)

        start = [jnp.zeros((AP, E), F32) if before is None else before[rows, lanes(q)] for q in range(Q)]
        total = lax.fori_loop(0, Q, face, tuple(start), unroll=Q)
        for q in range(Q):
            g[rows, lanes(q)] = total[q]


def early_own_kernel(state, x, s, l, stars, flux, marks, stiffness, lift_maps, rotations,
                     held, own, picked, solvers, same, volumes, lifts, turns, padded_state, y):
    widen(flux, solvers, 2 * Q * Q)
    sub = lax.broadcasted_iota(jnp.int32, (ALL, E), 0)
    for f in range(4):
        same[:, lanes(f)] = jnp.where(sub == marks[f : f + 1, :], 1.0, 0.0).astype(BF16)
    volumes[...] = volume_rows(stiffness)
    lifts[...] = lift_rows(lift_maps)
    turns[...] = turn_rows(rotations)
    padded_state[...] = jnp.zeros_like(padded_state)
    padded_state[:, 0:B, :] = state[...]
    own_part(lambda q: padded_state[q], x, s, l, stars, solvers, volumes, same, held, own, picked, y)


def late_own_kernel(middle, x, s, l, stars, solvers, volumes, same, held, own, picked, y):
    own_part(lambda q: middle[q], x, s, l, stars, solvers, volumes, same, held, own, picked, y)


def finished(held, own, picked, arrived, hot, marks, solvers, lifts, turns, turned_in, o, g):
    landed = jnp.concatenate(
        [ref[...] for ref in arrived[:-1]]
        + [arrived[-1][0:SLOT], jnp.zeros((CP - CUTS, Q * AP), F32)], axis=0
    )
    both = [
        picked[part * Q * AP : (part + 1) * Q * AP, :]
        + lax.dot_general(
            piece, hot[...], (((0,), (0,)), ((), ())), preferred_element_type=F32
        )
        for part, piece in enumerate(halves(landed))
    ]
    for q in range(Q):
        cols = slice(q * ALL, (q + 1) * ALL)
        top = both[0][q * AP : (q + 1) * AP].astype(BF16)
        turned_in[0:AP, cols] = top
        turned_in[AP : 2 * AP, cols] = both[1][q * AP : (q + 1) * AP].astype(BF16)
        turned_in[2 * AP : 3 * AP, cols] = top
    for q in range(Q):
        turned = dot(turns[...], turned_in[:, q * ALL : (q + 1) * ALL])
        for f in range(4):
            way = marks[4 + f : 5 + f, :]
            o[f * AP : (f + 1) * AP, lanes(q)] = jnp.where(
                way == 0,
                turned[0:AP, lanes(f)],
                jnp.where(way == 1, turned[AP : 2 * AP, lanes(f)], turned[2 * AP : 3 * AP, lanes(f)]),
            )
    fluxes(solvers, 1, o, g, own)
    results = []
    for q in range(Q):
        top, rest = halves(g[:, lanes(q)])
        results.append(held[q] - dot(lifts[...], jnp.concatenate([top, rest, top], axis=0)))
    return results


def middle_kernel(held, own, picked, coarse, hot, marks, stars, solvers, lifts, turns,
                  step1, step2, step3, step4, traces, *rest):
    arrived, (middle, x_out, s_out, l), sends = rest[:7], rest[7:11], rest[11:18]
    first, late, x, y, turned_in, o, g = rest[18:]
    values = finished(held, own, picked, arrived, hot, marks, solvers, lifts, turns, turned_in, o, g)
    for q in range(Q):
        first[q] = padded(values[q], PAD, E)
        middle[q] = values[q]
        late[q] = first[q] * EARLY[0]

    def add(k, q, rows, value):
        sign = -1.0 if k % 2 else 1.0
        late[q, 0:rows, :] = late[q, 0:rows, :] + value * (sign * EARLY[k] / FACT[k])

    taylor(first, (step1, step2, step3, step4), stars, x, y, add)
    fine = marks[8:9, :] == 1
    for q in range(Q):
        late[q, 0:40, :] = jnp.where(fine, late[q, 0:40, :], coarse[q])
        put_stack(x_out, PAD, q, late[q])
    s_out[...] = dot(traces[...], x_out[...])
    send_traces(s_out, hot, l, sends)


def last_kernel(held, own, picked, hot, marks, solvers, lifts, turns, *rest):
    arrived, out, (turned_in, o, g) = rest[:7], rest[7], rest[8:]
    values = finished(held, own, picked, arrived, hot, marks, solvers, lifts, turns, turned_in, o, g)
    for q in range(Q):
        out[q] = values[q][0:B]


def shape(dims, kind=F32):
    return jax.ShapeDtypeStruct(dims, kind)


CORE_ROWS = 24
SENDS = (
    [(SLOT, Q * AP)] * 2 + [(LAY, Q * AP)] * 2 + [(SLOT, Q * AP)] * 2 + [(CORE_ROWS, Q * AP)]
)
PADDED = pltpu.VMEM((Q, PAD, E), F32)
X = pltpu.VMEM((3 * PAD, WIDE), BF16)
Y = pltpu.VMEM((120, WIDE), F32)
TURNED = pltpu.VMEM((3 * AP, Q * ALL), BF16)
SIDE = pltpu.VMEM((4 * AP, WIDE), F32)


def call(kernel, operands, outs, scratch, flops, scalars=()):
    vmem, smem = pl.BlockSpec(memory_space=pltpu.VMEM), pl.BlockSpec(memory_space=pltpu.SMEM)
    return pl.pallas_call(
        kernel,
        out_shape=outs,
        in_specs=[smem if n in scalars else vmem for n in range(len(operands))],
        out_specs=jax.tree.map(lambda _: vmem, outs),
        scratch_shapes=scratch,
        compiler_params=pltpu.CompilerParams(vmem_limit_bytes=40 * 1024 * 1024),
        cost_estimate=pl.CostEstimate(flops=flops, bytes_accessed=2_000_000, transcendentals=0),
    )(*operands)


def exchange(blocks):
    count, layers = lax.axis_size("dom"), lax.axis_size("ply")

    def along_dom(step, block):
        if step % 2 == 0:
            pairs = [(i, (i + step) % count) for i in range(count)]
        else:
            pairs = []
            for even in range(0, count, 2):
                other = (even + step) % count
                pairs += [(even, other), (other, even)]
        return lax.ppermute(block, "dom", pairs)

    def along_ply(start, block):
        pairs = []
        for low in range(start, layers - 1, 2):
            pairs += [(low, low + 1), (low + 1, low)]
        return lax.ppermute(block, "ply", pairs)

    return (
        [along_dom(step, block) for step, block in zip(far_steps(count), blocks)]
        + [along_ply(start, block) for start, block in zip((0, 1), blocks[2:])]
        + [along_dom(step, block) for step, block in zip(near_steps(count), blocks[4:])]
    )


def body(state, star, flux, cluster, neighbour, orient, plane, thick,
         stiffness, trace_maps, lift_maps, rotations):
    stars = star.transpose(1, 2, 0, 3).reshape(Q * Q, 3, E).astype(F32)
    flux = flux.transpose(0, 2, 3, 1, 4).reshape(2 * Q * Q, 4, E)
    lift_maps = lift_maps.transpose(2, 0, 1)
    cluster = cluster.reshape(1, E)
    kept = [shape((3 * PAD, WIDE), BF16), shape((4 * AP, WIDE)), shape((Q, 40, E))]
    sends = [shape(dims) for dims in SENDS]
    split = shape((2 * Q * AP, ALL), BF16)
    products = [shape((3 * rows, 3 * reads), BF16) for rows, reads in STEPS]
    products.append(shape((4 * AP, 3 * PAD), BF16))
    own_outs = [kept[2], kept[1], shape((2 * Q * AP, ALL))]
    x_early, s_early, coarse, hot, marks, l_early, *rest = call(
        first_kernel,
        (state, stars, stiffness, trace_maps, plane, thick, neighbour, orient, cluster),
        kept + [shape((CP, ALL), BF16), shape((AP, E), jnp.int32), split]
        + products + sends,
        [PADDED, PADDED, X, Y],
        100_000_000, (4, 5),
    )
    steps, out_early = rest[:5], rest[5:]
    in_early = exchange(out_early)
    held, own, picked, solvers, same, volumes, lifts, turns = call(
        early_own_kernel,
        (state, x_early, s_early, l_early, stars, flux, marks, stiffness, lift_maps, rotations),
        own_outs + [
            shape((2 * Q * Q, 4, E)), shape((ALL, ALL), BF16), shape((120, 3 * PAD), BF16),
            shape((40, 12 * AP), BF16), shape((3 * AP, 3 * AP), BF16),
        ],
        [pltpu.VMEM((Q, 40, E), F32), Y], 200_000_000,
    )
    middle, x_late, s_late, l_late, *out_late = call(
        middle_kernel,
        (held, own, picked, coarse, hot, marks, stars, solvers, lifts, turns, *steps,
         *in_early),
        [kept[2], kept[0], kept[1], split] + sends,
        [PADDED, PADDED, X, Y, TURNED, SIDE, SIDE], 200_000_000,
    )
    in_late = exchange(out_late)
    held, own, picked = call(
        late_own_kernel, (middle, x_late, s_late, l_late, stars, solvers, volumes, same),
        own_outs, [Y], 200_000_000,
    )
    return call(
        last_kernel, (held, own, picked, hot, marks, solvers, lifts, turns, *in_late),
        shape((Q, B, E)), [TURNED, SIDE, SIDE], 100_000_000,
    )


def solution(mesh):
    both = ("dom", "ply")
    in_specs = (
        P(None, None, both),
        P(None, None, None, both),
        P(None, None, None, None, both),
        P(both),
        P(None, both),
        P(None, both),
        P(both, None),
        P(both, None),
        P(),
        P(),
        P(),
        P(),
    )
    return jax.shard_map(
        body, mesh=mesh, in_specs=in_specs, out_specs=P(None, None, both), check_vma=False
    )
```

time: 72.7 us -> 64 us (0.88)
  the two profiles are of different devices: /device:TPU:2 before, /device:TPU:1 now
where the time goes in v1:
time: 64 us; the launch traced here: 63.5 us
  starting transfers between devices  52.3 us (82%)
  Pallas kernels  8.22 us (13%)
  local copies, waits for them, and re-layouts  1.46 us (2%)
  other arithmetic  0.95 us (1%)
    ppermute x10, starting transfers between devices, along_dom(): return lax.ppermute(block, 'dom', pairs)  42.3 us
    ppermute x4, starting transfers between devices, along_ply(): return lax.ppermute(block, 'ply', pairs)  9.97 us
    pallas_call x5, Pallas kernels, call(): pl.pallas_call(kernel, out_shape=outs, in_specs=[smem if n in scalars els...  8.22 us
    unnamed x21, local copies, waits for them, and re-layouts  1.46 us
  transfers between devices with their start and end apart: 14, of which 1 were waited for; matrix products, arithmetic and copies ran while one was open for 0% of the time, Pallas kernels for 3%

profile of v1, /device:TPU:1, one launch (start us, length us, event | category | flops | bytes accessed | tf_op | source)
XLA Modules:
  0.0 63.5 jit_solution(3699190002681381584)
XLA Ops:
  0.0 0.8 %copy.13.trace_maps = f32[4,15,35]{2,1,0:T(8,128)S(1)} copy(f32[4,15,35]{2,0,1:T(4,128)} %param.21) | data formatting | bytes 16800 | tf_op args[9]
  0.8 0.9 %convert_element_type.11 = f32[3,9,9,128]{3,0,2,1:T(4,128)S(1)} convert(bf16[3,9,9,128]{3,0,2,1:T(4,128)(2,1)} %param.13) | non-fusion elementwise | flops 31104 | bytes 186624 | tf_op jit(solution)/shard_map/convert_element_type | solution.py:375
  1.8 0.6 copy-done.6
  2.4 0.0 copy-done.8
  2.5 2.3 %shard_map.118 = (bf16[144,1152]{1,0:T(8,128)(2,1)S(1)}, f32[64,1152]{1,0:T(8,128)S(1)}, f32[9,40,128]{2,1,0:T(8,128)S(1)}, bf16[80,512]{1,0:T(8,128)(2,1)S(1)},...) custom-call(f32[9,35,128]{2,1,0:T(8,128)S(1)} %copy-done, ...), custom_call_target="tpu_custom_call" | custom-call | flops 100000000 | bytes 2000000 | tf_op jit(solution)/shard_map/pallas_call | solution.py:336
  4.8 6.3 %collective-permute-start = (f32[8,144]{1,0:T(8,128)S(1)}, f32[8,144]{1,0:T(8,128)S(1)}, u32[]{:S(2)}, u32[]{:S(2)}) collective-permute-start(f32[8,144]{1,0:T(8,128)S(1)} %get-tuple-element.62), channel_id=1, source_target_pairs={{0,500},{500,0},{8,508},{508,8},{16,4},{4,16},{24,12},{12,24},{32,... | collective-permute-start | bytes 13832 | tf_op jit(solution)/shard_map/ppermute | solution.py:358
  11.1 4.8 %collective-permute-start.1 = (f32[8,144]{1,0:T(8,128)S(1)}, f32[8,144]{1,0:T(8,128)S(1)}, u32[]{:S(2)}, u32[]{:S(2)}) collective-permute-start(f32[8,144]{1,0:T(8,128)S(1)} %get-tuple-element.63), channel_id=1, source_target_pairs={{0,256},{4,260},{8,264},{12,268},{16,272},{20,276},{24,280},{28,28... | collective-permute-start | bytes 13832 | tf_op jit(solution)/shard_map/ppermute | solution.py:358
  15.9 9.2 %collective-permute-start.4 = (f32[8,144]{1,0:T(8,128)S(1)}, f32[8,144]{1,0:T(8,128)S(1)}, u32[]{:S(2)}, u32[]{:S(2)}) collective-permute-start(f32[8,144]{1,0:T(8,128)S(1)} %get-tuple-element.66), channel_id=1, source_target_pairs={{0,508},{508,0},{8,4},{4,8},{16,12},{12,16},{24,20},{20,24},{32,28... | collective-permute-start | bytes 13832 | tf_op jit(solution)/shard_map/ppermute | solution.py:358
  25.1 2.5 %collective-permute-start.5 = (f32[8,144]{1,0:T(8,128)S(1)}, f32[8,144]{1,0:T(8,128)S(1)}, u32[]{:S(2)}, u32[]{:S(2)}) collective-permute-start(f32[8,144]{1,0:T(8,128)S(1)} %get-tuple-element.67), channel_id=1, source_target_pairs={{0,12},{12,0},{8,20},{20,8},{16,28},{28,16},{24,36},{36,24},{32,44... | collective-permute-start | bytes 13832 | tf_op jit(solution)/shard_map/ppermute | solution.py:358
  27.6 3.1 %collective-permute-start.2 = (f32[16,144]{1,0:T(8,128)S(1)}, f32[16,144]{1,0:T(8,128)S(1)}, u32[]{:S(2)}, u32[]{:S(2)}) collective-permute-start(f32[16,144]{1,0:T(8,128)S(1)} %get-tuple-element.64), channel_id=1, source_target_pairs={{0,1},{1,0},{2,3},{3,2},{4,5},{5,4},{6,7},{7,6},{8,9},{9,8},{10,11... | collective-permute-start | bytes 27656 | tf_op jit(solution)/shard_map/ppermute | solution.py:364
  30.8 0.7 %collective-permute-start.3 = (f32[16,144]{1,0:T(8,128)S(1)}, f32[16,144]{1,0:T(8,128)S(1)}, u32[]{:S(2)}, u32[]{:S(2)}) collective-permute-start(f32[16,144]{1,0:T(8,128)S(1)} %get-tuple-element.65), channel_id=1, source_target_pairs={{1,2},{2,1},{5,6},{6,5},{9,10},{10,9},{13,14},{14,13},{17,18},{18,... | collective-permute-start | bytes 27656 | tf_op jit(solution)/shard_map/ppermute | solution.py:364
  31.4 1.9 %collective-permute-start.6 = (f32[24,144]{1,0:T(8,128)S(1)}, f32[24,144]{1,0:T(8,128)S(1)}, u32[]{:S(2)}, u32[]{:S(2)}) collective-permute-start(f32[24,144]{1,0:T(8,128)S(1)} %get-tuple-element.68), channel_id=1, source_target_pairs={{0,4},{4,0},{8,12},{12,8},{16,20},{20,16},{24,28},{28,24},{32,36},... | collective-permute-start | bytes 41480 | tf_op jit(solution)/shard_map/ppermute | solution.py:358
  33.4 1.1 %shard_map.119 = (f32[9,40,128]{2,1,0:T(8,128)S(1)}, f32[64,1152]{1,0:T(8,128)S(1)}, f32[288,512]{1,0:T(8,128)S(1)}, f32[162,4,128]{2,1,0:T(4,128)S(1)}, bf16[51...) custom-call(f32[9,35,128]{2,1,0:T(8,128)S(1)} %copy-done, ...), custom_call_target="tpu_custom_call" | custom-call | flops 200000000 | bytes 2000000 | tf_op jit(solution)/shard_map/pallas_call | solution.py:336
  34.6 2.4 %shard_map.120 = (f32[9,40,128]{2,1,0:T(8,128)S(1)}, bf16[144,1152]{1,0:T(8,128)(2,1)S(1)}, f32[64,1152]{1,0:T(8,128)S(1)}, bf16[288,512]{1,0:T(8,128)(2,1)S(1)}...) custom-call(f32[9,40,128]{2,1,0:T(8,128)S(1)} %get-tuple-element.49., ...), custom_call_target="tpu_custom_call" | custom-call | flops 200000000 | bytes 2000000 | tf_op jit(solution)/shard_map/pallas_call | solution.py:336
  36.9 2.9 %collective-permute-start.7 = (f32[8,144]{1,0:T(8,128)S(1)}, f32[8,144]{1,0:T(8,128)S(1)}, u32[]{:S(2)}, u32[]{:S(2)}) collective-permute-start(f32[8,144]{1,0:T(8,128)S(1)} %get-tuple-element.78), channel_id=1, source_target_pairs={{0,500},{500,0},{8,508},{508,8},{16,4},{4,16},{24,12},{12,24},{32,... | collective-permute-start | bytes 13832 | tf_op jit(solution)/shard_map/ppermute | solution.py:358
  39.8 4.5 %collective-permute-start.8 = (f32[8,144]{1,0:T(8,128)S(1)}, f32[8,144]{1,0:T(8,128)S(1)}, u32[]{:S(2)}, u32[]{:S(2)}) collective-permute-start(f32[8,144]{1,0:T(8,128)S(1)} %get-tuple-element.79), channel_id=1, source_target_pairs={{0,256},{4,260},{8,264},{12,268},{16,272},{20,276},{24,280},{28,28... | collective-permute-start | bytes 13832 | tf_op jit(solution)/shard_map/ppermute | solution.py:358
  44.3 6.3 %collective-permute-start.11 = (f32[8,144]{1,0:T(8,128)S(1)}, f32[8,144]{1,0:T(8,128)S(1)}, u32[]{:S(2)}, u32[]{:S(2)}) collective-permute-start(f32[8,144]{1,0:T(8,128)S(1)} %get-tuple-element.82), channel_id=1, source_target_pairs={{0,508},{508,0},{8,4},{4,8},{16,12},{12,16},{24,20},{20,24},{32,28... | collective-permute-start | bytes 13832 | tf_op jit(solution)/shard_map/ppermute | solution.py:358
  50.7 2.0 %collective-permute-start.12 = (f32[8,144]{1,0:T(8,128)S(1)}, f32[8,144]{1,0:T(8,128)S(1)}, u32[]{:S(2)}, u32[]{:S(2)}) collective-permute-start(f32[8,144]{1,0:T(8,128)S(1)} %get-tuple-element.83), channel_id=1, source_target_pairs={{0,12},{12,0},{8,20},{20,8},{16,28},{28,16},{24,36},{36,24},{32,44... | collective-permute-start | bytes 13832 | tf_op jit(solution)/shard_map/ppermute | solution.py:358
  52.6 5.5 %collective-permute-start.9 = (f32[16,144]{1,0:T(8,128)S(1)}, f32[16,144]{1,0:T(8,128)S(1)}, u32[]{:S(2)}, u32[]{:S(2)}) collective-permute-start(f32[16,144]{1,0:T(8,128)S(1)} %get-tuple-element.80), channel_id=1, source_target_pairs={{0,1},{1,0},{2,3},{3,2},{4,5},{5,4},{6,7},{7,6},{8,9},{9,8},{10,11... | collective-permute-start | bytes 27656 | tf_op jit(solution)/shard_map/ppermute | solution.py:364
  58.2 0.7 %collective-permute-start.10 = (f32[16,144]{1,0:T(8,128)S(1)}, f32[16,144]{1,0:T(8,128)S(1)}, u32[]{:S(2)}, u32[]{:S(2)}) collective-permute-start(f32[16,144]{1,0:T(8,128)S(1)} %get-tuple-element.81), channel_id=1, source_target_pairs={{1,2},{2,1},{5,6},{6,5},{9,10},{10,9},{13,14},{14,13},{17,18},{18,... | collective-permute-start | bytes 27656 | tf_op jit(solution)/shard_map/ppermute | solution.py:364
  58.9 1.9 %collective-permute-start.13 = (f32[24,144]{1,0:T(8,128)S(1)}, f32[24,144]{1,0:T(8,128)S(1)}, u32[]{:S(2)}, u32[]{:S(2)}) collective-permute-start(f32[24,144]{1,0:T(8,128)S(1)} %get-tuple-element.84), channel_id=1, source_target_pairs={{0,4},{4,0},{8,12},{12,8},{16,20},{20,16},{24,28},{28,24},{32,36},... | collective-permute-start | bytes 41480 | tf_op jit(solution)/shard_map/ppermute | solution.py:358
  60.8 1.0 %shard_map.121 = (f32[9,40,128]{2,1,0:T(8,128)S(1)}, f32[64,1152]{1,0:T(8,128)S(1)}, f32[288,512]{1,0:T(8,128)S(1)}) custom-call(f32[9,40,128]{2,1,0:T(8,128)S(1)} %get-tuple-element.69.middle, bf16[144,1152]{1,0:T(8,128)(2,1)S(1)} %get-tuple-element.70.x, f32[64,1152]{1,0:T(8,128)S(1)} %get-tuple-element.71.s, bf16[288,512]{1,0:T(8,128)(2,1)S(1)} %get-tuple-element.72.l, ...), custom_call_target="tpu_custom_call" | custom-call | flops 200000000 | bytes 2000000 | tf_op jit(solution)/shard_map/pallas_call | solution.py:336
  61.8 0.1 collective-permute-done.13.rest_6_
  61.9 1.5 %shard_map.122 = f32[9,35,128]{2,1,0:T(8,128)} custom-call(f32[9,40,128]{2,1,0:T(8,128)S(1)} %get-tuple-element.75.held, f32[64,1152]{1,0:T(8,128)S(1)} %get-tuple-element.76.own, f32[288,512]{1,0:T(8,128)S(1)} %get-tuple-element.77.picked, bf16[80,512]{1,0:T(8,128)(2,1)S(1)} %get-tuple-element.53.hot, s32[16,128]{1,0:T(8,128)S(1)} %get-tuple-element.48.marks, ...), custom_call_target="tpu_custom_call" | custom-call | flops 100000000 | bytes 2000000 | tf_op jit(solution)/shard_map/pallas_call | solution.py:336
  (31 shorter events, 0.1 us)
Async XLA Ops:
  0.0 1.8 %copy-start = (f32[9,35,128]{2,1,0:T(8,128)S(1)}, f32[9,35,128]{2,1,0:T(8,128)}, u32[]{:S(2)}) copy-start(f32[9,35,128]{2,1,0:T(8,128)} %state.3) | copy-start | bytes 483844
  0.8 1.0 %copy-start.1 = (f32[3,35,35]{2,1,0:T(8,128)S(1)}, f32[3,35,35]{2,1,0:T(8,128)}, u32[]{:S(2)}) copy-start(f32[3,35,35]{2,1,0:T(8,128)} %stiffness.3) | copy-start | bytes 44104
  0.8 1.0 %copy-start.5 = (s32[1,1024]{1,0:T(1,128)S(1)}, s32[1,1024]{1,0:T(1,128)}, u32[]{:S(2)}) copy-start(s32[1,1024]{1,0:T(1,128)} %plane.1) | copy-start | bytes 12292
  0.8 1.0 %copy-start.7 = (s32[4,128]{1,0:T(4,128)S(1)}, s32[4,128]{1,0:T(4,128)}, u32[]{:S(2)}) copy-start(s32[4,128]{1,0:T(4,128)} %orient.1) | copy-start | bytes 6148
  1.8 0.7 %copy-start.6 = (s32[4,128]{1,0:T(4,128)S(1)}, s32[4,128]{1,0:T(4,128)}, u32[]{:S(2)}) copy-start(s32[4,128]{1,0:T(4,128)} %neighbour.1) | copy-start | bytes 6148
  1.8 0.7 %copy-start.8 = (s32[2,16]{1,0:T(2,128)S(1)}, s32[2,16]{1,0:T(2,128)}, u32[]{:S(2)}) copy-start(s32[2,16]{1,0:T(2,128)} %thick.1) | copy-start | bytes 388
  1.8 0.7 %copy-start.9 = (s32[128]{0:T(128)S(1)}, s32[128]{0:T(128)}, u32[]{:S(2)}) copy-start(s32[128]{0:T(128)} %param.15) | copy-start | bytes 1540
  2.5 30.9 %copy-start.2 = (bf16[2,4,9,9,128]{4,1,3,2,0:T(4,128)(2,1)S(1)}, bf16[2,4,9,9,128]{4,1,3,2,0:T(4,128)(2,1)}, u32[]{:S(2)}) copy-start(bf16[2,4,9,9,128]{4,1,3,2,0:T(4,128)(2,1)} %param.14) | copy-start | bytes 497668
  2.5 30.9 %copy-start.3 = (f32[4,35,15]{1,0,2:T(4,128)S(1)}, f32[4,35,15]{1,0,2:T(4,128)}, u32[]{:S(2)}) copy-start(f32[4,35,15]{1,0,2:T(4,128)} %param.22) | copy-start | bytes 25204
  4.8 28.6 %copy-start.4 = (f32[3,15,15]{2,1,0:T(8,128)S(1)}, f32[3,15,15]{2,1,0:T(8,128)}, u32[]{:S(2)}) copy-start(f32[3,15,15]{2,1,0:T(8,128)} %rotations.1) | copy-start | bytes 8104
  4.8 26.0 %collective-permute-start = (f32[8,144]{1,0:T(8,128)S(1)}, f32[8,144]{1,0:T(8,128)S(1)}, u32[]{:S(2)}, u32[]{:S(2)}) collective-permute-start(f32[8,144]{1,0:T(8,128)S(1)} %get-tuple-element.62), channel_id=1, source_target_pairs={{0,500},{500,0},{8,508},{508,8},{16,4},{4,16},{24,12},{12,24},{32,... | collective-permute-start | bytes 13832 | tf_op jit(solution)/shard_map/ppermute | solution.py:358
  11.1 20.4 %collective-permute-start.1 = (f32[8,144]{1,0:T(8,128)S(1)}, f32[8,144]{1,0:T(8,128)S(1)}, u32[]{:S(2)}, u32[]{:S(2)}) collective-permute-start(f32[8,144]{1,0:T(8,128)S(1)} %get-tuple-element.63), channel_id=1, source_target_pairs={{0,256},{4,260},{8,264},{12,268},{16,272},{20,276},{24,280},{28,28... | collective-permute-start | bytes 13832 | tf_op jit(solution)/shard_map/ppermute | solution.py:358
  15.9 18.6 %collective-permute-start.4 = (f32[8,144]{1,0:T(8,128)S(1)}, f32[8,144]{1,0:T(8,128)S(1)}, u32[]{:S(2)}, u32[]{:S(2)}) collective-permute-start(f32[8,144]{1,0:T(8,128)S(1)} %get-tuple-element.66), channel_id=1, source_target_pairs={{0,508},{508,0},{8,4},{4,8},{16,12},{12,16},{24,20},{20,24},{32,28... | collective-permute-start | bytes 13832 | tf_op jit(solution)/shard_map/ppermute | solution.py:358
  25.1 9.4 %collective-permute-start.5 = (f32[8,144]{1,0:T(8,128)S(1)}, f32[8,144]{1,0:T(8,128)S(1)}, u32[]{:S(2)}, u32[]{:S(2)}) collective-permute-start(f32[8,144]{1,0:T(8,128)S(1)} %get-tuple-element.67), channel_id=1, source_target_pairs={{0,12},{12,0},{8,20},{20,8},{16,28},{28,16},{24,36},{36,24},{32,44... | collective-permute-start | bytes 13832 | tf_op jit(solution)/shard_map/ppermute | solution.py:358
  27.6 6.9 %collective-permute-start.2 = (f32[16,144]{1,0:T(8,128)S(1)}, f32[16,144]{1,0:T(8,128)S(1)}, u32[]{:S(2)}, u32[]{:S(2)}) collective-permute-start(f32[16,144]{1,0:T(8,128)S(1)} %get-tuple-element.64), channel_id=1, source_target_pairs={{0,1},{1,0},{2,3},{3,2},{4,5},{5,4},{6,7},{7,6},{8,9},{9,8},{10,11... | collective-permute-start | bytes 27656 | tf_op jit(solution)/shard_map/ppermute | solution.py:364
  30.8 3.8 %collective-permute-start.3 = (f32[16,144]{1,0:T(8,128)S(1)}, f32[16,144]{1,0:T(8,128)S(1)}, u32[]{:S(2)}, u32[]{:S(2)}) collective-permute-start(f32[16,144]{1,0:T(8,128)S(1)} %get-tuple-element.65), channel_id=1, source_target_pairs={{1,2},{2,1},{5,6},{6,5},{9,10},{10,9},{13,14},{14,13},{17,18},{18,... | collective-permute-start | bytes 27656 | tf_op jit(solution)/shard_map/ppermute | solution.py:364
  31.4 3.1 %collective-permute-start.6 = (f32[24,144]{1,0:T(8,128)S(1)}, f32[24,144]{1,0:T(8,128)S(1)}, u32[]{:S(2)}, u32[]{:S(2)}) collective-permute-start(f32[24,144]{1,0:T(8,128)S(1)} %get-tuple-element.68), channel_id=1, source_target_pairs={{0,4},{4,0},{8,12},{12,8},{16,20},{20,16},{24,28},{28,24},{32,36},... | collective-permute-start | bytes 41480 | tf_op jit(solution)/shard_map/ppermute | solution.py:358
  36.9 21.2 %collective-permute-start.7 = (f32[8,144]{1,0:T(8,128)S(1)}, f32[8,144]{1,0:T(8,128)S(1)}, u32[]{:S(2)}, u32[]{:S(2)}) collective-permute-start(f32[8,144]{1,0:T(8,128)S(1)} %get-tuple-element.78), channel_id=1, source_target_pairs={{0,500},{500,0},{8,508},{508,8},{16,4},{4,16},{24,12},{12,24},{32,... | collective-permute-start | bytes 13832 | tf_op jit(solution)/shard_map/ppermute | solution.py:358
  39.8 19.0 %collective-permute-start.8 = (f32[8,144]{1,0:T(8,128)S(1)}, f32[8,144]{1,0:T(8,128)S(1)}, u32[]{:S(2)}, u32[]{:S(2)}) collective-permute-start(f32[8,144]{1,0:T(8,128)S(1)} %get-tuple-element.79), channel_id=1, source_target_pairs={{0,256},{4,260},{8,264},{12,268},{16,272},{20,276},{24,280},{28,28... | collective-permute-start | bytes 13832 | tf_op jit(solution)/shard_map/ppermute | solution.py:358
  44.3 17.4 %collective-permute-start.11 = (f32[8,144]{1,0:T(8,128)S(1)}, f32[8,144]{1,0:T(8,128)S(1)}, u32[]{:S(2)}, u32[]{:S(2)}) collective-permute-start(f32[8,144]{1,0:T(8,128)S(1)} %get-tuple-element.82), channel_id=1, source_target_pairs={{0,508},{508,0},{8,4},{4,8},{16,12},{12,16},{24,20},{20,24},{32,28... | collective-permute-start | bytes 13832 | tf_op jit(solution)/shard_map/ppermute | solution.py:358
  50.7 11.1 %collective-permute-start.12 = (f32[8,144]{1,0:T(8,128)S(1)}, f32[8,144]{1,0:T(8,128)S(1)}, u32[]{:S(2)}, u32[]{:S(2)}) collective-permute-start(f32[8,144]{1,0:T(8,128)S(1)} %get-tuple-element.83), channel_id=1, source_target_pairs={{0,12},{12,0},{8,20},{20,8},{16,28},{28,16},{24,36},{36,24},{32,44... | collective-permute-start | bytes 13832 | tf_op jit(solution)/shard_map/ppermute | solution.py:358
  52.6 9.1 %collective-permute-start.9 = (f32[16,144]{1,0:T(8,128)S(1)}, f32[16,144]{1,0:T(8,128)S(1)}, u32[]{:S(2)}, u32[]{:S(2)}) collective-permute-start(f32[16,144]{1,0:T(8,128)S(1)} %get-tuple-element.80), channel_id=1, source_target_pairs={{0,1},{1,0},{2,3},{3,2},{4,5},{5,4},{6,7},{7,6},{8,9},{9,8},{10,11... | collective-permute-start | bytes 27656 | tf_op jit(solution)/shard_map/ppermute | solution.py:364
  58.2 3.6 %collective-permute-start.10 = (f32[16,144]{1,0:T(8,128)S(1)}, f32[16,144]{1,0:T(8,128)S(1)}, u32[]{:S(2)}, u32[]{:S(2)}) collective-permute-start(f32[16,144]{1,0:T(8,128)S(1)} %get-tuple-element.81), channel_id=1, source_target_pairs={{1,2},{2,1},{5,6},{6,5},{9,10},{10,9},{13,14},{14,13},{17,18},{18,... | collective-permute-start | bytes 27656 | tf_op jit(solution)/shard_map/ppermute | solution.py:364
  58.9 3.1 %collective-permute-start.13 = (f32[24,144]{1,0:T(8,128)S(1)}, f32[24,144]{1,0:T(8,128)S(1)}, u32[]{:S(2)}, u32[]{:S(2)}) collective-permute-start(f32[24,144]{1,0:T(8,128)S(1)} %get-tuple-element.84), channel_id=1, source_target_pairs={{0,4},{4,0},{8,12},{12,8},{16,20},{20,16},{24,28},{28,24},{32,36},... | collective-permute-start | bytes 41480 | tf_op jit(solution)/shard_map/ppermute | solution.py:358

commit v2 on v1

v2 whole, which is shorter than its diff:
```python
import jax
import jax.numpy as jnp
from jax import lax
from jax.experimental import pallas as pl
from jax.experimental.pallas import tpu as pltpu
from jax.sharding import PartitionSpec as P

F32, BF16 = jnp.float32, jnp.bfloat16
Q, B, A, ORDER = 9, 35, 15, 5
E = 128
PAD = 48
AP = 16
THICK, PLANE = 9, 16
SLOT, LAY = 8, 16
CUTS = 5 * SLOT + 2 * LAY
CP = 80
WIDE = Q * E
ALL = 4 * E

EARLY = [0.5 ** (k + 1) for k in range(ORDER)]
LATE = [1.0 - 0.5 ** (k + 1) for k in range(ORDER)]
FACT = [1.0, 2.0, 6.0, 24.0, 120.0]
STEPS = [(24, 48), (16, 48), (8, 32), (8, 16)]


def dot(a, b):
    return jnp.dot(a, b, preferred_element_type=F32)


def halves(x):
    top = x.astype(BF16)
    return top, (x - top.astype(F32)).astype(BF16)


def tripled(a):
    top = a.astype(BF16).astype(F32)
    return jnp.concatenate([top, top, a - top], axis=1).astype(BF16)


def padded(a, rows, cols):
    r, c = a.shape
    if c < cols:
        a = jnp.concatenate([a, jnp.zeros((r, cols - c), a.dtype)], axis=1)
    if r < rows:
        a = jnp.concatenate([a, jnp.zeros((rows - r, cols), a.dtype)], axis=0)
    return a


def lanes(p):
    return slice(p * E, (p + 1) * E)


def put_stack(ref, p, value, at=0, reach=PAD):
    top, rest = halves(value)
    for n, part in enumerate((top, rest, top)):
        ref[n * reach + at : n * reach + at + value.shape[0], lanes(p)] = part


def stiff_rows(stiffness):
    return [tripled(padded(stiffness[d][0:24], 24, PAD)).astype(F32) for d in range(3)]


def trace_rows(trace_maps):
    blocks = [tripled(padded(trace_maps[:, f, :], AP, PAD)).astype(F32) for f in range(4)]
    return jnp.concatenate(blocks, axis=0).astype(BF16)


def volume_rows(stiffness):
    blocks = [tripled(padded(stiffness[d].T, 40, PAD)).astype(F32) for d in range(3)]
    return jnp.concatenate(blocks, axis=0).astype(BF16)


def lift_rows(lift_maps):
    return tripled(jnp.concatenate([padded(lift_maps[:, f, :].T, 40, AP) for f in range(4)], axis=1))


def turn_rows(face_rotations):
    blocks = [tripled(padded(face_rotations[h], AP, AP)).astype(F32) for h in range(3)]
    return jnp.concatenate(blocks, axis=0)


def widen(source, target, blocks):
    for n in range(blocks):
        target[n] = source[n].astype(F32)


def star_apply(y, stars, rows):
    def one(p, total):
        total = list(total)
        at = pl.ds(pl.multiple_of(p * E, E), E)
        for d in range(3):
            value = y[d * rows : (d + 1) * rows, at]
            for q in range(Q):
                total[q] = total[q] + stars[q * Q + p, d : d + 1, :] * value
        return tuple(total)

    start = tuple(jnp.zeros((rows, E), F32) for _ in range(Q))
    return lax.fori_loop(0, Q, one, start, unroll=Q if rows < 40 else 3)


def taylor(first, steps, stars, x, y, add):
    values = [first[q] for q in range(Q)]
    for k, (rows, writes) in enumerate(STEPS):
        for p in range(Q):
            put_stack(x, p, padded(values[p], writes, E))
        y[0 : 3 * rows, :] = dot(steps[k][...], x[...])
        values = star_apply(y, stars, rows)
        for q in range(Q):
            add(k + 1, q, rows, values[q])


def far_steps(count):
    return (count - 3, count // 2)


def near_steps(count):
    return (count - 1, 3, 1)


def shared_faces(marks):
    dom, ply = lax.axis_index("dom"), lax.axis_index("ply")
    count = lax.axis_size("dom")
    odd, high = lax.rem(dom, 2), lax.rem(ply, 2)

    def column(row, start):
        dims = (SLOT, row.shape[1])
        sub = lax.broadcasted_iota(jnp.int32, dims, 0)
        lane = lax.broadcasted_iota(jnp.int32, dims, 1)
        picked = jnp.where(lane == sub + start, row.astype(F32), 0.0)
        return jnp.sum(picked, axis=1, keepdims=True)

    def plane_column(step):
        peer = lax.rem(dom + jnp.where(odd == 0, step, count - step), count)
        tile = E // SLOT
        return column(marks[pl.ds(PLANE + peer // tile, 1), :], lax.rem(peer, tile) * SLOT)

    def thick_columns(row):
        values = marks[pl.ds(THICK + row, 1), :]
        return [column(values, half) for half in (0, SLOT)]

    return (
        [plane_column(step) for step in far_steps(count)]
        + thick_columns(1 - high)
        + thick_columns(high)
        + [plane_column(step) for step in near_steps(count)]
    )


def pick_shared(marks, hot):
    columns = shared_faces(marks)
    columns.append(jnp.full((SLOT, 1), -1.0, F32))
    lane = lax.broadcasted_iota(jnp.int32, (AP, E), 1).astype(F32)
    for n in range(0, len(columns), 2):
        column = jnp.concatenate(columns[n : n + 2], axis=0)
        for f in range(4):
            hot[n * SLOT : (n + 2) * SLOT, lanes(f)] = jnp.where(
                column == lane + float(f * E), 1.0, 0.0
            ).astype(BF16)


def send_traces(s, hot, l, outs):
    split_traces(s, l)
    total = None
    for part in (1, 0):
        piece = lax.dot_general(
            hot[...],
            l[part * Q * AP : (part + 1) * Q * AP, :],
            (((1,), (1,)), ((), ())),
            preferred_element_type=F32,
        )
        total = piece if total is None else total + piece
    at = 0
    for out in outs[:-1]:
        out[...] = total[at : at + out.shape[0]]
        at += out.shape[0]
    outs[-1][...] = jnp.zeros_like(outs[-1])
    outs[-1][0:SLOT] = total[at : at + SLOT]


def split_traces(s, l):
    for q in range(Q):
        for f in range(4):
            top, rest = halves(s[f * AP : (f + 1) * AP, lanes(q)])
            l[q * AP : (q + 1) * AP, lanes(f)] = top
            l[Q * AP + q * AP : Q * AP + (q + 1) * AP, lanes(f)] = rest


def first_kernel(state, stars, stiffness, trace_maps, marks,
                 x_out, s_out, coarse, hot, l, step1, step2, step3, traces, *rest):
    sends, (first, early, x, y) = rest[:7], rest[7:]
    steps = (step1, step2, step3, step3)
    blocks = stiff_rows(stiffness)
    for step, (rows, _) in zip(steps, STEPS):
        step[...] = jnp.concatenate([block[0:rows] for block in blocks], axis=0).astype(BF16)
    traces[...] = trace_rows(trace_maps)
    pick_shared(marks, hot)
    first[...] = jnp.zeros_like(first)
    first[:, 0:B, :] = state[...]
    early[...] = first[...] * EARLY[0]
    coarse[...] = first[:, 0:40, :] * LATE[0]

    def add(k, q, rows, value):
        sign = -1.0 if k % 2 else 1.0
        early[q, 0:rows, :] = early[q, 0:rows, :] + value * (sign * EARLY[k] / FACT[k])
        coarse[q, 0:rows, :] = coarse[q, 0:rows, :] + value * (sign * LATE[k] / FACT[k])

    taylor(first, steps, stars, x, y, add)
    for p in range(Q):
        put_stack(x_out, p, early[p])
    s_out[...] = dot(traces[...], x_out[...])
    send_traces(s_out, hot, l, sends)


def put_near(near, picked):
    for q in range(Q):
        cols = slice(q * ALL, (q + 1) * ALL)
        near[0:AP, cols] = picked[q * AP : (q + 1) * AP].astype(BF16)
        near[AP : 2 * AP, cols] = picked[(Q + q) * AP : (Q + q + 1) * AP].astype(BF16)


def own_part(base, x, s, l, stars, solvers, volumes, same, held, own, near, y):
    put_near(near, dot(l[...], same[...]))
    y[...] = dot(volumes[...], x[...])
    sums = star_apply(y, stars, 40)
    for q in range(Q):
        held[q] = base(q) + sums[q]
    for f, rows, total in fluxes(solvers, 0, s, None):
        for q in range(Q):
            own[rows, lanes(q)] = total[q]


def fluxes(solvers, side, values, before):
    for f in range(4):
        rows = slice(f * AP, (f + 1) * AP)

        def face(p, total):
            total = list(total)
            at = pl.ds(pl.multiple_of(p * E, E), E)
            value = values[rows, at]
            for q in range(Q):
                total[q] = total[q] + solvers[(side * Q + q) * Q + p, f : f + 1, :] * value
            return tuple(total)

        start = [jnp.zeros((AP, E), F32) if before is None else before[rows, lanes(q)] for q in range(Q)]
        total = lax.fori_loop(0, Q, face, tuple(start), unroll=Q)
        yield f, rows, total


def early_own_kernel(state, x, s, l, stars, flux, marks, stiffness, lift_maps, rotations,
                     held, own, near, solvers, same, volumes, lifts, turns, padded_state, y):
    widen(flux, solvers, 2 * Q * Q)
    sub = lax.broadcasted_iota(jnp.int32, (ALL, E), 0)
    for f in range(4):
        same[:, lanes(f)] = jnp.where(sub == marks[f : f + 1, :], 1.0, 0.0).astype(BF16)
    volumes[...] = volume_rows(stiffness)
    lifts[...] = lift_rows(lift_maps)
    turns[...] = turn_rows(rotations).astype(BF16)
    padded_state[...] = jnp.zeros_like(padded_state)
    padded_state[:, 0:B, :] = state[...]
    own_part(lambda q: padded_state[q], x, s, l, stars, solvers, volumes, same, held, own, near, y)


def late_own_kernel(middle, x, s, l, stars, solvers, volumes, same, held, own, near, y):
    own_part(lambda q: middle[q], x, s, l, stars, solvers, volumes, same, held, own, near, y)


def finished(held, own, near, arrived, hot, marks, solvers, lifts, turns, o, g, y):
    landed = jnp.concatenate(
        [ref[...] for ref in arrived[:-1]]
        + [arrived[-1][0:SLOT], jnp.zeros((CP - CUTS, Q * AP), F32)],
        axis=0,
    )
    pieces = [
        lax.dot_general(piece, hot[...], (((0,), (0,)), ((), ())), preferred_element_type=F32)
        for piece in halves(landed)
    ]
    ways = [jnp.broadcast_to(marks[4 + f : 5 + f, :], (AP, E)) for f in range(4)]
    masks = [(way == 0, way == 1) for way in ways]
    for q in range(Q):
        cols = slice(q * ALL, (q + 1) * ALL)
        top = near[0:AP, cols] + pieces[0][q * AP : (q + 1) * AP].astype(BF16)
        rest = near[AP : 2 * AP, cols] + pieces[1][q * AP : (q + 1) * AP].astype(BF16)
        turned = dot(turns[...], jnp.concatenate([top, rest, top], axis=0))
        for f in range(4):
            first, second = masks[f]
            o[f * AP : (f + 1) * AP, lanes(q)] = jnp.where(
                first,
                turned[0:AP, lanes(f)],
                jnp.where(second, turned[AP : 2 * AP, lanes(f)], turned[2 * AP : 3 * AP, lanes(f)]),
            )
    for f, rows, total in fluxes(solvers, 1, o, own):
        for q in range(Q):
            put_stack(g, q, total[q], f * AP, 4 * AP)
    y[...] = dot(lifts[...], g[...])
    return [held[q] - y[:, lanes(q)] for q in range(Q)]


def middle_kernel(held, own, near, coarse, hot, marks, stars, solvers, lifts, turns,
                  step1, step2, step3, traces, *rest):
    arrived, (middle, x_out, s_out, l), sends = rest[:7], rest[7:11], rest[11:18]
    first, late, x, y, lifted, o, g = rest[18:]
    values = finished(
        held, own, near, arrived, hot, marks, solvers, lifts, turns, o, g, lifted
    )
    for q in range(Q):
        first[q] = padded(values[q], PAD, E)
        middle[q] = values[q]
        late[q] = first[q] * EARLY[0]

    def add(k, q, rows, value):
        sign = -1.0 if k % 2 else 1.0
        late[q, 0:rows, :] = late[q, 0:rows, :] + value * (sign * EARLY[k] / FACT[k])

    taylor(first, (step1, step2, step3, step3), stars, x, y, add)
    fine = marks[8:9, :] == 1
    for q in range(Q):
        late[q, 0:40, :] = jnp.where(fine, late[q, 0:40, :], coarse[q])
        put_stack(x_out, q, late[q])
    s_out[...] = dot(traces[...], x_out[...])
    send_traces(s_out, hot, l, sends)


def last_kernel(held, own, near, hot, marks, solvers, lifts, turns, *rest):
    arrived, out, (o, g, lifted) = rest[:7], rest[7], rest[8:]
    values = finished(
        held, own, near, arrived, hot, marks, solvers, lifts, turns, o, g, lifted
    )
    for q in range(Q):
        out[q] = values[q][0:B]


def shape(dims, kind=F32):
    return jax.ShapeDtypeStruct(dims, kind)


CORE_ROWS = 24
SENDS = (
    [(SLOT, Q * AP)] * 2 + [(LAY, Q * AP)] * 2 + [(SLOT, Q * AP)] * 2 + [(CORE_ROWS, Q * AP)]
)
PADDED = pltpu.VMEM((Q, PAD, E), F32)
X = pltpu.VMEM((3 * PAD, WIDE), BF16)
Y = pltpu.VMEM((120, WIDE), F32)
SIDE = pltpu.VMEM((4 * AP, WIDE), F32)
STACK = pltpu.VMEM((12 * AP, WIDE), BF16)
LIFTED = pltpu.VMEM((40, WIDE), F32)


def call(kernel, operands, outs, scratch, flops):
    vmem = pl.BlockSpec(memory_space=pltpu.VMEM)
    return pl.pallas_call(
        kernel,
        out_shape=outs,
        in_specs=[vmem] * len(operands),
        out_specs=jax.tree.map(lambda _: vmem, outs),
        scratch_shapes=scratch,
        compiler_params=pltpu.CompilerParams(vmem_limit_bytes=40 * 1024 * 1024),
        cost_estimate=pl.CostEstimate(flops=flops, bytes_accessed=2_000_000, transcendentals=0),
    )(*operands)


def exchange(blocks):
    count, layers = lax.axis_size("dom"), lax.axis_size("ply")

    def along_dom(step, block):
        if step % 2 == 0:
            pairs = [(i, (i + step) % count) for i in range(count)]
        else:
            pairs = []
            for even in range(0, count, 2):
                other = (even + step) % count
                pairs += [(even, other), (other, even)]
        return lax.ppermute(block, "dom", pairs)

    def along_ply(start, block):
        pairs = []
        for low in range(start, layers - 1, 2):
            pairs += [(low, low + 1), (low + 1, low)]
        return lax.ppermute(block, "ply", pairs)

    return (
        [along_dom(step, block) for step, block in zip(far_steps(count), blocks)]
        + [along_ply(start, block) for start, block in zip((0, 1), blocks[2:])]
        + [along_dom(step, block) for step, block in zip(near_steps(count), blocks[4:])]
    )


def body(state, star, flux, cluster, neighbour, orient, plane, thick,
         stiffness, trace_maps, lift_maps, rotations):
    stars = star.transpose(1, 2, 0, 3).reshape(Q * Q, 3, E).astype(F32)
    flux = flux.transpose(0, 2, 3, 1, 4).reshape(2 * Q * Q, 4, E)
    trace_maps = trace_maps.transpose(1, 0, 2)
    lift_maps = lift_maps.transpose(2, 0, 1)
    marks = jnp.concatenate(
        [
            neighbour,
            orient,
            cluster.reshape(1, E),
            jnp.pad(thick, ((0, 0), (0, E - LAY))),
            jnp.zeros((PLANE - THICK - 2, E), jnp.int32),
            plane.reshape(-1, E),
        ],
        axis=0,
    )
    kept = [shape((3 * PAD, WIDE), BF16), shape((4 * AP, WIDE)), shape((Q, 40, E))]
    sends = [shape(dims) for dims in SENDS]
    split = shape((2 * Q * AP, ALL), BF16)
    products = [shape((3 * rows, 3 * PAD), BF16) for rows, _ in STEPS[:3]]
    products.append(shape((4 * AP, 3 * PAD), BF16))
    own_outs = [kept[2], kept[1], shape((2 * AP, Q * ALL), BF16)]
    x_early, s_early, coarse, hot, l_early, *rest = call(
        first_kernel,
        (state, stars, stiffness, trace_maps, marks),
        kept + [shape((CP, ALL), BF16), split]
        + products + sends,
        [PADDED, PADDED, X, Y],
        100_000_000,
    )
    steps, out_early = rest[:4], rest[4:]
    in_early = exchange(out_early)
    held, own, near, solvers, same, volumes, lifts, turns = call(
        early_own_kernel,
        (state, x_early, s_early, l_early, stars, flux, marks, stiffness, lift_maps, rotations),
        own_outs + [
            shape((2 * Q * Q, 4, E)), shape((ALL, ALL), BF16), shape((120, 3 * PAD), BF16),
            shape((40, 12 * AP), BF16), shape((3 * AP, 3 * AP), BF16),
        ],
        [pltpu.VMEM((Q, 40, E), F32), Y], 200_000_000,
    )
    middle, x_late, s_late, l_late, *out_late = call(
        middle_kernel,
        (held, own, near, coarse, hot, marks, stars, solvers, lifts, turns, *steps,
         *in_early),
        [kept[2], kept[0], kept[1], split] + sends,
        [PADDED, PADDED, X, Y, LIFTED, SIDE, STACK], 200_000_000,
    )
    in_late = exchange(out_late)
    held, own, near = call(
        late_own_kernel, (middle, x_late, s_late, l_late, stars, solvers, volumes, same),
        own_outs, [Y], 200_000_000,
    )
    return call(
        last_kernel, (held, own, near, hot, marks, solvers, lifts, turns, *in_late),
        shape((Q, B, E)), [SIDE, STACK, LIFTED], 100_000_000,
    )


def solution(mesh):
    both = ("dom", "ply")
    in_specs = (
        P(None, None, both),
        P(None, None, None, both),
        P(None, None, None, None, both),
        P(both),
        P(None, both),
        P(None, both),
        P(both, None),
        P(both, None),
        P(),
        P(),
        P(),
        P(),
    )
    return jax.shard_map(
        body, mesh=mesh, in_specs=in_specs, out_specs=P(None, None, both), check_vma=False
    )
```

time: 64 us -> 63.1 us (0.986)
  local copies, waits for them, and re-layouts: 1.46 us -> 0.73 us
    unnamed x21 -> x22, local copies, waits for them, and re-layouts: 1.46 us -> 0.67 us
where the time goes in v2:
time: 63.1 us; the launch traced here: 62.5 us
  starting transfers between devices  52.3 us (83%)
  Pallas kernels  7.89 us (13%)
  other arithmetic  1.04 us (2%)
  local copies, waits for them, and re-layouts  0.73 us (1%)
    ppermute x10, starting transfers between devices, along_dom(): return lax.ppermute(block, 'dom', pairs)  42.4 us
    ppermute x4, starting transfers between devices, along_ply(): return lax.ppermute(block, 'ply', pairs)  9.96 us
    pallas_call x5, Pallas kernels, call(): pl.pallas_call(kernel, out_shape=outs, in_specs=[vmem] * len(operands), o...  7.89 us
  transfers between devices with their start and end apart: 14, of which 1 were waited for; matrix products, arithmetic and copies ran while one was open for 0% of the time, Pallas kernels for 3%

profile of v2, /device:TPU:1, one launch (start us, length us, event | category | flops | bytes accessed | tf_op | source)
XLA Modules:
  0.0 62.5 jit_solution(5803359150502441271)
XLA Ops:
  0.0 1.0 %convert_element_type.11 = f32[3,9,9,128]{3,0,2,1:T(4,128)S(1)} convert(bf16[3,9,9,128]{3,0,2,1:T(4,128)(2,1)} %param.13) | non-fusion elementwise | flops 31104 | bytes 186624 | tf_op jit(solution)/shard_map/convert_element_type | solution.py:389
  1.1 0.0 copy-start.3
  1.2 0.6 %copy-done.3 = f32[4,15,35]{2,0,1:T(4,128)S(1)} copy-done((f32[4,15,35]{2,0,1:T(4,128)S(1)}, f32[4,15,35]{2,0,1:T(4,128)}, u32[]{:S(2)}) %copy-start.3) | copy-done | bytes 8424
  1.9 1.7 %shard_map.118 = (bf16[144,1152]{1,0:T(8,128)(2,1)S(1)}, f32[64,1152]{1,0:T(8,128)S(1)}, f32[9,40,128]{2,1,0:T(8,128)S(1)}, bf16[80,512]{1,0:T(8,128)(2,1)S(1)},...) custom-call(f32[9,35,128]{2,1,0:T(8,128)S(1)} %copy-done, ...), custom_call_target="tpu_custom_call" | custom-call | flops 100000000 | bytes 2000000 | tf_op jit(solution)/shard_map/pallas_call | solution.py:350
  3.6 6.3 %collective-permute-start = (f32[8,144]{1,0:T(8,128)S(1)}, f32[8,144]{1,0:T(8,128)S(1)}, u32[]{:S(2)}, u32[]{:S(2)}) collective-permute-start(f32[8,144]{1,0:T(8,128)S(1)} %get-tuple-element.58), channel_id=1, source_target_pairs={{0,500},{500,0},{8,508},{508,8},{16,4},{4,16},{24,12},{12,24},{32,... | collective-permute-start | bytes 13832 | tf_op jit(solution)/shard_map/ppermute | solution.py:372
  9.9 4.8 %collective-permute-start.1 = (f32[8,144]{1,0:T(8,128)S(1)}, f32[8,144]{1,0:T(8,128)S(1)}, u32[]{:S(2)}, u32[]{:S(2)}) collective-permute-start(f32[8,144]{1,0:T(8,128)S(1)} %get-tuple-element.59), channel_id=1, source_target_pairs={{0,256},{4,260},{8,264},{12,268},{16,272},{20,276},{24,280},{28,28... | collective-permute-start | bytes 13832 | tf_op jit(solution)/shard_map/ppermute | solution.py:372
  14.7 9.2 %collective-permute-start.4 = (f32[8,144]{1,0:T(8,128)S(1)}, f32[8,144]{1,0:T(8,128)S(1)}, u32[]{:S(2)}, u32[]{:S(2)}) collective-permute-start(f32[8,144]{1,0:T(8,128)S(1)} %get-tuple-element.62), channel_id=1, source_target_pairs={{0,508},{508,0},{8,4},{4,8},{16,12},{12,16},{24,20},{20,24},{32,28... | collective-permute-start | bytes 13832 | tf_op jit(solution)/shard_map/ppermute | solution.py:372
  23.9 2.5 %collective-permute-start.5 = (f32[8,144]{1,0:T(8,128)S(1)}, f32[8,144]{1,0:T(8,128)S(1)}, u32[]{:S(2)}, u32[]{:S(2)}) collective-permute-start(f32[8,144]{1,0:T(8,128)S(1)} %get-tuple-element.63), channel_id=1, source_target_pairs={{0,12},{12,0},{8,20},{20,8},{16,28},{28,16},{24,36},{36,24},{32,44... | collective-permute-start | bytes 13832 | tf_op jit(solution)/shard_map/ppermute | solution.py:372
  26.5 3.1 %collective-permute-start.2 = (f32[16,144]{1,0:T(8,128)S(1)}, f32[16,144]{1,0:T(8,128)S(1)}, u32[]{:S(2)}, u32[]{:S(2)}) collective-permute-start(f32[16,144]{1,0:T(8,128)S(1)} %get-tuple-element.60), channel_id=1, source_target_pairs={{0,1},{1,0},{2,3},{3,2},{4,5},{5,4},{6,7},{7,6},{8,9},{9,8},{10,11... | collective-permute-start | bytes 27656 | tf_op jit(solution)/shard_map/ppermute | solution.py:378
  29.6 0.0 collective-permute-done.rest_0_
  29.6 0.7 %collective-permute-start.3 = (f32[16,144]{1,0:T(8,128)S(1)}, f32[16,144]{1,0:T(8,128)S(1)}, u32[]{:S(2)}, u32[]{:S(2)}) collective-permute-start(f32[16,144]{1,0:T(8,128)S(1)} %get-tuple-element.61), channel_id=1, source_target_pairs={{1,2},{2,1},{5,6},{6,5},{9,10},{10,9},{13,14},{14,13},{17,18},{18,... | collective-permute-start | bytes 27656 | tf_op jit(solution)/shard_map/ppermute | solution.py:378
  30.3 1.9 %collective-permute-start.6 = (f32[24,144]{1,0:T(8,128)S(1)}, f32[24,144]{1,0:T(8,128)S(1)}, u32[]{:S(2)}, u32[]{:S(2)}) collective-permute-start(f32[24,144]{1,0:T(8,128)S(1)} %get-tuple-element.64), channel_id=1, source_target_pairs={{0,4},{4,0},{8,12},{12,8},{16,20},{20,16},{24,28},{28,24},{32,36},... | collective-permute-start | bytes 41480 | tf_op jit(solution)/shard_map/ppermute | solution.py:372
  32.2 1.1 %shard_map.119 = (f32[9,40,128]{2,1,0:T(8,128)S(1)}, f32[64,1152]{1,0:T(8,128)S(1)}, bf16[32,4608]{1,0:T(8,128)(2,1)S(1)}, f32[162,4,128]{2,1,0:T(4,128)S(1)}, b...) custom-call(f32[9,35,128]{2,1,0:T(8,128)S(1)} %copy-done, ...), custom_call_target="tpu_custom_call" | custom-call | flops 200000000 | bytes 2000000 | tf_op jit(solution)/shard_map/pallas_call | solution.py:350
  33.4 2.5 %shard_map.120 = (f32[9,40,128]{2,1,0:T(8,128)S(1)}, bf16[144,1152]{1,0:T(8,128)(2,1)S(1)}, f32[64,1152]{1,0:T(8,128)S(1)}, bf16[288,512]{1,0:T(8,128)(2,1)S(1)}...) custom-call(f32[9,40,128]{2,1,0:T(8,128)S(1)} %get-tuple-element.46., ...), custom_call_target="tpu_custom_call" | custom-call | flops 200000000 | bytes 2000000 | tf_op jit(solution)/shard_map/pallas_call | solution.py:350
  35.9 2.9 %collective-permute-start.7 = (f32[8,144]{1,0:T(8,128)S(1)}, f32[8,144]{1,0:T(8,128)S(1)}, u32[]{:S(2)}, u32[]{:S(2)}) collective-permute-start(f32[8,144]{1,0:T(8,128)S(1)} %get-tuple-element.74), channel_id=1, source_target_pairs={{0,500},{500,0},{8,508},{508,8},{16,4},{4,16},{24,12},{12,24},{32,... | collective-permute-start | bytes 13832 | tf_op jit(solution)/shard_map/ppermute | solution.py:372
  38.8 4.5 %collective-permute-start.8 = (f32[8,144]{1,0:T(8,128)S(1)}, f32[8,144]{1,0:T(8,128)S(1)}, u32[]{:S(2)}, u32[]{:S(2)}) collective-permute-start(f32[8,144]{1,0:T(8,128)S(1)} %get-tuple-element.75), channel_id=1, source_target_pairs={{0,256},{4,260},{8,264},{12,268},{16,272},{20,276},{24,280},{28,28... | collective-permute-start | bytes 13832 | tf_op jit(solution)/shard_map/ppermute | solution.py:372
  43.3 6.3 %collective-permute-start.11 = (f32[8,144]{1,0:T(8,128)S(1)}, f32[8,144]{1,0:T(8,128)S(1)}, u32[]{:S(2)}, u32[]{:S(2)}) collective-permute-start(f32[8,144]{1,0:T(8,128)S(1)} %get-tuple-element.78), channel_id=1, source_target_pairs={{0,508},{508,0},{8,4},{4,8},{16,12},{12,16},{24,20},{20,24},{32,28... | collective-permute-start | bytes 13832 | tf_op jit(solution)/shard_map/ppermute | solution.py:372
  49.7 2.0 %collective-permute-start.12 = (f32[8,144]{1,0:T(8,128)S(1)}, f32[8,144]{1,0:T(8,128)S(1)}, u32[]{:S(2)}, u32[]{:S(2)}) collective-permute-start(f32[8,144]{1,0:T(8,128)S(1)} %get-tuple-element.79), channel_id=1, source_target_pairs={{0,12},{12,0},{8,20},{20,8},{16,28},{28,16},{24,36},{36,24},{32,44... | collective-permute-start | bytes 13832 | tf_op jit(solution)/shard_map/ppermute | solution.py:372
  51.6 5.5 %collective-permute-start.9 = (f32[16,144]{1,0:T(8,128)S(1)}, f32[16,144]{1,0:T(8,128)S(1)}, u32[]{:S(2)}, u32[]{:S(2)}) collective-permute-start(f32[16,144]{1,0:T(8,128)S(1)} %get-tuple-element.76), channel_id=1, source_target_pairs={{0,1},{1,0},{2,3},{3,2},{4,5},{5,4},{6,7},{7,6},{8,9},{9,8},{10,11... | collective-permute-start | bytes 27656 | tf_op jit(solution)/shard_map/ppermute | solution.py:378
  57.2 0.7 %collective-permute-start.10 = (f32[16,144]{1,0:T(8,128)S(1)}, f32[16,144]{1,0:T(8,128)S(1)}, u32[]{:S(2)}, u32[]{:S(2)}) collective-permute-start(f32[16,144]{1,0:T(8,128)S(1)} %get-tuple-element.77), channel_id=1, source_target_pairs={{1,2},{2,1},{5,6},{6,5},{9,10},{10,9},{13,14},{14,13},{17,18},{18,... | collective-permute-start | bytes 27656 | tf_op jit(solution)/shard_map/ppermute | solution.py:378
  57.9 1.9 %collective-permute-start.13 = (f32[24,144]{1,0:T(8,128)S(1)}, f32[24,144]{1,0:T(8,128)S(1)}, u32[]{:S(2)}, u32[]{:S(2)}) collective-permute-start(f32[24,144]{1,0:T(8,128)S(1)} %get-tuple-element.80), channel_id=1, source_target_pairs={{0,4},{4,0},{8,12},{12,8},{16,20},{20,16},{24,28},{28,24},{32,36},... | collective-permute-start | bytes 41480 | tf_op jit(solution)/shard_map/ppermute | solution.py:372
  59.8 1.0 %shard_map.121 = (f32[9,40,128]{2,1,0:T(8,128)S(1)}, f32[64,1152]{1,0:T(8,128)S(1)}, bf16[32,4608]{1,0:T(8,128)(2,1)S(1)}) custom-call(f32[9,40,128]{2,1,0:T(8,128)S(1)} %get-tuple-element.65.middle, bf16[144,1152]{1,0:T(8,128)(2,1)S(1)} %get-tuple-element.66.x, f32[64,1152]{1,0:T(8,128)S(1)} %get-tuple-element.67.s, ...), custom_call_target="tpu_custom_call" | custom-call | flops 200000000 | bytes 2000000 | tf_op jit(solution)/shard_map/pallas_call | solution.py:350
  60.8 0.2 collective-permute-done.13.rest_6_
  61.0 1.6 %shard_map.122 = f32[9,35,128]{2,1,0:T(8,128)} custom-call(f32[9,40,128]{2,1,0:T(8,128)S(1)} %get-tuple-element.71.held, f32[64,1152]{1,0:T(8,128)S(1)} %get-tuple-element.72.own, bf16[32,4608]{1,0:T(8,128)(2,1)S(1)} %get-tuple-element.73.near, bf16[80,512]{1,0:T(8,128)(2,1)S(1)} %get-tuple-element.50.hot, s32[24,128]{1,0:T(8,128)S(1)} %concatenate.3.marks, ...), custom_call_target="tpu_custom_call" | custom-call | flops 100000000 | bytes 2000000 | tf_op jit(solution)/shard_map/pallas_call | solution.py:350
  (35 shorter events, 0.1 us)
Async XLA Ops:
  0.0 1.1 %copy-start.9 = (s32[2,16]{1,0:T(2,128)S(1)}, s32[2,16]{1,0:T(2,128)}, u32[]{:S(2)}) copy-start(s32[2,16]{1,0:T(2,128)} %param.19) | copy-start | bytes 388
  0.0 1.2 %copy-start = (f32[9,35,128]{2,1,0:T(8,128)S(1)}, f32[9,35,128]{2,1,0:T(8,128)}, u32[]{:S(2)}) copy-start(f32[9,35,128]{2,1,0:T(8,128)} %state.3) | copy-start | bytes 483844
  0.0 1.1 %copy-start.6 = (s32[1,1024]{1,0:T(1,128)S(1)}, s32[1,1024]{1,0:T(1,128)}, u32[]{:S(2)}) copy-start(s32[1,1024]{1,0:T(1,128)} %param.18) | copy-start | bytes 12292
  0.0 1.1 %copy-start.7 = (s32[4,128]{1,0:T(4,128)S(1)}, s32[4,128]{1,0:T(4,128)}, u32[]{:S(2)}) copy-start(s32[4,128]{1,0:T(4,128)} %param.16) | copy-start | bytes 6148
  0.0 1.1 %copy-start.8 = (s32[4,128]{1,0:T(4,128)S(1)}, s32[4,128]{1,0:T(4,128)}, u32[]{:S(2)}) copy-start(s32[4,128]{1,0:T(4,128)} %param.17) | copy-start | bytes 6148
  0.0 1.1 %copy-start.10 = (s32[128]{0:T(128)S(1)}, s32[128]{0:T(128)}, u32[]{:S(2)}) copy-start(s32[128]{0:T(128)} %param.15) | copy-start | bytes 1540
  0.0 1.2 %copy-start.1 = (f32[3,35,35]{2,1,0:T(8,128)S(1)}, f32[3,35,35]{2,1,0:T(8,128)}, u32[]{:S(2)}) copy-start(f32[3,35,35]{2,1,0:T(8,128)} %stiffness.3) | copy-start | bytes 44104
  1.9 30.4 %copy-start.2 = (bf16[2,4,9,9,128]{4,1,3,2,0:T(4,128)(2,1)S(1)}, bf16[2,4,9,9,128]{4,1,3,2,0:T(4,128)(2,1)}, u32[]{:S(2)}) copy-start(bf16[2,4,9,9,128]{4,1,3,2,0:T(4,128)(2,1)} %param.14) | copy-start | bytes 497668
  1.9 30.4 %copy-start.4 = (f32[4,35,15]{1,0,2:T(4,128)S(1)}, f32[4,35,15]{1,0,2:T(4,128)}, u32[]{:S(2)}) copy-start(f32[4,35,15]{1,0,2:T(4,128)} %param.22) | copy-start | bytes 25204
  1.9 30.4 %copy-start.5 = (f32[3,15,15]{2,1,0:T(8,128)S(1)}, f32[3,15,15]{2,1,0:T(8,128)}, u32[]{:S(2)}) copy-start(f32[3,15,15]{2,1,0:T(8,128)} %rotations.1) | copy-start | bytes 8104
  3.6 26.0 %collective-permute-start = (f32[8,144]{1,0:T(8,128)S(1)}, f32[8,144]{1,0:T(8,128)S(1)}, u32[]{:S(2)}, u32[]{:S(2)}) collective-permute-start(f32[8,144]{1,0:T(8,128)S(1)} %get-tuple-element.58), channel_id=1, source_target_pairs={{0,500},{500,0},{8,508},{508,8},{16,4},{4,16},{24,12},{12,24},{32,... | collective-permute-start | bytes 13832 | tf_op jit(solution)/shard_map/ppermute | solution.py:372
  9.9 20.4 %collective-permute-start.1 = (f32[8,144]{1,0:T(8,128)S(1)}, f32[8,144]{1,0:T(8,128)S(1)}, u32[]{:S(2)}, u32[]{:S(2)}) collective-permute-start(f32[8,144]{1,0:T(8,128)S(1)} %get-tuple-element.59), channel_id=1, source_target_pairs={{0,256},{4,260},{8,264},{12,268},{16,272},{20,276},{24,280},{28,28... | collective-permute-start | bytes 13832 | tf_op jit(solution)/shard_map/ppermute | solution.py:372
  14.7 18.6 %collective-permute-start.4 = (f32[8,144]{1,0:T(8,128)S(1)}, f32[8,144]{1,0:T(8,128)S(1)}, u32[]{:S(2)}, u32[]{:S(2)}) collective-permute-start(f32[8,144]{1,0:T(8,128)S(1)} %get-tuple-element.62), channel_id=1, source_target_pairs={{0,508},{508,0},{8,4},{4,8},{16,12},{12,16},{24,20},{20,24},{32,28... | collective-permute-start | bytes 13832 | tf_op jit(solution)/shard_map/ppermute | solution.py:372
  23.9 9.4 %collective-permute-start.5 = (f32[8,144]{1,0:T(8,128)S(1)}, f32[8,144]{1,0:T(8,128)S(1)}, u32[]{:S(2)}, u32[]{:S(2)}) collective-permute-start(f32[8,144]{1,0:T(8,128)S(1)} %get-tuple-element.63), channel_id=1, source_target_pairs={{0,12},{12,0},{8,20},{20,8},{16,28},{28,16},{24,36},{36,24},{32,44... | collective-permute-start | bytes 13832 | tf_op jit(solution)/shard_map/ppermute | solution.py:372
  26.5 6.9 %collective-permute-start.2 = (f32[16,144]{1,0:T(8,128)S(1)}, f32[16,144]{1,0:T(8,128)S(1)}, u32[]{:S(2)}, u32[]{:S(2)}) collective-permute-start(f32[16,144]{1,0:T(8,128)S(1)} %get-tuple-element.60), channel_id=1, source_target_pairs={{0,1},{1,0},{2,3},{3,2},{4,5},{5,4},{6,7},{7,6},{8,9},{9,8},{10,11... | collective-permute-start | bytes 27656 | tf_op jit(solution)/shard_map/ppermute | solution.py:378
  29.6 3.8 %collective-permute-start.3 = (f32[16,144]{1,0:T(8,128)S(1)}, f32[16,144]{1,0:T(8,128)S(1)}, u32[]{:S(2)}, u32[]{:S(2)}) collective-permute-start(f32[16,144]{1,0:T(8,128)S(1)} %get-tuple-element.61), channel_id=1, source_target_pairs={{1,2},{2,1},{5,6},{6,5},{9,10},{10,9},{13,14},{14,13},{17,18},{18,... | collective-permute-start | bytes 27656 | tf_op jit(solution)/shard_map/ppermute | solution.py:378
  30.3 3.1 %collective-permute-start.6 = (f32[24,144]{1,0:T(8,128)S(1)}, f32[24,144]{1,0:T(8,128)S(1)}, u32[]{:S(2)}, u32[]{:S(2)}) collective-permute-start(f32[24,144]{1,0:T(8,128)S(1)} %get-tuple-element.64), channel_id=1, source_target_pairs={{0,4},{4,0},{8,12},{12,8},{16,20},{20,16},{24,28},{28,24},{32,36},... | collective-permute-start | bytes 41480 | tf_op jit(solution)/shard_map/ppermute | solution.py:372
  35.9 21.3 %collective-permute-start.7 = (f32[8,144]{1,0:T(8,128)S(1)}, f32[8,144]{1,0:T(8,128)S(1)}, u32[]{:S(2)}, u32[]{:S(2)}) collective-permute-start(f32[8,144]{1,0:T(8,128)S(1)} %get-tuple-element.74), channel_id=1, source_target_pairs={{0,500},{500,0},{8,508},{508,8},{16,4},{4,16},{24,12},{12,24},{32,... | collective-permute-start | bytes 13832 | tf_op jit(solution)/shard_map/ppermute | solution.py:372
  38.8 19.0 %collective-permute-start.8 = (f32[8,144]{1,0:T(8,128)S(1)}, f32[8,144]{1,0:T(8,128)S(1)}, u32[]{:S(2)}, u32[]{:S(2)}) collective-permute-start(f32[8,144]{1,0:T(8,128)S(1)} %get-tuple-element.75), channel_id=1, source_target_pairs={{0,256},{4,260},{8,264},{12,268},{16,272},{20,276},{24,280},{28,28... | collective-permute-start | bytes 13832 | tf_op jit(solution)/shard_map/ppermute | solution.py:372
  43.3 17.4 %collective-permute-start.11 = (f32[8,144]{1,0:T(8,128)S(1)}, f32[8,144]{1,0:T(8,128)S(1)}, u32[]{:S(2)}, u32[]{:S(2)}) collective-permute-start(f32[8,144]{1,0:T(8,128)S(1)} %get-tuple-element.78), channel_id=1, source_target_pairs={{0,508},{508,0},{8,4},{4,8},{16,12},{12,16},{24,20},{20,24},{32,28... | collective-permute-start | bytes 13832 | tf_op jit(solution)/shard_map/ppermute | solution.py:372
  49.7 11.1 %collective-permute-start.12 = (f32[8,144]{1,0:T(8,128)S(1)}, f32[8,144]{1,0:T(8,128)S(1)}, u32[]{:S(2)}, u32[]{:S(2)}) collective-permute-start(f32[8,144]{1,0:T(8,128)S(1)} %get-tuple-element.79), channel_id=1, source_target_pairs={{0,12},{12,0},{8,20},{20,8},{16,28},{28,16},{24,36},{36,24},{32,44... | collective-permute-start | bytes 13832 | tf_op jit(solution)/shard_map/ppermute | solution.py:372
  51.6 9.1 %collective-permute-start.9 = (f32[16,144]{1,0:T(8,128)S(1)}, f32[16,144]{1,0:T(8,128)S(1)}, u32[]{:S(2)}, u32[]{:S(2)}) collective-permute-start(f32[16,144]{1,0:T(8,128)S(1)} %get-tuple-element.76), channel_id=1, source_target_pairs={{0,1},{1,0},{2,3},{3,2},{4,5},{5,4},{6,7},{7,6},{8,9},{9,8},{10,11... | collective-permute-start | bytes 27656 | tf_op jit(solution)/shard_map/ppermute | solution.py:378
  57.2 3.6 %collective-permute-start.10 = (f32[16,144]{1,0:T(8,128)S(1)}, f32[16,144]{1,0:T(8,128)S(1)}, u32[]{:S(2)}, u32[]{:S(2)}) collective-permute-start(f32[16,144]{1,0:T(8,128)S(1)} %get-tuple-element.77), channel_id=1, source_target_pairs={{1,2},{2,1},{5,6},{6,5},{9,10},{10,9},{13,14},{14,13},{17,18},{18,... | collective-permute-start | bytes 27656 | tf_op jit(solution)/shard_map/ppermute | solution.py:378
  57.9 3.1 %collective-permute-start.13 = (f32[24,144]{1,0:T(8,128)S(1)}, f32[24,144]{1,0:T(8,128)S(1)}, u32[]{:S(2)}, u32[]{:S(2)}) collective-permute-start(f32[24,144]{1,0:T(8,128)S(1)} %get-tuple-element.80), channel_id=1, source_target_pairs={{0,4},{4,0},{8,12},{12,8},{16,20},{20,16},{24,28},{28,24},{32,36},... | collective-permute-start | bytes 41480 | tf_op jit(solution)/shard_map/ppermute | solution.py:372
  (1 other events, 0.8 us)

commit v3 on v2

--- a/solution.py
+++ b/solution.py
@@ -110,11 +110,11 @@
 
 
 def far_steps(count):
-    return (count - 3, count // 2)
+    return (count - 1, 3, count - 3, count // 2)
 
 
 def near_steps(count):
-    return (count - 1, 3, 1)
+    return (1,)
 
 
 def shared_faces(marks):
@@ -264,7 +264,7 @@
     own_part(lambda q: middle[q], x, s, l, stars, solvers, volumes, same, held, own, near, y)
 
 
-def finished(held, own, near, arrived, hot, marks, solvers, lifts, turns, o, g, y):
+def finished(held, own, near, arrived, hot, marks, solvers, lifts, turns, o, g):
     landed = jnp.concatenate(
         [ref[...] for ref in arrived[:-1]]
         + [arrived[-1][0:SLOT], jnp.zeros((CP - CUTS, Q * AP), F32)],
@@ -291,16 +291,20 @@
     for f, rows, total in fluxes(solvers, 1, o, own):
         for q in range(Q):
             put_stack(g, q, total[q], f * AP, 4 * AP)
-    y[...] = dot(lifts[...], g[...])
-    return [held[q] - y[:, lanes(q)] for q in range(Q)]
+    results = []
+    for q in range(0, Q, 2):
+        group = range(q, min(q + 2, Q))
+        lifted = dot(lifts[...], g[:, q * E : (group[-1] + 1) * E])
+        results += [held[n] - lifted[:, lanes(n - q)] for n in group]
+    return results
 
 
 def middle_kernel(held, own, near, coarse, hot, marks, stars, solvers, lifts, turns,
                   step1, step2, step3, traces, *rest):
     arrived, (middle, x_out, s_out, l), sends = rest[:7], rest[7:11], rest[11:18]
-    first, late, x, y, lifted, o, g = rest[18:]
+    first, late, x, y, o, g = rest[18:]
     values = finished(
-        held, own, near, arrived, hot, marks, solvers, lifts, turns, o, g, lifted
+        held, own, near, arrived, hot, marks, solvers, lifts, turns, o, g
     )
     for q in range(Q):
         first[q] = padded(values[q], PAD, E)
@@ -321,9 +325,9 @@
 
 
 def last_kernel(held, own, near, hot, marks, solvers, lifts, turns, *rest):
-    arrived, out, (o, g, lifted) = rest[:7], rest[7], rest[8:]
+    arrived, out, (o, g) = rest[:7], rest[7], rest[8:]
     values = finished(
-        held, own, near, arrived, hot, marks, solvers, lifts, turns, o, g, lifted
+        held, own, near, arrived, hot, marks, solvers, lifts, turns, o, g
     )
     for q in range(Q):
         out[q] = values[q][0:B]
@@ -335,14 +339,13 @@
 
 CORE_ROWS = 24
 SENDS = (
-    [(SLOT, Q * AP)] * 2 + [(LAY, Q * AP)] * 2 + [(SLOT, Q * AP)] * 2 + [(CORE_ROWS, Q * AP)]
+    [(SLOT, Q * AP)] * 4 + [(LAY, Q * AP)] * 2 + [(CORE_ROWS, Q * AP)]
 )
 PADDED = pltpu.VMEM((Q, PAD, E), F32)
 X = pltpu.VMEM((3 * PAD, WIDE), BF16)
 Y = pltpu.VMEM((120, WIDE), F32)
 SIDE = pltpu.VMEM((4 * AP, WIDE), F32)
 STACK = pltpu.VMEM((12 * AP, WIDE), BF16)
-LIFTED = pltpu.VMEM((40, WIDE), F32)
 
 
 def call(kernel, operands, outs, scratch, flops):
@@ -379,8 +382,8 @@
 
     return (
         [along_dom(step, block) for step, block in zip(far_steps(count), blocks)]
-        + [along_ply(start, block) for start, block in zip((0, 1), blocks[2:])]
-        + [along_dom(step, block) for step, block in zip(near_steps(count), blocks[4:])]
+        + [along_ply(start, block) for start, block in zip((0, 1), blocks[4:])]
+        + [along_dom(step, block) for step, block in zip(near_steps(count), blocks[6:])]
     )
 
 
@@ -431,7 +434,7 @@
         (held, own, near, coarse, hot, marks, stars, solvers, lifts, turns, *steps,
          *in_early),
         [kept[2], kept[0], kept[1], split] + sends,
-        [PADDED, PADDED, X, Y, LIFTED, SIDE, STACK], 200_000_000,
+        [PADDED, PADDED, X, Y, SIDE, STACK], 200_000_000,
     )
     in_late = exchange(out_late)
     held, own, near = call(
@@ -440,7 +443,7 @@
     )
     return call(
         last_kernel, (held, own, near, hot, marks, solvers, lifts, turns, *in_late),
-        shape((Q, B, E)), [SIDE, STACK, LIFTED], 100_000_000,
+        shape((Q, B, E)), [SIDE, STACK], 100_000_000,
     )
 
 

time: 63.1 us -> 62.8 us (level)
  transfers between devices with their start and end apart: 14 -> 14, of which waited for: 1 -> 0; matrix products, arithmetic and copies ran while one was open for 0% -> 0% of each run, Pallas kernels for 3% -> 3%
where the time goes in v3:
time: 62.8 us; the launch traced here: 62.2 us
  starting transfers between devices  52.2 us (83%)
  Pallas kernels  7.91 us (13%)
  other arithmetic  1.04 us (2%)
  local copies, waits for them, and re-layouts  0.73 us (1%)
    ppermute x10, starting transfers between devices, along_dom(): return lax.ppermute(block, 'dom', pairs)  42.4 us
    ppermute x4, starting transfers between devices, along_ply(): return lax.ppermute(block, 'ply', pairs)  9.72 us
    pallas_call x5, Pallas kernels, call(): pl.pallas_call(kernel, out_shape=outs, in_specs=[vmem] * len(operands), o...  7.91 us
  transfers between devices with their start and end apart: 14, of which 0 were waited for; matrix products, arithmetic and copies ran while one was open for 0% of the time, Pallas kernels for 3%

profile of v3, /device:TPU:1, one launch (start us, length us, event | category | flops | bytes accessed | tf_op | source)
XLA Modules:
  0.0 62.2 jit_solution(330880248311154585)
XLA Ops:
  0.0 1.0 %convert_element_type.11 = f32[3,9,9,128]{3,0,2,1:T(4,128)S(1)} convert(bf16[3,9,9,128]{3,0,2,1:T(4,128)(2,1)} %param.13) | non-fusion elementwise | flops 31104 | bytes 186624 | tf_op jit(solution)/shard_map/convert_element_type | solution.py:392
  1.1 0.0 copy-start.3
  1.2 0.6 %copy-done.3 = f32[4,15,35]{2,0,1:T(4,128)S(1)} copy-done((f32[4,15,35]{2,0,1:T(4,128)S(1)}, f32[4,15,35]{2,0,1:T(4,128)}, u32[]{:S(2)}) %copy-start.3) | copy-done | bytes 8424
  1.9 1.7 %shard_map.118 = (bf16[144,1152]{1,0:T(8,128)(2,1)S(1)}, f32[64,1152]{1,0:T(8,128)S(1)}, f32[9,40,128]{2,1,0:T(8,128)S(1)}, bf16[80,512]{1,0:T(8,128)(2,1)S(1)},...) custom-call(f32[9,35,128]{2,1,0:T(8,128)S(1)} %copy-done, ...), custom_call_target="tpu_custom_call" | custom-call | flops 100000000 | bytes 2000000 | tf_op jit(solution)/shard_map/pallas_call | solution.py:353
  3.6 4.9 %collective-permute-start = (f32[8,144]{1,0:T(8,128)S(1)}, f32[8,144]{1,0:T(8,128)S(1)}, u32[]{:S(2)}, u32[]{:S(2)}) collective-permute-start(f32[8,144]{1,0:T(8,128)S(1)} %get-tuple-element.58), channel_id=1, source_target_pairs={{0,508},{508,0},{8,4},{4,8},{16,12},{12,16},{24,20},{20,24},{32,28... | collective-permute-start | bytes 13832 | tf_op jit(solution)/shard_map/ppermute | solution.py:375
  8.6 12.4 %collective-permute-start.1 = (f32[8,144]{1,0:T(8,128)S(1)}, f32[8,144]{1,0:T(8,128)S(1)}, u32[]{:S(2)}, u32[]{:S(2)}) collective-permute-start(f32[8,144]{1,0:T(8,128)S(1)} %get-tuple-element.59), channel_id=1, source_target_pairs={{0,12},{12,0},{8,20},{20,8},{16,28},{28,16},{24,36},{36,24},{32,44... | collective-permute-start | bytes 13832 | tf_op jit(solution)/shard_map/ppermute | solution.py:375
  21.0 1.9 %collective-permute-start.2 = (f32[8,144]{1,0:T(8,128)S(1)}, f32[8,144]{1,0:T(8,128)S(1)}, u32[]{:S(2)}, u32[]{:S(2)}) collective-permute-start(f32[8,144]{1,0:T(8,128)S(1)} %get-tuple-element.60), channel_id=1, source_target_pairs={{0,500},{500,0},{8,508},{508,8},{16,4},{4,16},{24,12},{12,24},{32,... | collective-permute-start | bytes 13832 | tf_op jit(solution)/shard_map/ppermute | solution.py:375
  22.9 2.3 %collective-permute-start.3 = (f32[8,144]{1,0:T(8,128)S(1)}, f32[8,144]{1,0:T(8,128)S(1)}, u32[]{:S(2)}, u32[]{:S(2)}) collective-permute-start(f32[8,144]{1,0:T(8,128)S(1)} %get-tuple-element.61), channel_id=1, source_target_pairs={{0,256},{4,260},{8,264},{12,268},{16,272},{20,276},{24,280},{28,28... | collective-permute-start | bytes 13832 | tf_op jit(solution)/shard_map/ppermute | solution.py:375
  25.1 3.1 %collective-permute-start.4 = (f32[16,144]{1,0:T(8,128)S(1)}, f32[16,144]{1,0:T(8,128)S(1)}, u32[]{:S(2)}, u32[]{:S(2)}) collective-permute-start(f32[16,144]{1,0:T(8,128)S(1)} %get-tuple-element.62), channel_id=1, source_target_pairs={{0,1},{1,0},{2,3},{3,2},{4,5},{5,4},{6,7},{7,6},{8,9},{9,8},{10,11... | collective-permute-start | bytes 27656 | tf_op jit(solution)/shard_map/ppermute | solution.py:381
  28.3 0.0 collective-permute-done.rest_0_
  28.3 0.7 %collective-permute-start.5 = (f32[16,144]{1,0:T(8,128)S(1)}, f32[16,144]{1,0:T(8,128)S(1)}, u32[]{:S(2)}, u32[]{:S(2)}) collective-permute-start(f32[16,144]{1,0:T(8,128)S(1)} %get-tuple-element.63), channel_id=1, source_target_pairs={{1,2},{2,1},{5,6},{6,5},{9,10},{10,9},{13,14},{14,13},{17,18},{18,... | collective-permute-start | bytes 27656 | tf_op jit(solution)/shard_map/ppermute | solution.py:381
  29.0 4.0 %collective-permute-start.6 = (f32[24,144]{1,0:T(8,128)S(1)}, f32[24,144]{1,0:T(8,128)S(1)}, u32[]{:S(2)}, u32[]{:S(2)}) collective-permute-start(f32[24,144]{1,0:T(8,128)S(1)} %get-tuple-element.64), channel_id=1, source_target_pairs={{0,4},{4,0},{8,12},{12,8},{16,20},{20,16},{24,28},{28,24},{32,36},... | collective-permute-start | bytes 41480 | tf_op jit(solution)/shard_map/ppermute | solution.py:375
  33.0 1.1 %shard_map.119 = (f32[9,40,128]{2,1,0:T(8,128)S(1)}, f32[64,1152]{1,0:T(8,128)S(1)}, bf16[32,4608]{1,0:T(8,128)(2,1)S(1)}, f32[162,4,128]{2,1,0:T(4,128)S(1)}, b...) custom-call(f32[9,35,128]{2,1,0:T(8,128)S(1)} %copy-done, ...), custom_call_target="tpu_custom_call" | custom-call | flops 200000000 | bytes 2000000 | tf_op jit(solution)/shard_map/pallas_call | solution.py:353
  34.1 0.0 collective-permute-done.2.rest_2_
  34.2 2.5 %shard_map.120 = (f32[9,40,128]{2,1,0:T(8,128)S(1)}, bf16[144,1152]{1,0:T(8,128)(2,1)S(1)}, f32[64,1152]{1,0:T(8,128)S(1)}, bf16[288,512]{1,0:T(8,128)(2,1)S(1)}...) custom-call(f32[9,40,128]{2,1,0:T(8,128)S(1)} %get-tuple-element.46., ...), custom_call_target="tpu_custom_call" | custom-call | flops 200000000 | bytes 2000000 | tf_op jit(solution)/shard_map/pallas_call | solution.py:353
  36.7 2.5 %collective-permute-start.7 = (f32[8,144]{1,0:T(8,128)S(1)}, f32[8,144]{1,0:T(8,128)S(1)}, u32[]{:S(2)}, u32[]{:S(2)}) collective-permute-start(f32[8,144]{1,0:T(8,128)S(1)} %get-tuple-element.74), channel_id=1, source_target_pairs={{0,508},{508,0},{8,4},{4,8},{16,12},{12,16},{24,20},{20,24},{32,28... | collective-permute-start | bytes 13832 | tf_op jit(solution)/shard_map/ppermute | solution.py:375
  39.3 4.8 %collective-permute-start.8 = (f32[8,144]{1,0:T(8,128)S(1)}, f32[8,144]{1,0:T(8,128)S(1)}, u32[]{:S(2)}, u32[]{:S(2)}) collective-permute-start(f32[8,144]{1,0:T(8,128)S(1)} %get-tuple-element.75), channel_id=1, source_target_pairs={{0,12},{12,0},{8,20},{20,8},{16,28},{28,16},{24,36},{36,24},{32,44... | collective-permute-start | bytes 13832 | tf_op jit(solution)/shard_map/ppermute | solution.py:375
  44.1 2.6 %collective-permute-start.9 = (f32[8,144]{1,0:T(8,128)S(1)}, f32[8,144]{1,0:T(8,128)S(1)}, u32[]{:S(2)}, u32[]{:S(2)}) collective-permute-start(f32[8,144]{1,0:T(8,128)S(1)} %get-tuple-element.76), channel_id=1, source_target_pairs={{0,500},{500,0},{8,508},{508,8},{16,4},{4,16},{24,12},{12,24},{32,... | collective-permute-start | bytes 13832 | tf_op jit(solution)/shard_map/ppermute | solution.py:375
  46.7 3.1 %collective-permute-start.10 = (f32[8,144]{1,0:T(8,128)S(1)}, f32[8,144]{1,0:T(8,128)S(1)}, u32[]{:S(2)}, u32[]{:S(2)}) collective-permute-start(f32[8,144]{1,0:T(8,128)S(1)} %get-tuple-element.77), channel_id=1, source_target_pairs={{0,256},{4,260},{8,264},{12,268},{16,272},{20,276},{24,280},{28,28... | collective-permute-start | bytes 13832 | tf_op jit(solution)/shard_map/ppermute | solution.py:375
  49.8 5.3 %collective-permute-start.11 = (f32[16,144]{1,0:T(8,128)S(1)}, f32[16,144]{1,0:T(8,128)S(1)}, u32[]{:S(2)}, u32[]{:S(2)}) collective-permute-start(f32[16,144]{1,0:T(8,128)S(1)} %get-tuple-element.78), channel_id=1, source_target_pairs={{0,1},{1,0},{2,3},{3,2},{4,5},{5,4},{6,7},{7,6},{8,9},{9,8},{10,11... | collective-permute-start | bytes 27656 | tf_op jit(solution)/shard_map/ppermute | solution.py:381
  55.1 0.7 %collective-permute-start.12 = (f32[16,144]{1,0:T(8,128)S(1)}, f32[16,144]{1,0:T(8,128)S(1)}, u32[]{:S(2)}, u32[]{:S(2)}) collective-permute-start(f32[16,144]{1,0:T(8,128)S(1)} %get-tuple-element.79), channel_id=1, source_target_pairs={{1,2},{2,1},{5,6},{6,5},{9,10},{10,9},{13,14},{14,13},{17,18},{18,... | collective-permute-start | bytes 27656 | tf_op jit(solution)/shard_map/ppermute | solution.py:381
  55.8 3.8 %collective-permute-start.13 = (f32[24,144]{1,0:T(8,128)S(1)}, f32[24,144]{1,0:T(8,128)S(1)}, u32[]{:S(2)}, u32[]{:S(2)}) collective-permute-start(f32[24,144]{1,0:T(8,128)S(1)} %get-tuple-element.80), channel_id=1, source_target_pairs={{0,4},{4,0},{8,12},{12,8},{16,20},{20,16},{24,28},{28,24},{32,36},... | collective-permute-start | bytes 41480 | tf_op jit(solution)/shard_map/ppermute | solution.py:375
  59.6 1.0 %shard_map.121 = (f32[9,40,128]{2,1,0:T(8,128)S(1)}, f32[64,1152]{1,0:T(8,128)S(1)}, bf16[32,4608]{1,0:T(8,128)(2,1)S(1)}) custom-call(f32[9,40,128]{2,1,0:T(8,128)S(1)} %get-tuple-element.65.middle, bf16[144,1152]{1,0:T(8,128)(2,1)S(1)} %get-tuple-element.66.x, f32[64,1152]{1,0:T(8,128)S(1)} %get-tuple-element.67.s, ...), custom_call_target="tpu_custom_call" | custom-call | flops 200000000 | bytes 2000000 | tf_op jit(solution)/shard_map/pallas_call | solution.py:353
  60.7 1.6 %shard_map.122 = f32[9,35,128]{2,1,0:T(8,128)} custom-call(f32[9,40,128]{2,1,0:T(8,128)S(1)} %get-tuple-element.71.held, f32[64,1152]{1,0:T(8,128)S(1)} %get-tuple-element.72.own, bf16[32,4608]{1,0:T(8,128)(2,1)S(1)} %get-tuple-element.73.near, bf16[80,512]{1,0:T(8,128)(2,1)S(1)} %get-tuple-element.50.hot, s32[24,128]{1,0:T(8,128)S(1)} %concatenate.3.marks, ...), custom_call_target="tpu_custom_call" | custom-call | flops 100000000 | bytes 2000000 | tf_op jit(solution)/shard_map/pallas_call | solution.py:353
  (35 shorter events, 0.1 us)
Async XLA Ops:
  0.0 1.1 %copy-start.9 = (s32[2,16]{1,0:T(2,128)S(1)}, s32[2,16]{1,0:T(2,128)}, u32[]{:S(2)}) copy-start(s32[2,16]{1,0:T(2,128)} %param.19) | copy-start | bytes 388
  0.0 1.2 %copy-start = (f32[9,35,128]{2,1,0:T(8,128)S(1)}, f32[9,35,128]{2,1,0:T(8,128)}, u32[]{:S(2)}) copy-start(f32[9,35,128]{2,1,0:T(8,128)} %state.3) | copy-start | bytes 483844
  0.0 1.1 %copy-start.6 = (s32[1,1024]{1,0:T(1,128)S(1)}, s32[1,1024]{1,0:T(1,128)}, u32[]{:S(2)}) copy-start(s32[1,1024]{1,0:T(1,128)} %param.18) | copy-start | bytes 12292
  0.0 1.1 %copy-start.7 = (s32[4,128]{1,0:T(4,128)S(1)}, s32[4,128]{1,0:T(4,128)}, u32[]{:S(2)}) copy-start(s32[4,128]{1,0:T(4,128)} %param.16) | copy-start | bytes 6148
  0.0 1.1 %copy-start.8 = (s32[4,128]{1,0:T(4,128)S(1)}, s32[4,128]{1,0:T(4,128)}, u32[]{:S(2)}) copy-start(s32[4,128]{1,0:T(4,128)} %param.17) | copy-start | bytes 6148
  0.0 1.1 %copy-start.10 = (s32[128]{0:T(128)S(1)}, s32[128]{0:T(128)}, u32[]{:S(2)}) copy-start(s32[128]{0:T(128)} %param.15) | copy-start | bytes 1540
  0.0 1.2 %copy-start.1 = (f32[3,35,35]{2,1,0:T(8,128)S(1)}, f32[3,35,35]{2,1,0:T(8,128)}, u32[]{:S(2)}) copy-start(f32[3,35,35]{2,1,0:T(8,128)} %stiffness.3) | copy-start | bytes 44104
  1.9 31.1 %copy-start.2 = (bf16[2,4,9,9,128]{4,1,3,2,0:T(4,128)(2,1)S(1)}, bf16[2,4,9,9,128]{4,1,3,2,0:T(4,128)(2,1)}, u32[]{:S(2)}) copy-start(bf16[2,4,9,9,128]{4,1,3,2,0:T(4,128)(2,1)} %param.14) | copy-start | bytes 497668
  1.9 31.1 %copy-start.4 = (f32[4,35,15]{1,0,2:T(4,128)S(1)}, f32[4,35,15]{1,0,2:T(4,128)}, u32[]{:S(2)}) copy-start(f32[4,35,15]{1,0,2:T(4,128)} %param.22) | copy-start | bytes 25204
  1.9 31.2 %copy-start.5 = (f32[3,15,15]{2,1,0:T(8,128)S(1)}, f32[3,15,15]{2,1,0:T(8,128)}, u32[]{:S(2)}) copy-start(f32[3,15,15]{2,1,0:T(8,128)} %rotations.1) | copy-start | bytes 8104
  3.6 24.7 %collective-permute-start = (f32[8,144]{1,0:T(8,128)S(1)}, f32[8,144]{1,0:T(8,128)S(1)}, u32[]{:S(2)}, u32[]{:S(2)}) collective-permute-start(f32[8,144]{1,0:T(8,128)S(1)} %get-tuple-element.58), channel_id=1, source_target_pairs={{0,508},{508,0},{8,4},{4,8},{16,12},{12,16},{24,20},{20,24},{32,28... | collective-permute-start | bytes 13832 | tf_op jit(solution)/shard_map/ppermute | solution.py:375
  8.6 20.4 %collective-permute-start.1 = (f32[8,144]{1,0:T(8,128)S(1)}, f32[8,144]{1,0:T(8,128)S(1)}, u32[]{:S(2)}, u32[]{:S(2)}) collective-permute-start(f32[8,144]{1,0:T(8,128)S(1)} %get-tuple-element.59), channel_id=1, source_target_pairs={{0,12},{12,0},{8,20},{20,8},{16,28},{28,16},{24,36},{36,24},{32,44... | collective-permute-start | bytes 13832 | tf_op jit(solution)/shard_map/ppermute | solution.py:375
  21.0 13.2 %collective-permute-start.2 = (f32[8,144]{1,0:T(8,128)S(1)}, f32[8,144]{1,0:T(8,128)S(1)}, u32[]{:S(2)}, u32[]{:S(2)}) collective-permute-start(f32[8,144]{1,0:T(8,128)S(1)} %get-tuple-element.60), channel_id=1, source_target_pairs={{0,500},{500,0},{8,508},{508,8},{16,4},{4,16},{24,12},{12,24},{32,... | collective-permute-start | bytes 13832 | tf_op jit(solution)/shard_map/ppermute | solution.py:375
  22.9 11.2 %collective-permute-start.3 = (f32[8,144]{1,0:T(8,128)S(1)}, f32[8,144]{1,0:T(8,128)S(1)}, u32[]{:S(2)}, u32[]{:S(2)}) collective-permute-start(f32[8,144]{1,0:T(8,128)S(1)} %get-tuple-element.61), channel_id=1, source_target_pairs={{0,256},{4,260},{8,264},{12,268},{16,272},{20,276},{24,280},{28,28... | collective-permute-start | bytes 13832 | tf_op jit(solution)/shard_map/ppermute | solution.py:375
  25.1 9.0 %collective-permute-start.4 = (f32[16,144]{1,0:T(8,128)S(1)}, f32[16,144]{1,0:T(8,128)S(1)}, u32[]{:S(2)}, u32[]{:S(2)}) collective-permute-start(f32[16,144]{1,0:T(8,128)S(1)} %get-tuple-element.62), channel_id=1, source_target_pairs={{0,1},{1,0},{2,3},{3,2},{4,5},{5,4},{6,7},{7,6},{8,9},{9,8},{10,11... | collective-permute-start | bytes 27656 | tf_op jit(solution)/shard_map/ppermute | solution.py:381
  28.3 5.9 %collective-permute-start.5 = (f32[16,144]{1,0:T(8,128)S(1)}, f32[16,144]{1,0:T(8,128)S(1)}, u32[]{:S(2)}, u32[]{:S(2)}) collective-permute-start(f32[16,144]{1,0:T(8,128)S(1)} %get-tuple-element.63), channel_id=1, source_target_pairs={{1,2},{2,1},{5,6},{6,5},{9,10},{10,9},{13,14},{14,13},{17,18},{18,... | collective-permute-start | bytes 27656 | tf_op jit(solution)/shard_map/ppermute | solution.py:381
  29.0 5.2 %collective-permute-start.6 = (f32[24,144]{1,0:T(8,128)S(1)}, f32[24,144]{1,0:T(8,128)S(1)}, u32[]{:S(2)}, u32[]{:S(2)}) collective-permute-start(f32[24,144]{1,0:T(8,128)S(1)} %get-tuple-element.64), channel_id=1, source_target_pairs={{0,4},{4,0},{8,12},{12,8},{16,20},{20,16},{24,28},{28,24},{32,36},... | collective-permute-start | bytes 41480 | tf_op jit(solution)/shard_map/ppermute | solution.py:375
  36.7 18.4 %collective-permute-start.7 = (f32[8,144]{1,0:T(8,128)S(1)}, f32[8,144]{1,0:T(8,128)S(1)}, u32[]{:S(2)}, u32[]{:S(2)}) collective-permute-start(f32[8,144]{1,0:T(8,128)S(1)} %get-tuple-element.74), channel_id=1, source_target_pairs={{0,508},{508,0},{8,4},{4,8},{16,12},{12,16},{24,20},{20,24},{32,28... | collective-permute-start | bytes 13832 | tf_op jit(solution)/shard_map/ppermute | solution.py:375
  39.3 16.5 %collective-permute-start.8 = (f32[8,144]{1,0:T(8,128)S(1)}, f32[8,144]{1,0:T(8,128)S(1)}, u32[]{:S(2)}, u32[]{:S(2)}) collective-permute-start(f32[8,144]{1,0:T(8,128)S(1)} %get-tuple-element.75), channel_id=1, source_target_pairs={{0,12},{12,0},{8,20},{20,8},{16,28},{28,16},{24,36},{36,24},{32,44... | collective-permute-start | bytes 13832 | tf_op jit(solution)/shard_map/ppermute | solution.py:375
  44.1 16.5 %collective-permute-start.9 = (f32[8,144]{1,0:T(8,128)S(1)}, f32[8,144]{1,0:T(8,128)S(1)}, u32[]{:S(2)}, u32[]{:S(2)}) collective-permute-start(f32[8,144]{1,0:T(8,128)S(1)} %get-tuple-element.76), channel_id=1, source_target_pairs={{0,500},{500,0},{8,508},{508,8},{16,4},{4,16},{24,12},{12,24},{32,... | collective-permute-start | bytes 13832 | tf_op jit(solution)/shard_map/ppermute | solution.py:375
  46.7 13.9 %collective-permute-start.10 = (f32[8,144]{1,0:T(8,128)S(1)}, f32[8,144]{1,0:T(8,128)S(1)}, u32[]{:S(2)}, u32[]{:S(2)}) collective-permute-start(f32[8,144]{1,0:T(8,128)S(1)} %get-tuple-element.77), channel_id=1, source_target_pairs={{0,256},{4,260},{8,264},{12,268},{16,272},{20,276},{24,280},{28,28... | collective-permute-start | bytes 13832 | tf_op jit(solution)/shard_map/ppermute | solution.py:375
  49.8 10.8 %collective-permute-start.11 = (f32[16,144]{1,0:T(8,128)S(1)}, f32[16,144]{1,0:T(8,128)S(1)}, u32[]{:S(2)}, u32[]{:S(2)}) collective-permute-start(f32[16,144]{1,0:T(8,128)S(1)} %get-tuple-element.78), channel_id=1, source_target_pairs={{0,1},{1,0},{2,3},{3,2},{4,5},{5,4},{6,7},{7,6},{8,9},{9,8},{10,11... | collective-permute-start | bytes 27656 | tf_op jit(solution)/shard_map/ppermute | solution.py:381
  55.1 5.5 %collective-permute-start.12 = (f32[16,144]{1,0:T(8,128)S(1)}, f32[16,144]{1,0:T(8,128)S(1)}, u32[]{:S(2)}, u32[]{:S(2)}) collective-permute-start(f32[16,144]{1,0:T(8,128)S(1)} %get-tuple-element.79), channel_id=1, source_target_pairs={{1,2},{2,1},{5,6},{6,5},{9,10},{10,9},{13,14},{14,13},{17,18},{18,... | collective-permute-start | bytes 27656 | tf_op jit(solution)/shard_map/ppermute | solution.py:381
  55.8 4.9 %collective-permute-start.13 = (f32[24,144]{1,0:T(8,128)S(1)}, f32[24,144]{1,0:T(8,128)S(1)}, u32[]{:S(2)}, u32[]{:S(2)}) collective-permute-start(f32[24,144]{1,0:T(8,128)S(1)} %get-tuple-element.80), channel_id=1, source_target_pairs={{0,4},{4,0},{8,12},{12,8},{16,20},{20,16},{24,28},{28,24},{32,36},... | collective-permute-start | bytes 41480 | tf_op jit(solution)/shard_map/ppermute | solution.py:375
  (1 other events, 0.8 us)

commit v4 on v3

--- a/solution.py
+++ b/solution.py
@@ -185,15 +185,11 @@
             l[Q * AP + q * AP : Q * AP + (q + 1) * AP, lanes(f)] = rest
 
 
-def first_kernel(state, stars, stiffness, trace_maps, marks,
-                 x_out, s_out, coarse, hot, l, step1, step2, step3, traces, *rest):
-    sends, (first, early, x, y) = rest[:7], rest[7:]
+def first_kernel(state, stars, stiffness, x_out, coarse, step1, step2, step3, first, early, x, y):
     steps = (step1, step2, step3, step3)
     blocks = stiff_rows(stiffness)
     for step, (rows, _) in zip(steps, STEPS):
         step[...] = jnp.concatenate([block[0:rows] for block in blocks], axis=0).astype(BF16)
-    traces[...] = trace_rows(trace_maps)
-    pick_shared(marks, hot)
     first[...] = jnp.zeros_like(first)
     first[:, 0:B, :] = state[...]
     early[...] = first[...] * EARLY[0]
@@ -207,7 +203,12 @@
     taylor(first, steps, stars, x, y, add)
     for p in range(Q):
         put_stack(x_out, p, early[p])
-    s_out[...] = dot(traces[...], x_out[...])
+
+
+def first_send_kernel(x, trace_maps, marks, s_out, l, hot, traces, *sends):
+    pick_shared(marks, hot)
+    traces[...] = trace_rows(trace_maps)
+    s_out[...] = dot(traces[...], x[...])
     send_traces(s_out, hot, l, sends)
 
 
@@ -408,17 +409,16 @@
     sends = [shape(dims) for dims in SENDS]
     split = shape((2 * Q * AP, ALL), BF16)
     products = [shape((3 * rows, 3 * PAD), BF16) for rows, _ in STEPS[:3]]
-    products.append(shape((4 * AP, 3 * PAD), BF16))
     own_outs = [kept[2], kept[1], shape((2 * AP, Q * ALL), BF16)]
-    x_early, s_early, coarse, hot, l_early, *rest = call(
-        first_kernel,
-        (state, stars, stiffness, trace_maps, marks),
-        kept + [shape((CP, ALL), BF16), split]
-        + products + sends,
-        [PADDED, PADDED, X, Y],
-        100_000_000,
-    )
-    steps, out_early = rest[:4], rest[4:]
+    x_early, coarse, *steps = call(
+        first_kernel, (state, stars, stiffness), [kept[0], kept[2]] + products,
+        [PADDED, PADDED, X, Y], 100_000_000,
+    )
+    s_early, l_early, hot, traces, *out_early = call(
+        first_send_kernel, (x_early, trace_maps, marks),
+        [kept[1], split, shape((CP, ALL), BF16), shape((4 * AP, 3 * PAD), BF16)] + sends,
+        [], 100_000_000,
+    )
     in_early = exchange(out_early)
     held, own, near, solvers, same, volumes, lifts, turns = call(
         early_own_kernel,
@@ -431,7 +431,7 @@
     )
     middle, x_late, s_late, l_late, *out_late = call(
         middle_kernel,
-        (held, own, near, coarse, hot, marks, stars, solvers, lifts, turns, *steps,
+        (held, own, near, coarse, hot, marks, stars, solvers, lifts, turns, *steps, traces,
          *in_early),
         [kept[2], kept[0], kept[1], split] + sends,
         [PADDED, PADDED, X, Y, SIDE, STACK], 200_000_000,

time: 62.8 us -> 62.9 us (level)
    pallas_call x5 -> x6, Pallas kernels: 7.91 us -> 8.02 us  [call(): pl.pallas_call(kernel, out_shape=outs, in_specs=[vmem] * len(operands), o...]
where the time goes in v4:
time: 62.9 us; the launch traced here: 62.3 us
  starting transfers between devices  52.2 us (83%)
  Pallas kernels  8.02 us (13%)
  other arithmetic  0.94 us (1%)
  local copies, waits for them, and re-layouts  0.77 us (1%)
    ppermute x10, starting transfers between devices, along_dom(): return lax.ppermute(block, 'dom', pairs)  42.4 us
    ppermute x4, starting transfers between devices, along_ply(): return lax.ppermute(block, 'ply', pairs)  9.72 us
    pallas_call x6, Pallas kernels, call(): pl.pallas_call(kernel, out_shape=outs, in_specs=[vmem] * len(operands), o...  8.02 us
  transfers between devices with their start and end apart: 14, of which 0 were waited for; matrix products, arithmetic and copies ran while one was open for 0% of the time, Pallas kernels for 3%

profile of v4, /device:TPU:1, one launch (start us, length us, event | category | flops | bytes accessed | tf_op | source)
XLA Modules:
  0.0 62.3 jit_solution(5493392650230194482)
XLA Ops:
  0.0 0.9 %convert_element_type.11 = f32[3,9,9,128]{3,0,2,1:T(4,128)S(1)} convert(bf16[3,9,9,128]{3,0,2,1:T(4,128)(2,1)} %param.13) | non-fusion elementwise | flops 31104 | bytes 186624 | tf_op jit(solution)/shard_map/convert_element_type | solution.py:393
  1.0 0.0 copy-done
  1.0 0.0 copy-start.8
  1.0 1.3 %shard_map.118 = (bf16[144,1152]{1,0:T(8,128)(2,1)S(1)}, f32[9,40,128]{2,1,0:T(8,128)S(1)}, bf16[72,144]{1,0:T(8,128)(2,1)S(1)}, bf16[48,144]{1,0:T(8,128)(2,1)S(1)}, bf16[24,144]{1,0:T(8,128)(2,1)S(1)}) custom-call(f32[9,35,128]{2,1,0:T(8,128)S(1)} %copy-done, f32[81,3,128]{2,1,0:T(4,128)S(1)} %bitcast.10, f32[3,35,35]{2,1,0:T(8,128)S(1)} %copy-done.1), custom_call_target="tpu_custom_call" | custom-call | flops 100000000 | bytes 2000000 | tf_op jit(solution)/shard_map/pallas_call | solution.py:354
  2.5 0.6 %copy-done.3 = f32[4,15,35]{2,0,1:T(4,128)S(1)} copy-done((f32[4,15,35]{2,0,1:T(4,128)S(1)}, f32[4,15,35]{2,0,1:T(4,128)}, u32[]{:S(2)}) %copy-start.3) | copy-done | bytes 8424
  3.1 0.5 shard_map.119
  3.7 4.9 %collective-permute-start = (f32[8,144]{1,0:T(8,128)S(1)}, f32[8,144]{1,0:T(8,128)S(1)}, u32[]{:S(2)}, u32[]{:S(2)}) collective-permute-start(f32[8,144]{1,0:T(8,128)S(1)} %get-tuple-element.58), channel_id=1, source_target_pairs={{0,508},{508,0},{8,4},{4,8},{16,12},{12,16},{24,20},{20,24},{32,28... | collective-permute-start | bytes 13832 | tf_op jit(solution)/shard_map/ppermute | solution.py:376
  8.6 12.4 %collective-permute-start.1 = (f32[8,144]{1,0:T(8,128)S(1)}, f32[8,144]{1,0:T(8,128)S(1)}, u32[]{:S(2)}, u32[]{:S(2)}) collective-permute-start(f32[8,144]{1,0:T(8,128)S(1)} %get-tuple-element.59), channel_id=1, source_target_pairs={{0,12},{12,0},{8,20},{20,8},{16,28},{28,16},{24,36},{36,24},{32,44... | collective-permute-start | bytes 13832 | tf_op jit(solution)/shard_map/ppermute | solution.py:376
  21.0 1.9 %collective-permute-start.2 = (f32[8,144]{1,0:T(8,128)S(1)}, f32[8,144]{1,0:T(8,128)S(1)}, u32[]{:S(2)}, u32[]{:S(2)}) collective-permute-start(f32[8,144]{1,0:T(8,128)S(1)} %get-tuple-element.60), channel_id=1, source_target_pairs={{0,500},{500,0},{8,508},{508,8},{16,4},{4,16},{24,12},{12,24},{32,... | collective-permute-start | bytes 13832 | tf_op jit(solution)/shard_map/ppermute | solution.py:376
  22.9 2.3 %collective-permute-start.3 = (f32[8,144]{1,0:T(8,128)S(1)}, f32[8,144]{1,0:T(8,128)S(1)}, u32[]{:S(2)}, u32[]{:S(2)}) collective-permute-start(f32[8,144]{1,0:T(8,128)S(1)} %get-tuple-element.61), channel_id=1, source_target_pairs={{0,256},{4,260},{8,264},{12,268},{16,272},{20,276},{24,280},{28,28... | collective-permute-start | bytes 13832 | tf_op jit(solution)/shard_map/ppermute | solution.py:376
  25.2 3.1 %collective-permute-start.4 = (f32[16,144]{1,0:T(8,128)S(1)}, f32[16,144]{1,0:T(8,128)S(1)}, u32[]{:S(2)}, u32[]{:S(2)}) collective-permute-start(f32[16,144]{1,0:T(8,128)S(1)} %get-tuple-element.62), channel_id=1, source_target_pairs={{0,1},{1,0},{2,3},{3,2},{4,5},{5,4},{6,7},{7,6},{8,9},{9,8},{10,11... | collective-permute-start | bytes 27656 | tf_op jit(solution)/shard_map/ppermute | solution.py:382
  28.4 0.7 %collective-permute-start.5 = (f32[16,144]{1,0:T(8,128)S(1)}, f32[16,144]{1,0:T(8,128)S(1)}, u32[]{:S(2)}, u32[]{:S(2)}) collective-permute-start(f32[16,144]{1,0:T(8,128)S(1)} %get-tuple-element.63), channel_id=1, source_target_pairs={{1,2},{2,1},{5,6},{6,5},{9,10},{10,9},{13,14},{14,13},{17,18},{18,... | collective-permute-start | bytes 27656 | tf_op jit(solution)/shard_map/ppermute | solution.py:382
  29.0 4.0 %collective-permute-start.6 = (f32[24,144]{1,0:T(8,128)S(1)}, f32[24,144]{1,0:T(8,128)S(1)}, u32[]{:S(2)}, u32[]{:S(2)}) collective-permute-start(f32[24,144]{1,0:T(8,128)S(1)} %get-tuple-element.64), channel_id=1, source_target_pairs={{0,4},{4,0},{8,12},{12,8},{16,20},{20,16},{24,28},{28,24},{32,36},... | collective-permute-start | bytes 41480 | tf_op jit(solution)/shard_map/ppermute | solution.py:376
  33.1 1.1 %shard_map.120 = (f32[9,40,128]{2,1,0:T(8,128)S(1)}, f32[64,1152]{1,0:T(8,128)S(1)}, bf16[32,4608]{1,0:T(8,128)(2,1)S(1)}, f32[162,4,128]{2,1,0:T(4,128)S(1)}, b...) custom-call(f32[9,35,128]{2,1,0:T(8,128)S(1)} %copy-done, ...), custom_call_target="tpu_custom_call" | custom-call | flops 200000000 | bytes 2000000 | tf_op jit(solution)/shard_map/pallas_call | solution.py:354
  34.2 2.5 %shard_map.121 = (f32[9,40,128]{2,1,0:T(8,128)S(1)}, bf16[144,1152]{1,0:T(8,128)(2,1)S(1)}, f32[64,1152]{1,0:T(8,128)S(1)}, bf16[288,512]{1,0:T(8,128)(2,1)S(1)}...) custom-call(f32[9,40,128]{2,1,0:T(8,128)S(1)} %get-tuple-element.46., ...), custom_call_target="tpu_custom_call" | custom-call | flops 200000000 | bytes 2000000 | tf_op jit(solution)/shard_map/pallas_call | solution.py:354
  36.8 2.5 %collective-permute-start.7 = (f32[8,144]{1,0:T(8,128)S(1)}, f32[8,144]{1,0:T(8,128)S(1)}, u32[]{:S(2)}, u32[]{:S(2)}) collective-permute-start(f32[8,144]{1,0:T(8,128)S(1)} %get-tuple-element.74), channel_id=1, source_target_pairs={{0,508},{508,0},{8,4},{4,8},{16,12},{12,16},{24,20},{20,24},{32,28... | collective-permute-start | bytes 13832 | tf_op jit(solution)/shard_map/ppermute | solution.py:376
  39.3 4.8 %collective-permute-start.8 = (f32[8,144]{1,0:T(8,128)S(1)}, f32[8,144]{1,0:T(8,128)S(1)}, u32[]{:S(2)}, u32[]{:S(2)}) collective-permute-start(f32[8,144]{1,0:T(8,128)S(1)} %get-tuple-element.75), channel_id=1, source_target_pairs={{0,12},{12,0},{8,20},{20,8},{16,28},{28,16},{24,36},{36,24},{32,44... | collective-permute-start | bytes 13832 | tf_op jit(solution)/shard_map/ppermute | solution.py:376
  44.2 2.6 %collective-permute-start.9 = (f32[8,144]{1,0:T(8,128)S(1)}, f32[8,144]{1,0:T(8,128)S(1)}, u32[]{:S(2)}, u32[]{:S(2)}) collective-permute-start(f32[8,144]{1,0:T(8,128)S(1)} %get-tuple-element.76), channel_id=1, source_target_pairs={{0,500},{500,0},{8,508},{508,8},{16,4},{4,16},{24,12},{12,24},{32,... | collective-permute-start | bytes 13832 | tf_op jit(solution)/shard_map/ppermute | solution.py:376
  46.8 3.1 %collective-permute-start.10 = (f32[8,144]{1,0:T(8,128)S(1)}, f32[8,144]{1,0:T(8,128)S(1)}, u32[]{:S(2)}, u32[]{:S(2)}) collective-permute-start(f32[8,144]{1,0:T(8,128)S(1)} %get-tuple-element.77), channel_id=1, source_target_pairs={{0,256},{4,260},{8,264},{12,268},{16,272},{20,276},{24,280},{28,28... | collective-permute-start | bytes 13832 | tf_op jit(solution)/shard_map/ppermute | solution.py:376
  49.9 5.3 %collective-permute-start.11 = (f32[16,144]{1,0:T(8,128)S(1)}, f32[16,144]{1,0:T(8,128)S(1)}, u32[]{:S(2)}, u32[]{:S(2)}) collective-permute-start(f32[16,144]{1,0:T(8,128)S(1)} %get-tuple-element.78), channel_id=1, source_target_pairs={{0,1},{1,0},{2,3},{3,2},{4,5},{5,4},{6,7},{7,6},{8,9},{9,8},{10,11... | collective-permute-start | bytes 27656 | tf_op jit(solution)/shard_map/ppermute | solution.py:382
  55.2 0.7 %collective-permute-start.12 = (f32[16,144]{1,0:T(8,128)S(1)}, f32[16,144]{1,0:T(8,128)S(1)}, u32[]{:S(2)}, u32[]{:S(2)}) collective-permute-start(f32[16,144]{1,0:T(8,128)S(1)} %get-tuple-element.79), channel_id=1, source_target_pairs={{1,2},{2,1},{5,6},{6,5},{9,10},{10,9},{13,14},{14,13},{17,18},{18,... | collective-permute-start | bytes 27656 | tf_op jit(solution)/shard_map/ppermute | solution.py:382
  55.9 3.8 %collective-permute-start.13 = (f32[24,144]{1,0:T(8,128)S(1)}, f32[24,144]{1,0:T(8,128)S(1)}, u32[]{:S(2)}, u32[]{:S(2)}) collective-permute-start(f32[24,144]{1,0:T(8,128)S(1)} %get-tuple-element.80), channel_id=1, source_target_pairs={{0,4},{4,0},{8,12},{12,8},{16,20},{20,16},{24,28},{28,24},{32,36},... | collective-permute-start | bytes 41480 | tf_op jit(solution)/shard_map/ppermute | solution.py:376
  59.7 1.0 %shard_map.122 = (f32[9,40,128]{2,1,0:T(8,128)S(1)}, f32[64,1152]{1,0:T(8,128)S(1)}, bf16[32,4608]{1,0:T(8,128)(2,1)S(1)}) custom-call(f32[9,40,128]{2,1,0:T(8,128)S(1)} %get-tuple-element.65.middle, bf16[144,1152]{1,0:T(8,128)(2,1)S(1)} %get-tuple-element.66.x, f32[64,1152]{1,0:T(8,128)S(1)} %get-tuple-element.67.s, ...), custom_call_target="tpu_custom_call" | custom-call | flops 200000000 | bytes 2000000 | tf_op jit(solution)/shard_map/pallas_call | solution.py:354
  60.7 1.6 %shard_map.123 = f32[9,35,128]{2,1,0:T(8,128)} custom-call(f32[9,40,128]{2,1,0:T(8,128)S(1)} %get-tuple-element.71.held, f32[64,1152]{1,0:T(8,128)S(1)} %get-tuple-element.72.own, bf16[32,4608]{1,0:T(8,128)(2,1)S(1)} %get-tuple-element.73.near, bf16[80,512]{1,0:T(8,128)(2,1)S(1)} %get-tuple-element.50.hot, s32[24,128]{1,0:T(8,128)S(1)} %concatenate.3.marks, ...), custom_call_target="tpu_custom_call" | custom-call | flops 100000000 | bytes 2000000 | tf_op jit(solution)/shard_map/pallas_call | solution.py:354
  (36 shorter events, 0.1 us)
Async XLA Ops:
  0.0 1.0 %copy-start.9 = (s32[2,16]{1,0:T(2,128)S(1)}, s32[2,16]{1,0:T(2,128)}, u32[]{:S(2)}) copy-start(s32[2,16]{1,0:T(2,128)} %param.19) | copy-start | bytes 388
  0.0 1.0 %copy-start.1 = (f32[3,35,35]{2,1,0:T(8,128)S(1)}, f32[3,35,35]{2,1,0:T(8,128)}, u32[]{:S(2)}) copy-start(f32[3,35,35]{2,1,0:T(8,128)} %stiffness.3) | copy-start | bytes 44104
  0.0 1.0 %copy-start = (f32[9,35,128]{2,1,0:T(8,128)S(1)}, f32[9,35,128]{2,1,0:T(8,128)}, u32[]{:S(2)}) copy-start(f32[9,35,128]{2,1,0:T(8,128)} %state.3) | copy-start | bytes 483844
  1.0 1.4 %copy-start.6 = (s32[1,1024]{1,0:T(1,128)S(1)}, s32[1,1024]{1,0:T(1,128)}, u32[]{:S(2)}) copy-start(s32[1,1024]{1,0:T(1,128)} %param.18) | copy-start | bytes 12292
  1.0 1.4 %copy-start.7 = (s32[4,128]{1,0:T(4,128)S(1)}, s32[4,128]{1,0:T(4,128)}, u32[]{:S(2)}) copy-start(s32[4,128]{1,0:T(4,128)} %param.16) | copy-start | bytes 6148
  1.0 1.4 %copy-start.8 = (s32[4,128]{1,0:T(4,128)S(1)}, s32[4,128]{1,0:T(4,128)}, u32[]{:S(2)}) copy-start(s32[4,128]{1,0:T(4,128)} %param.17) | copy-start | bytes 6148
  1.0 1.4 %copy-start.10 = (s32[128]{0:T(128)S(1)}, s32[128]{0:T(128)}, u32[]{:S(2)}) copy-start(s32[128]{0:T(128)} %param.15) | copy-start | bytes 1540
  3.1 29.9 %copy-start.2 = (bf16[2,4,9,9,128]{4,1,3,2,0:T(4,128)(2,1)S(1)}, bf16[2,4,9,9,128]{4,1,3,2,0:T(4,128)(2,1)}, u32[]{:S(2)}) copy-start(bf16[2,4,9,9,128]{4,1,3,2,0:T(4,128)(2,1)} %param.14) | copy-start | bytes 497668
  3.1 29.9 %copy-start.4 = (f32[4,35,15]{1,0,2:T(4,128)S(1)}, f32[4,35,15]{1,0,2:T(4,128)}, u32[]{:S(2)}) copy-start(f32[4,35,15]{1,0,2:T(4,128)} %param.22) | copy-start | bytes 25204
  3.1 29.9 %copy-start.5 = (f32[3,15,15]{2,1,0:T(8,128)S(1)}, f32[3,15,15]{2,1,0:T(8,128)}, u32[]{:S(2)}) copy-start(f32[3,15,15]{2,1,0:T(8,128)} %rotations.1) | copy-start | bytes 8104
  3.7 24.7 %collective-permute-start = (f32[8,144]{1,0:T(8,128)S(1)}, f32[8,144]{1,0:T(8,128)S(1)}, u32[]{:S(2)}, u32[]{:S(2)}) collective-permute-start(f32[8,144]{1,0:T(8,128)S(1)} %get-tuple-element.58), channel_id=1, source_target_pairs={{0,508},{508,0},{8,4},{4,8},{16,12},{12,16},{24,20},{20,24},{32,28... | collective-permute-start | bytes 13832 | tf_op jit(solution)/shard_map/ppermute | solution.py:376
  8.6 20.4 %collective-permute-start.1 = (f32[8,144]{1,0:T(8,128)S(1)}, f32[8,144]{1,0:T(8,128)S(1)}, u32[]{:S(2)}, u32[]{:S(2)}) collective-permute-start(f32[8,144]{1,0:T(8,128)S(1)} %get-tuple-element.59), channel_id=1, source_target_pairs={{0,12},{12,0},{8,20},{20,8},{16,28},{28,16},{24,36},{36,24},{32,44... | collective-permute-start | bytes 13832 | tf_op jit(solution)/shard_map/ppermute | solution.py:376
  21.0 13.2 %collective-permute-start.2 = (f32[8,144]{1,0:T(8,128)S(1)}, f32[8,144]{1,0:T(8,128)S(1)}, u32[]{:S(2)}, u32[]{:S(2)}) collective-permute-start(f32[8,144]{1,0:T(8,128)S(1)} %get-tuple-element.60), channel_id=1, source_target_pairs={{0,500},{500,0},{8,508},{508,8},{16,4},{4,16},{24,12},{12,24},{32,... | collective-permute-start | bytes 13832 | tf_op jit(solution)/shard_map/ppermute | solution.py:376
  22.9 11.3 %collective-permute-start.3 = (f32[8,144]{1,0:T(8,128)S(1)}, f32[8,144]{1,0:T(8,128)S(1)}, u32[]{:S(2)}, u32[]{:S(2)}) collective-permute-start(f32[8,144]{1,0:T(8,128)S(1)} %get-tuple-element.61), channel_id=1, source_target_pairs={{0,256},{4,260},{8,264},{12,268},{16,272},{20,276},{24,280},{28,28... | collective-permute-start | bytes 13832 | tf_op jit(solution)/shard_map/ppermute | solution.py:376
  25.2 9.0 %collective-permute-start.4 = (f32[16,144]{1,0:T(8,128)S(1)}, f32[16,144]{1,0:T(8,128)S(1)}, u32[]{:S(2)}, u32[]{:S(2)}) collective-permute-start(f32[16,144]{1,0:T(8,128)S(1)} %get-tuple-element.62), channel_id=1, source_target_pairs={{0,1},{1,0},{2,3},{3,2},{4,5},{5,4},{6,7},{7,6},{8,9},{9,8},{10,11... | collective-permute-start | bytes 27656 | tf_op jit(solution)/shard_map/ppermute | solution.py:382
  28.4 5.9 %collective-permute-start.5 = (f32[16,144]{1,0:T(8,128)S(1)}, f32[16,144]{1,0:T(8,128)S(1)}, u32[]{:S(2)}, u32[]{:S(2)}) collective-permute-start(f32[16,144]{1,0:T(8,128)S(1)} %get-tuple-element.63), channel_id=1, source_target_pairs={{1,2},{2,1},{5,6},{6,5},{9,10},{10,9},{13,14},{14,13},{17,18},{18,... | collective-permute-start | bytes 27656 | tf_op jit(solution)/shard_map/ppermute | solution.py:382
  29.0 5.2 %collective-permute-start.6 = (f32[24,144]{1,0:T(8,128)S(1)}, f32[24,144]{1,0:T(8,128)S(1)}, u32[]{:S(2)}, u32[]{:S(2)}) collective-permute-start(f32[24,144]{1,0:T(8,128)S(1)} %get-tuple-element.64), channel_id=1, source_target_pairs={{0,4},{4,0},{8,12},{12,8},{16,20},{20,16},{24,28},{28,24},{32,36},... | collective-permute-start | bytes 41480 | tf_op jit(solution)/shard_map/ppermute | solution.py:376
  36.8 18.4 %collective-permute-start.7 = (f32[8,144]{1,0:T(8,128)S(1)}, f32[8,144]{1,0:T(8,128)S(1)}, u32[]{:S(2)}, u32[]{:S(2)}) collective-permute-start(f32[8,144]{1,0:T(8,128)S(1)} %get-tuple-element.74), channel_id=1, source_target_pairs={{0,508},{508,0},{8,4},{4,8},{16,12},{12,16},{24,20},{20,24},{32,28... | collective-permute-start | bytes 13832 | tf_op jit(solution)/shard_map/ppermute | solution.py:376
  39.3 16.5 %collective-permute-start.8 = (f32[8,144]{1,0:T(8,128)S(1)}, f32[8,144]{1,0:T(8,128)S(1)}, u32[]{:S(2)}, u32[]{:S(2)}) collective-permute-start(f32[8,144]{1,0:T(8,128)S(1)} %get-tuple-element.75), channel_id=1, source_target_pairs={{0,12},{12,0},{8,20},{20,8},{16,28},{28,16},{24,36},{36,24},{32,44... | collective-permute-start | bytes 13832 | tf_op jit(solution)/shard_map/ppermute | solution.py:376
  44.2 16.5 %collective-permute-start.9 = (f32[8,144]{1,0:T(8,128)S(1)}, f32[8,144]{1,0:T(8,128)S(1)}, u32[]{:S(2)}, u32[]{:S(2)}) collective-permute-start(f32[8,144]{1,0:T(8,128)S(1)} %get-tuple-element.76), channel_id=1, source_target_pairs={{0,500},{500,0},{8,508},{508,8},{16,4},{4,16},{24,12},{12,24},{32,... | collective-permute-start | bytes 13832 | tf_op jit(solution)/shard_map/ppermute | solution.py:376
  46.8 13.9 %collective-permute-start.10 = (f32[8,144]{1,0:T(8,128)S(1)}, f32[8,144]{1,0:T(8,128)S(1)}, u32[]{:S(2)}, u32[]{:S(2)}) collective-permute-start(f32[8,144]{1,0:T(8,128)S(1)} %get-tuple-element.77), channel_id=1, source_target_pairs={{0,256},{4,260},{8,264},{12,268},{16,272},{20,276},{24,280},{28,28... | collective-permute-start | bytes 13832 | tf_op jit(solution)/shard_map/ppermute | solution.py:376
  49.9 10.8 %collective-permute-start.11 = (f32[16,144]{1,0:T(8,128)S(1)}, f32[16,144]{1,0:T(8,128)S(1)}, u32[]{:S(2)}, u32[]{:S(2)}) collective-permute-start(f32[16,144]{1,0:T(8,128)S(1)} %get-tuple-element.78), channel_id=1, source_target_pairs={{0,1},{1,0},{2,3},{3,2},{4,5},{5,4},{6,7},{7,6},{8,9},{9,8},{10,11... | collective-permute-start | bytes 27656 | tf_op jit(solution)/shard_map/ppermute | solution.py:382
  55.2 5.5 %collective-permute-start.12 = (f32[16,144]{1,0:T(8,128)S(1)}, f32[16,144]{1,0:T(8,128)S(1)}, u32[]{:S(2)}, u32[]{:S(2)}) collective-permute-start(f32[16,144]{1,0:T(8,128)S(1)} %get-tuple-element.79), channel_id=1, source_target_pairs={{1,2},{2,1},{5,6},{6,5},{9,10},{10,9},{13,14},{14,13},{17,18},{18,... | collective-permute-start | bytes 27656 | tf_op jit(solution)/shard_map/ppermute | solution.py:382
  55.9 4.9 %collective-permute-start.13 = (f32[24,144]{1,0:T(8,128)S(1)}, f32[24,144]{1,0:T(8,128)S(1)}, u32[]{:S(2)}, u32[]{:S(2)}) collective-permute-start(f32[24,144]{1,0:T(8,128)S(1)} %get-tuple-element.80), channel_id=1, source_target_pairs={{0,4},{4,0},{8,12},{12,8},{16,20},{20,16},{24,28},{28,24},{32,36},... | collective-permute-start | bytes 41480 | tf_op jit(solution)/shard_map/ppermute | solution.py:376
  (1 other events, 0.8 us)

commit v5 on v3

--- a/solution.py
+++ b/solution.py
@@ -95,7 +95,7 @@
         return tuple(total)
 
     start = tuple(jnp.zeros((rows, E), F32) for _ in range(Q))
-    return lax.fori_loop(0, Q, one, start, unroll=Q if rows < 40 else 3)
+    return lax.fori_loop(0, Q, one, start, unroll=Q)
 
 
 def taylor(first, steps, stars, x, y, add):
@@ -160,15 +160,10 @@
 
 def send_traces(s, hot, l, outs):
     split_traces(s, l)
-    total = None
-    for part in (1, 0):
-        piece = lax.dot_general(
-            hot[...],
-            l[part * Q * AP : (part + 1) * Q * AP, :],
-            (((1,), (1,)), ((), ())),
-            preferred_element_type=F32,
-        )
-        total = piece if total is None else total + piece
+    parts = lax.dot_general(
+        l[...], hot[...], (((1,), (1,)), ((), ())), preferred_element_type=F32
+    )
+    total = (parts[0 : Q * AP] + parts[Q * AP : 2 * Q * AP]).T
     at = 0
     for out in outs[:-1]:
         out[...] = total[at : at + out.shape[0]]

time: 62.8 us -> 62.7 us (level)
  no operation moved by 1% of the time
where the time goes in v5:
time: 62.7 us; the launch traced here: 62.2 us
  starting transfers between devices  52.1 us (83%)
  Pallas kernels  7.89 us (13%)
  other arithmetic  1.04 us (2%)
  local copies, waits for them, and re-layouts  0.73 us (1%)
    ppermute x10, starting transfers between devices, along_dom(): return lax.ppermute(block, 'dom', pairs)  42.4 us
    ppermute x4, starting transfers between devices, along_ply(): return lax.ppermute(block, 'ply', pairs)  9.73 us
    pallas_call x5, Pallas kernels, call(): pl.pallas_call(kernel, out_shape=outs, in_specs=[vmem] * len(operands), o...  7.89 us
  transfers between devices with their start and end apart: 14, of which 0 were waited for; matrix products, arithmetic and copies ran while one was open for 0% of the time, Pallas kernels for 3%

profile of v5, /device:TPU:1, one launch (start us, length us, event | category | flops | bytes accessed | tf_op | source)
XLA Modules:
  0.0 62.2 jit_solution(13224664553372411671)
XLA Ops:
  0.0 1.0 %convert_element_type.11 = f32[3,9,9,128]{3,0,2,1:T(4,128)S(1)} convert(bf16[3,9,9,128]{3,0,2,1:T(4,128)(2,1)} %param.13) | non-fusion elementwise | flops 31104 | bytes 186624 | tf_op jit(solution)/shard_map/convert_element_type | solution.py:387
  1.1 0.0 copy-start.3
  1.2 0.6 %copy-done.3 = f32[4,15,35]{2,0,1:T(4,128)S(1)} copy-done((f32[4,15,35]{2,0,1:T(4,128)S(1)}, f32[4,15,35]{2,0,1:T(4,128)}, u32[]{:S(2)}) %copy-start.3) | copy-done | bytes 8424
  1.9 1.8 %shard_map.118 = (bf16[144,1152]{1,0:T(8,128)(2,1)S(1)}, f32[64,1152]{1,0:T(8,128)S(1)}, f32[9,40,128]{2,1,0:T(8,128)S(1)}, bf16[80,512]{1,0:T(8,128)(2,1)S(1)},...) custom-call(f32[9,35,128]{2,1,0:T(8,128)S(1)} %copy-done, ...), custom_call_target="tpu_custom_call" | custom-call | flops 100000000 | bytes 2000000 | tf_op jit(solution)/shard_map/pallas_call | solution.py:348
  3.7 4.9 %collective-permute-start = (f32[8,144]{1,0:T(8,128)S(1)}, f32[8,144]{1,0:T(8,128)S(1)}, u32[]{:S(2)}, u32[]{:S(2)}) collective-permute-start(f32[8,144]{1,0:T(8,128)S(1)} %get-tuple-element.58), channel_id=1, source_target_pairs={{0,508},{508,0},{8,4},{4,8},{16,12},{12,16},{24,20},{20,24},{32,28... | collective-permute-start | bytes 13832 | tf_op jit(solution)/shard_map/ppermute | solution.py:370
  8.6 12.4 %collective-permute-start.1 = (f32[8,144]{1,0:T(8,128)S(1)}, f32[8,144]{1,0:T(8,128)S(1)}, u32[]{:S(2)}, u32[]{:S(2)}) collective-permute-start(f32[8,144]{1,0:T(8,128)S(1)} %get-tuple-element.59), channel_id=1, source_target_pairs={{0,12},{12,0},{8,20},{20,8},{16,28},{28,16},{24,36},{36,24},{32,44... | collective-permute-start | bytes 13832 | tf_op jit(solution)/shard_map/ppermute | solution.py:370
  21.0 1.9 %collective-permute-start.2 = (f32[8,144]{1,0:T(8,128)S(1)}, f32[8,144]{1,0:T(8,128)S(1)}, u32[]{:S(2)}, u32[]{:S(2)}) collective-permute-start(f32[8,144]{1,0:T(8,128)S(1)} %get-tuple-element.60), channel_id=1, source_target_pairs={{0,500},{500,0},{8,508},{508,8},{16,4},{4,16},{24,12},{12,24},{32,... | collective-permute-start | bytes 13832 | tf_op jit(solution)/shard_map/ppermute | solution.py:370
  22.9 2.3 %collective-permute-start.3 = (f32[8,144]{1,0:T(8,128)S(1)}, f32[8,144]{1,0:T(8,128)S(1)}, u32[]{:S(2)}, u32[]{:S(2)}) collective-permute-start(f32[8,144]{1,0:T(8,128)S(1)} %get-tuple-element.61), channel_id=1, source_target_pairs={{0,256},{4,260},{8,264},{12,268},{16,272},{20,276},{24,280},{28,28... | collective-permute-start | bytes 13832 | tf_op jit(solution)/shard_map/ppermute | solution.py:370
  25.2 3.1 %collective-permute-start.4 = (f32[16,144]{1,0:T(8,128)S(1)}, f32[16,144]{1,0:T(8,128)S(1)}, u32[]{:S(2)}, u32[]{:S(2)}) collective-permute-start(f32[16,144]{1,0:T(8,128)S(1)} %get-tuple-element.62), channel_id=1, source_target_pairs={{0,1},{1,0},{2,3},{3,2},{4,5},{5,4},{6,7},{7,6},{8,9},{9,8},{10,11... | collective-permute-start | bytes 27656 | tf_op jit(solution)/shard_map/ppermute | solution.py:376
  28.3 0.0 collective-permute-done.rest_0_
  28.3 0.7 %collective-permute-start.5 = (f32[16,144]{1,0:T(8,128)S(1)}, f32[16,144]{1,0:T(8,128)S(1)}, u32[]{:S(2)}, u32[]{:S(2)}) collective-permute-start(f32[16,144]{1,0:T(8,128)S(1)} %get-tuple-element.63), channel_id=1, source_target_pairs={{1,2},{2,1},{5,6},{6,5},{9,10},{10,9},{13,14},{14,13},{17,18},{18,... | collective-permute-start | bytes 27656 | tf_op jit(solution)/shard_map/ppermute | solution.py:376
  29.0 4.0 %collective-permute-start.6 = (f32[24,144]{1,0:T(8,128)S(1)}, f32[24,144]{1,0:T(8,128)S(1)}, u32[]{:S(2)}, u32[]{:S(2)}) collective-permute-start(f32[24,144]{1,0:T(8,128)S(1)} %get-tuple-element.64), channel_id=1, source_target_pairs={{0,4},{4,0},{8,12},{12,8},{16,20},{20,16},{24,28},{28,24},{32,36},... | collective-permute-start | bytes 41480 | tf_op jit(solution)/shard_map/ppermute | solution.py:370
  33.1 1.1 %shard_map.119 = (f32[9,40,128]{2,1,0:T(8,128)S(1)}, f32[64,1152]{1,0:T(8,128)S(1)}, bf16[32,4608]{1,0:T(8,128)(2,1)S(1)}, f32[162,4,128]{2,1,0:T(4,128)S(1)}, b...) custom-call(f32[9,35,128]{2,1,0:T(8,128)S(1)} %copy-done, ...), custom_call_target="tpu_custom_call" | custom-call | flops 200000000 | bytes 2000000 | tf_op jit(solution)/shard_map/pallas_call | solution.py:348
  34.1 0.0 collective-permute-done.3.rest_3_
  34.2 2.5 %shard_map.120 = (f32[9,40,128]{2,1,0:T(8,128)S(1)}, bf16[144,1152]{1,0:T(8,128)(2,1)S(1)}, f32[64,1152]{1,0:T(8,128)S(1)}, bf16[288,512]{1,0:T(8,128)(2,1)S(1)}...) custom-call(f32[9,40,128]{2,1,0:T(8,128)S(1)} %get-tuple-element.46., ...), custom_call_target="tpu_custom_call" | custom-call | flops 200000000 | bytes 2000000 | tf_op jit(solution)/shard_map/pallas_call | solution.py:348
  36.7 2.5 %collective-permute-start.7 = (f32[8,144]{1,0:T(8,128)S(1)}, f32[8,144]{1,0:T(8,128)S(1)}, u32[]{:S(2)}, u32[]{:S(2)}) collective-permute-start(f32[8,144]{1,0:T(8,128)S(1)} %get-tuple-element.74), channel_id=1, source_target_pairs={{0,508},{508,0},{8,4},{4,8},{16,12},{12,16},{24,20},{20,24},{32,28... | collective-permute-start | bytes 13832 | tf_op jit(solution)/shard_map/ppermute | solution.py:370
  39.3 4.8 %collective-permute-start.8 = (f32[8,144]{1,0:T(8,128)S(1)}, f32[8,144]{1,0:T(8,128)S(1)}, u32[]{:S(2)}, u32[]{:S(2)}) collective-permute-start(f32[8,144]{1,0:T(8,128)S(1)} %get-tuple-element.75), channel_id=1, source_target_pairs={{0,12},{12,0},{8,20},{20,8},{16,28},{28,16},{24,36},{36,24},{32,44... | collective-permute-start | bytes 13832 | tf_op jit(solution)/shard_map/ppermute | solution.py:370
  44.1 2.6 %collective-permute-start.9 = (f32[8,144]{1,0:T(8,128)S(1)}, f32[8,144]{1,0:T(8,128)S(1)}, u32[]{:S(2)}, u32[]{:S(2)}) collective-permute-start(f32[8,144]{1,0:T(8,128)S(1)} %get-tuple-element.76), channel_id=1, source_target_pairs={{0,500},{500,0},{8,508},{508,8},{16,4},{4,16},{24,12},{12,24},{32,... | collective-permute-start | bytes 13832 | tf_op jit(solution)/shard_map/ppermute | solution.py:370
  46.7 3.1 %collective-permute-start.10 = (f32[8,144]{1,0:T(8,128)S(1)}, f32[8,144]{1,0:T(8,128)S(1)}, u32[]{:S(2)}, u32[]{:S(2)}) collective-permute-start(f32[8,144]{1,0:T(8,128)S(1)} %get-tuple-element.77), channel_id=1, source_target_pairs={{0,256},{4,260},{8,264},{12,268},{16,272},{20,276},{24,280},{28,28... | collective-permute-start | bytes 13832 | tf_op jit(solution)/shard_map/ppermute | solution.py:370
  49.8 5.3 %collective-permute-start.11 = (f32[16,144]{1,0:T(8,128)S(1)}, f32[16,144]{1,0:T(8,128)S(1)}, u32[]{:S(2)}, u32[]{:S(2)}) collective-permute-start(f32[16,144]{1,0:T(8,128)S(1)} %get-tuple-element.78), channel_id=1, source_target_pairs={{0,1},{1,0},{2,3},{3,2},{4,5},{5,4},{6,7},{7,6},{8,9},{9,8},{10,11... | collective-permute-start | bytes 27656 | tf_op jit(solution)/shard_map/ppermute | solution.py:376
  55.1 0.7 %collective-permute-start.12 = (f32[16,144]{1,0:T(8,128)S(1)}, f32[16,144]{1,0:T(8,128)S(1)}, u32[]{:S(2)}, u32[]{:S(2)}) collective-permute-start(f32[16,144]{1,0:T(8,128)S(1)} %get-tuple-element.79), channel_id=1, source_target_pairs={{1,2},{2,1},{5,6},{6,5},{9,10},{10,9},{13,14},{14,13},{17,18},{18,... | collective-permute-start | bytes 27656 | tf_op jit(solution)/shard_map/ppermute | solution.py:376
  55.8 3.8 %collective-permute-start.13 = (f32[24,144]{1,0:T(8,128)S(1)}, f32[24,144]{1,0:T(8,128)S(1)}, u32[]{:S(2)}, u32[]{:S(2)}) collective-permute-start(f32[24,144]{1,0:T(8,128)S(1)} %get-tuple-element.80), channel_id=1, source_target_pairs={{0,4},{4,0},{8,12},{12,8},{16,20},{20,16},{24,28},{28,24},{32,36},... | collective-permute-start | bytes 41480 | tf_op jit(solution)/shard_map/ppermute | solution.py:370
  59.6 0.9 %shard_map.121 = (f32[9,40,128]{2,1,0:T(8,128)S(1)}, f32[64,1152]{1,0:T(8,128)S(1)}, bf16[32,4608]{1,0:T(8,128)(2,1)S(1)}) custom-call(f32[9,40,128]{2,1,0:T(8,128)S(1)} %get-tuple-element.65.middle, bf16[144,1152]{1,0:T(8,128)(2,1)S(1)} %get-tuple-element.66.x, f32[64,1152]{1,0:T(8,128)S(1)} %get-tuple-element.67.s, ...), custom_call_target="tpu_custom_call" | custom-call | flops 200000000 | bytes 2000000 | tf_op jit(solution)/shard_map/pallas_call | solution.py:348
  60.6 1.6 %shard_map.122 = f32[9,35,128]{2,1,0:T(8,128)} custom-call(f32[9,40,128]{2,1,0:T(8,128)S(1)} %get-tuple-element.71.held, f32[64,1152]{1,0:T(8,128)S(1)} %get-tuple-element.72.own, bf16[32,4608]{1,0:T(8,128)(2,1)S(1)} %get-tuple-element.73.near, bf16[80,512]{1,0:T(8,128)(2,1)S(1)} %get-tuple-element.50.hot, s32[24,128]{1,0:T(8,128)S(1)} %concatenate.3.marks, ...), custom_call_target="tpu_custom_call" | custom-call | flops 100000000 | bytes 2000000 | tf_op jit(solution)/shard_map/pallas_call | solution.py:348
  (35 shorter events, 0.1 us)
Async XLA Ops:
  0.0 1.1 %copy-start.9 = (s32[2,16]{1,0:T(2,128)S(1)}, s32[2,16]{1,0:T(2,128)}, u32[]{:S(2)}) copy-start(s32[2,16]{1,0:T(2,128)} %param.19) | copy-start | bytes 388
  0.0 1.2 %copy-start = (f32[9,35,128]{2,1,0:T(8,128)S(1)}, f32[9,35,128]{2,1,0:T(8,128)}, u32[]{:S(2)}) copy-start(f32[9,35,128]{2,1,0:T(8,128)} %state.3) | copy-start | bytes 483844
  0.0 1.1 %copy-start.6 = (s32[1,1024]{1,0:T(1,128)S(1)}, s32[1,1024]{1,0:T(1,128)}, u32[]{:S(2)}) copy-start(s32[1,1024]{1,0:T(1,128)} %param.18) | copy-start | bytes 12292
  0.0 1.1 %copy-start.7 = (s32[4,128]{1,0:T(4,128)S(1)}, s32[4,128]{1,0:T(4,128)}, u32[]{:S(2)}) copy-start(s32[4,128]{1,0:T(4,128)} %param.16) | copy-start | bytes 6148
  0.0 1.1 %copy-start.8 = (s32[4,128]{1,0:T(4,128)S(1)}, s32[4,128]{1,0:T(4,128)}, u32[]{:S(2)}) copy-start(s32[4,128]{1,0:T(4,128)} %param.17) | copy-start | bytes 6148
  0.0 1.1 %copy-start.10 = (s32[128]{0:T(128)S(1)}, s32[128]{0:T(128)}, u32[]{:S(2)}) copy-start(s32[128]{0:T(128)} %param.15) | copy-start | bytes 1540
  0.0 1.2 %copy-start.1 = (f32[3,35,35]{2,1,0:T(8,128)S(1)}, f32[3,35,35]{2,1,0:T(8,128)}, u32[]{:S(2)}) copy-start(f32[3,35,35]{2,1,0:T(8,128)} %stiffness.3) | copy-start | bytes 44104
  1.9 31.2 %copy-start.2 = (bf16[2,4,9,9,128]{4,1,3,2,0:T(4,128)(2,1)S(1)}, bf16[2,4,9,9,128]{4,1,3,2,0:T(4,128)(2,1)}, u32[]{:S(2)}) copy-start(bf16[2,4,9,9,128]{4,1,3,2,0:T(4,128)(2,1)} %param.14) | copy-start | bytes 497668
  1.9 31.2 %copy-start.4 = (f32[4,35,15]{1,0,2:T(4,128)S(1)}, f32[4,35,15]{1,0,2:T(4,128)}, u32[]{:S(2)}) copy-start(f32[4,35,15]{1,0,2:T(4,128)} %param.22) | copy-start | bytes 25204
  1.9 31.2 %copy-start.5 = (f32[3,15,15]{2,1,0:T(8,128)S(1)}, f32[3,15,15]{2,1,0:T(8,128)}, u32[]{:S(2)}) copy-start(f32[3,15,15]{2,1,0:T(8,128)} %rotations.1) | copy-start | bytes 8104
  3.7 24.7 %collective-permute-start = (f32[8,144]{1,0:T(8,128)S(1)}, f32[8,144]{1,0:T(8,128)S(1)}, u32[]{:S(2)}, u32[]{:S(2)}) collective-permute-start(f32[8,144]{1,0:T(8,128)S(1)} %get-tuple-element.58), channel_id=1, source_target_pairs={{0,508},{508,0},{8,4},{4,8},{16,12},{12,16},{24,20},{20,24},{32,28... | collective-permute-start | bytes 13832 | tf_op jit(solution)/shard_map/ppermute | solution.py:370
  8.6 20.4 %collective-permute-start.1 = (f32[8,144]{1,0:T(8,128)S(1)}, f32[8,144]{1,0:T(8,128)S(1)}, u32[]{:S(2)}, u32[]{:S(2)}) collective-permute-start(f32[8,144]{1,0:T(8,128)S(1)} %get-tuple-element.59), channel_id=1, source_target_pairs={{0,12},{12,0},{8,20},{20,8},{16,28},{28,16},{24,36},{36,24},{32,44... | collective-permute-start | bytes 13832 | tf_op jit(solution)/shard_map/ppermute | solution.py:370
  21.0 13.1 %collective-permute-start.2 = (f32[8,144]{1,0:T(8,128)S(1)}, f32[8,144]{1,0:T(8,128)S(1)}, u32[]{:S(2)}, u32[]{:S(2)}) collective-permute-start(f32[8,144]{1,0:T(8,128)S(1)} %get-tuple-element.60), channel_id=1, source_target_pairs={{0,500},{500,0},{8,508},{508,8},{16,4},{4,16},{24,12},{12,24},{32,... | collective-permute-start | bytes 13832 | tf_op jit(solution)/shard_map/ppermute | solution.py:370
  22.9 11.2 %collective-permute-start.3 = (f32[8,144]{1,0:T(8,128)S(1)}, f32[8,144]{1,0:T(8,128)S(1)}, u32[]{:S(2)}, u32[]{:S(2)}) collective-permute-start(f32[8,144]{1,0:T(8,128)S(1)} %get-tuple-element.61), channel_id=1, source_target_pairs={{0,256},{4,260},{8,264},{12,268},{16,272},{20,276},{24,280},{28,28... | collective-permute-start | bytes 13832 | tf_op jit(solution)/shard_map/ppermute | solution.py:370
  25.2 9.0 %collective-permute-start.4 = (f32[16,144]{1,0:T(8,128)S(1)}, f32[16,144]{1,0:T(8,128)S(1)}, u32[]{:S(2)}, u32[]{:S(2)}) collective-permute-start(f32[16,144]{1,0:T(8,128)S(1)} %get-tuple-element.62), channel_id=1, source_target_pairs={{0,1},{1,0},{2,3},{3,2},{4,5},{5,4},{6,7},{7,6},{8,9},{9,8},{10,11... | collective-permute-start | bytes 27656 | tf_op jit(solution)/shard_map/ppermute | solution.py:376
  28.3 5.8 %collective-permute-start.5 = (f32[16,144]{1,0:T(8,128)S(1)}, f32[16,144]{1,0:T(8,128)S(1)}, u32[]{:S(2)}, u32[]{:S(2)}) collective-permute-start(f32[16,144]{1,0:T(8,128)S(1)} %get-tuple-element.63), channel_id=1, source_target_pairs={{1,2},{2,1},{5,6},{6,5},{9,10},{10,9},{13,14},{14,13},{17,18},{18,... | collective-permute-start | bytes 27656 | tf_op jit(solution)/shard_map/ppermute | solution.py:376
  29.0 5.2 %collective-permute-start.6 = (f32[24,144]{1,0:T(8,128)S(1)}, f32[24,144]{1,0:T(8,128)S(1)}, u32[]{:S(2)}, u32[]{:S(2)}) collective-permute-start(f32[24,144]{1,0:T(8,128)S(1)} %get-tuple-element.64), channel_id=1, source_target_pairs={{0,4},{4,0},{8,12},{12,8},{16,20},{20,16},{24,28},{28,24},{32,36},... | collective-permute-start | bytes 41480 | tf_op jit(solution)/shard_map/ppermute | solution.py:370
  36.7 18.4 %collective-permute-start.7 = (f32[8,144]{1,0:T(8,128)S(1)}, f32[8,144]{1,0:T(8,128)S(1)}, u32[]{:S(2)}, u32[]{:S(2)}) collective-permute-start(f32[8,144]{1,0:T(8,128)S(1)} %get-tuple-element.74), channel_id=1, source_target_pairs={{0,508},{508,0},{8,4},{4,8},{16,12},{12,16},{24,20},{20,24},{32,28... | collective-permute-start | bytes 13832 | tf_op jit(solution)/shard_map/ppermute | solution.py:370
  39.3 16.5 %collective-permute-start.8 = (f32[8,144]{1,0:T(8,128)S(1)}, f32[8,144]{1,0:T(8,128)S(1)}, u32[]{:S(2)}, u32[]{:S(2)}) collective-permute-start(f32[8,144]{1,0:T(8,128)S(1)} %get-tuple-element.75), channel_id=1, source_target_pairs={{0,12},{12,0},{8,20},{20,8},{16,28},{28,16},{24,36},{36,24},{32,44... | collective-permute-start | bytes 13832 | tf_op jit(solution)/shard_map/ppermute | solution.py:370
  44.1 16.5 %collective-permute-start.9 = (f32[8,144]{1,0:T(8,128)S(1)}, f32[8,144]{1,0:T(8,128)S(1)}, u32[]{:S(2)}, u32[]{:S(2)}) collective-permute-start(f32[8,144]{1,0:T(8,128)S(1)} %get-tuple-element.76), channel_id=1, source_target_pairs={{0,500},{500,0},{8,508},{508,8},{16,4},{4,16},{24,12},{12,24},{32,... | collective-permute-start | bytes 13832 | tf_op jit(solution)/shard_map/ppermute | solution.py:370
  46.7 13.9 %collective-permute-start.10 = (f32[8,144]{1,0:T(8,128)S(1)}, f32[8,144]{1,0:T(8,128)S(1)}, u32[]{:S(2)}, u32[]{:S(2)}) collective-permute-start(f32[8,144]{1,0:T(8,128)S(1)} %get-tuple-element.77), channel_id=1, source_target_pairs={{0,256},{4,260},{8,264},{12,268},{16,272},{20,276},{24,280},{28,28... | collective-permute-start | bytes 13832 | tf_op jit(solution)/shard_map/ppermute | solution.py:370
  49.8 10.8 %collective-permute-start.11 = (f32[16,144]{1,0:T(8,128)S(1)}, f32[16,144]{1,0:T(8,128)S(1)}, u32[]{:S(2)}, u32[]{:S(2)}) collective-permute-start(f32[16,144]{1,0:T(8,128)S(1)} %get-tuple-element.78), channel_id=1, source_target_pairs={{0,1},{1,0},{2,3},{3,2},{4,5},{5,4},{6,7},{7,6},{8,9},{9,8},{10,11... | collective-permute-start | bytes 27656 | tf_op jit(solution)/shard_map/ppermute | solution.py:376
  55.1 5.5 %collective-permute-start.12 = (f32[16,144]{1,0:T(8,128)S(1)}, f32[16,144]{1,0:T(8,128)S(1)}, u32[]{:S(2)}, u32[]{:S(2)}) collective-permute-start(f32[16,144]{1,0:T(8,128)S(1)} %get-tuple-element.79), channel_id=1, source_target_pairs={{1,2},{2,1},{5,6},{6,5},{9,10},{10,9},{13,14},{14,13},{17,18},{18,... | collective-permute-start | bytes 27656 | tf_op jit(solution)/shard_map/ppermute | solution.py:376
  55.8 4.8 %collective-permute-start.13 = (f32[24,144]{1,0:T(8,128)S(1)}, f32[24,144]{1,0:T(8,128)S(1)}, u32[]{:S(2)}, u32[]{:S(2)}) collective-permute-start(f32[24,144]{1,0:T(8,128)S(1)} %get-tuple-element.80), channel_id=1, source_target_pairs={{0,4},{4,0},{8,12},{12,8},{16,20},{20,16},{24,28},{28,24},{32,36},... | collective-permute-start | bytes 41480 | tf_op jit(solution)/shard_map/ppermute | solution.py:370
  (1 other events, 0.8 us)

commit v6 on v3

--- a/solution.py
+++ b/solution.py
@@ -10,7 +10,7 @@
 E = 128
 PAD = 48
 AP = 16
-THICK, PLANE = 9, 16
+THICK, PLANE = 9, 11
 SLOT, LAY = 8, 16
 CUTS = 5 * SLOT + 2 * LAY
 CP = 80
@@ -399,7 +399,6 @@
             orient,
             cluster.reshape(1, E),
             jnp.pad(thick, ((0, 0), (0, E - LAY))),
-            jnp.zeros((PLANE - THICK - 2, E), jnp.int32),
             plane.reshape(-1, E),
         ],
         axis=0,

time: 62.8 us -> 63.5 us (1.011)
  local copies, waits for them, and re-layouts: 0.73 us -> 1.54 us
    concatenate x1, local copies, waits for them, and re-layouts: 0.04 us -> 0.81 us  [body(): jnp.concatenate([neighbour, orient, cluster.reshape(1, E), jnp.pad(thick,...]
    pad x1, local copies, waits for them, and re-layouts: 0.01 us -> 0.69 us  [body(): jnp.pad(thick, ((0, 0), (0, E - LAY)))]
where the time goes in v6:
time: 63.5 us; the launch traced here: 62.9 us
  starting transfers between devices  52.2 us (82%)
  Pallas kernels  7.91 us (12%)
  local copies, waits for them, and re-layouts  1.54 us (2%)
  other arithmetic  0.96 us (2%)
    ppermute x10, starting transfers between devices, along_dom(): return lax.ppermute(block, 'dom', pairs)  42.4 us
    ppermute x4, starting transfers between devices, along_ply(): return lax.ppermute(block, 'ply', pairs)  9.73 us
    pallas_call x5, Pallas kernels, call(): pl.pallas_call(kernel, out_shape=outs, in_specs=[vmem] * len(operands), o...  7.91 us
  transfers between devices with their start and end apart: 14, of which 0 were waited for; matrix products, arithmetic and copies ran while one was open for 0% of the time, Pallas kernels for 3%

profile of v6, /device:TPU:1, one launch (start us, length us, event | category | flops | bytes accessed | tf_op | source)
XLA Modules:
  0.0 62.9 jit_solution(6720670042026915647)
XLA Ops:
  0.0 1.0 %convert_element_type.11 = f32[3,9,9,128]{3,0,2,1:T(4,128)S(1)} convert(bf16[3,9,9,128]{3,0,2,1:T(4,128)(2,1)} %param.13) | non-fusion elementwise | flops 31104 | bytes 186624 | tf_op jit(solution)/shard_map/convert_element_type | solution.py:392
  1.0 0.0 copy-start.3
  1.0 0.7 %pad.4 = s32[2,128]{1,0:T(2,128)S(1)} pad(s32[2,16]{1,0:T(2,128)} %param.19, s32[]{:T(128)} %constant.0.clone.1), padding=0_0x0_112 | pad | bytes 1156 | tf_op jit(solution)/shard_map/jit(_pad)/pad | solution.py:401
  1.7 0.8 %concatenate.3.marks = s32[19,128]{1,0:T(8,128)S(1)} concatenate(s32[4,128]{1,0:T(4,128)} %param.16, s32[4,128]{1,0:T(4,128)} %param.17, s32[1,128]{1,0:T(1,128)S(1)} %bitcast.18, s32[2,128]{1,0:T(2,128)S(1)} %pad.4, s32[8,128]{1,0:T(8,128)S(1)} %bitcast.17), dimensions={0} | concatenate | bytes 19456 | tf_op jit(solution)/shard_map/concatenate | solution.py:396
  2.6 0.0 copy-start.5
  2.6 1.8 %shard_map.118 = (bf16[144,1152]{1,0:T(8,128)(2,1)S(1)}, f32[64,1152]{1,0:T(8,128)S(1)}, f32[9,40,128]{2,1,0:T(8,128)S(1)}, bf16[80,512]{1,0:T(8,128)(2,1)S(1)},...) custom-call(f32[9,35,128]{2,1,0:T(8,128)S(1)} %copy-done, ...), custom_call_target="tpu_custom_call" | custom-call | flops 100000000 | bytes 2000000 | tf_op jit(solution)/shard_map/pallas_call | solution.py:353
  4.3 4.9 %collective-permute-start = (f32[8,144]{1,0:T(8,128)S(1)}, f32[8,144]{1,0:T(8,128)S(1)}, u32[]{:S(2)}, u32[]{:S(2)}) collective-permute-start(f32[8,144]{1,0:T(8,128)S(1)} %get-tuple-element.58), channel_id=1, source_target_pairs={{0,508},{508,0},{8,4},{4,8},{16,12},{12,16},{24,20},{20,24},{32,28... | collective-permute-start | bytes 13832 | tf_op jit(solution)/shard_map/ppermute | solution.py:375
  9.3 12.4 %collective-permute-start.1 = (f32[8,144]{1,0:T(8,128)S(1)}, f32[8,144]{1,0:T(8,128)S(1)}, u32[]{:S(2)}, u32[]{:S(2)}) collective-permute-start(f32[8,144]{1,0:T(8,128)S(1)} %get-tuple-element.59), channel_id=1, source_target_pairs={{0,12},{12,0},{8,20},{20,8},{16,28},{28,16},{24,36},{36,24},{32,44... | collective-permute-start | bytes 13832 | tf_op jit(solution)/shard_map/ppermute | solution.py:375
  21.7 1.9 %collective-permute-start.2 = (f32[8,144]{1,0:T(8,128)S(1)}, f32[8,144]{1,0:T(8,128)S(1)}, u32[]{:S(2)}, u32[]{:S(2)}) collective-permute-start(f32[8,144]{1,0:T(8,128)S(1)} %get-tuple-element.60), channel_id=1, source_target_pairs={{0,500},{500,0},{8,508},{508,8},{16,4},{4,16},{24,12},{12,24},{32,... | collective-permute-start | bytes 13832 | tf_op jit(solution)/shard_map/ppermute | solution.py:375
  23.6 2.3 %collective-permute-start.3 = (f32[8,144]{1,0:T(8,128)S(1)}, f32[8,144]{1,0:T(8,128)S(1)}, u32[]{:S(2)}, u32[]{:S(2)}) collective-permute-start(f32[8,144]{1,0:T(8,128)S(1)} %get-tuple-element.61), channel_id=1, source_target_pairs={{0,256},{4,260},{8,264},{12,268},{16,272},{20,276},{24,280},{28,28... | collective-permute-start | bytes 13832 | tf_op jit(solution)/shard_map/ppermute | solution.py:375
  25.9 3.1 %collective-permute-start.4 = (f32[16,144]{1,0:T(8,128)S(1)}, f32[16,144]{1,0:T(8,128)S(1)}, u32[]{:S(2)}, u32[]{:S(2)}) collective-permute-start(f32[16,144]{1,0:T(8,128)S(1)} %get-tuple-element.62), channel_id=1, source_target_pairs={{0,1},{1,0},{2,3},{3,2},{4,5},{5,4},{6,7},{7,6},{8,9},{9,8},{10,11... | collective-permute-start | bytes 27656 | tf_op jit(solution)/shard_map/ppermute | solution.py:381
  29.0 0.7 %collective-permute-start.5 = (f32[16,144]{1,0:T(8,128)S(1)}, f32[16,144]{1,0:T(8,128)S(1)}, u32[]{:S(2)}, u32[]{:S(2)}) collective-permute-start(f32[16,144]{1,0:T(8,128)S(1)} %get-tuple-element.63), channel_id=1, source_target_pairs={{1,2},{2,1},{5,6},{6,5},{9,10},{10,9},{13,14},{14,13},{17,18},{18,... | collective-permute-start | bytes 27656 | tf_op jit(solution)/shard_map/ppermute | solution.py:381
  29.7 4.0 %collective-permute-start.6 = (f32[24,144]{1,0:T(8,128)S(1)}, f32[24,144]{1,0:T(8,128)S(1)}, u32[]{:S(2)}, u32[]{:S(2)}) collective-permute-start(f32[24,144]{1,0:T(8,128)S(1)} %get-tuple-element.64), channel_id=1, source_target_pairs={{0,4},{4,0},{8,12},{12,8},{16,20},{20,16},{24,28},{28,24},{32,36},... | collective-permute-start | bytes 41480 | tf_op jit(solution)/shard_map/ppermute | solution.py:375
  33.7 1.1 %shard_map.119 = (f32[9,40,128]{2,1,0:T(8,128)S(1)}, f32[64,1152]{1,0:T(8,128)S(1)}, bf16[32,4608]{1,0:T(8,128)(2,1)S(1)}, f32[162,4,128]{2,1,0:T(4,128)S(1)}, b...) custom-call(f32[9,35,128]{2,1,0:T(8,128)S(1)} %copy-done, ...), custom_call_target="tpu_custom_call" | custom-call | flops 200000000 | bytes 2000000 | tf_op jit(solution)/shard_map/pallas_call | solution.py:353
  34.9 2.5 %shard_map.120 = (f32[9,40,128]{2,1,0:T(8,128)S(1)}, bf16[144,1152]{1,0:T(8,128)(2,1)S(1)}, f32[64,1152]{1,0:T(8,128)S(1)}, bf16[288,512]{1,0:T(8,128)(2,1)S(1)}...) custom-call(f32[9,40,128]{2,1,0:T(8,128)S(1)} %get-tuple-element.46., ...), custom_call_target="tpu_custom_call" | custom-call | flops 200000000 | bytes 2000000 | tf_op jit(solution)/shard_map/pallas_call | solution.py:353
  37.4 2.5 %collective-permute-start.7 = (f32[8,144]{1,0:T(8,128)S(1)}, f32[8,144]{1,0:T(8,128)S(1)}, u32[]{:S(2)}, u32[]{:S(2)}) collective-permute-start(f32[8,144]{1,0:T(8,128)S(1)} %get-tuple-element.74), channel_id=1, source_target_pairs={{0,508},{508,0},{8,4},{4,8},{16,12},{12,16},{24,20},{20,24},{32,28... | collective-permute-start | bytes 13832 | tf_op jit(solution)/shard_map/ppermute | solution.py:375
  40.0 4.8 %collective-permute-start.8 = (f32[8,144]{1,0:T(8,128)S(1)}, f32[8,144]{1,0:T(8,128)S(1)}, u32[]{:S(2)}, u32[]{:S(2)}) collective-permute-start(f32[8,144]{1,0:T(8,128)S(1)} %get-tuple-element.75), channel_id=1, source_target_pairs={{0,12},{12,0},{8,20},{20,8},{16,28},{28,16},{24,36},{36,24},{32,44... | collective-permute-start | bytes 13832 | tf_op jit(solution)/shard_map/ppermute | solution.py:375
  44.8 2.6 %collective-permute-start.9 = (f32[8,144]{1,0:T(8,128)S(1)}, f32[8,144]{1,0:T(8,128)S(1)}, u32[]{:S(2)}, u32[]{:S(2)}) collective-permute-start(f32[8,144]{1,0:T(8,128)S(1)} %get-tuple-element.76), channel_id=1, source_target_pairs={{0,500},{500,0},{8,508},{508,8},{16,4},{4,16},{24,12},{12,24},{32,... | collective-permute-start | bytes 13832 | tf_op jit(solution)/shard_map/ppermute | solution.py:375
  47.4 3.1 %collective-permute-start.10 = (f32[8,144]{1,0:T(8,128)S(1)}, f32[8,144]{1,0:T(8,128)S(1)}, u32[]{:S(2)}, u32[]{:S(2)}) collective-permute-start(f32[8,144]{1,0:T(8,128)S(1)} %get-tuple-element.77), channel_id=1, source_target_pairs={{0,256},{4,260},{8,264},{12,268},{16,272},{20,276},{24,280},{28,28... | collective-permute-start | bytes 13832 | tf_op jit(solution)/shard_map/ppermute | solution.py:375
  50.5 5.3 %collective-permute-start.11 = (f32[16,144]{1,0:T(8,128)S(1)}, f32[16,144]{1,0:T(8,128)S(1)}, u32[]{:S(2)}, u32[]{:S(2)}) collective-permute-start(f32[16,144]{1,0:T(8,128)S(1)} %get-tuple-element.78), channel_id=1, source_target_pairs={{0,1},{1,0},{2,3},{3,2},{4,5},{5,4},{6,7},{7,6},{8,9},{9,8},{10,11... | collective-permute-start | bytes 27656 | tf_op jit(solution)/shard_map/ppermute | solution.py:381
  55.8 0.7 %collective-permute-start.12 = (f32[16,144]{1,0:T(8,128)S(1)}, f32[16,144]{1,0:T(8,128)S(1)}, u32[]{:S(2)}, u32[]{:S(2)}) collective-permute-start(f32[16,144]{1,0:T(8,128)S(1)} %get-tuple-element.79), channel_id=1, source_target_pairs={{1,2},{2,1},{5,6},{6,5},{9,10},{10,9},{13,14},{14,13},{17,18},{18,... | collective-permute-start | bytes 27656 | tf_op jit(solution)/shard_map/ppermute | solution.py:381
  56.5 3.8 %collective-permute-start.13 = (f32[24,144]{1,0:T(8,128)S(1)}, f32[24,144]{1,0:T(8,128)S(1)}, u32[]{:S(2)}, u32[]{:S(2)}) collective-permute-start(f32[24,144]{1,0:T(8,128)S(1)} %get-tuple-element.80), channel_id=1, source_target_pairs={{0,4},{4,0},{8,12},{12,8},{16,20},{20,16},{24,28},{28,24},{32,36},... | collective-permute-start | bytes 41480 | tf_op jit(solution)/shard_map/ppermute | solution.py:375
  60.3 1.0 %shard_map.121 = (f32[9,40,128]{2,1,0:T(8,128)S(1)}, f32[64,1152]{1,0:T(8,128)S(1)}, bf16[32,4608]{1,0:T(8,128)(2,1)S(1)}) custom-call(f32[9,40,128]{2,1,0:T(8,128)S(1)} %get-tuple-element.65.middle, bf16[144,1152]{1,0:T(8,128)(2,1)S(1)} %get-tuple-element.66.x, f32[64,1152]{1,0:T(8,128)S(1)} %get-tuple-element.67.s, ...), custom_call_target="tpu_custom_call" | custom-call | flops 200000000 | bytes 2000000 | tf_op jit(solution)/shard_map/pallas_call | solution.py:353
  61.4 1.6 %shard_map.122 = f32[9,35,128]{2,1,0:T(8,128)} custom-call(f32[9,40,128]{2,1,0:T(8,128)S(1)} %get-tuple-element.71.held, f32[64,1152]{1,0:T(8,128)S(1)} %get-tuple-element.72.own, bf16[32,4608]{1,0:T(8,128)(2,1)S(1)} %get-tuple-element.73.near, bf16[80,512]{1,0:T(8,128)(2,1)S(1)} %get-tuple-element.50.hot, s32[19,128]{1,0:T(8,128)S(1)} %concatenate.3.marks, ...), custom_call_target="tpu_custom_call" | custom-call | flops 100000000 | bytes 2000000 | tf_op jit(solution)/shard_map/pallas_call | solution.py:353
  (28 shorter events, 0.1 us)
Async XLA Ops:
  0.0 2.5 %copy-start = (f32[9,35,128]{2,1,0:T(8,128)S(1)}, f32[9,35,128]{2,1,0:T(8,128)}, u32[]{:S(2)}) copy-start(f32[9,35,128]{2,1,0:T(8,128)} %state.3) | copy-start | bytes 483844
  0.0 1.7 %copy-start.6 = (s32[1,1024]{1,0:T(1,128)S(1)}, s32[1,1024]{1,0:T(1,128)}, u32[]{:S(2)}) copy-start(s32[1,1024]{1,0:T(1,128)} %param.18) | copy-start | bytes 12292
  0.0 1.7 %copy-start.7 = (s32[128]{0:T(128)S(1)}, s32[128]{0:T(128)}, u32[]{:S(2)}) copy-start(s32[128]{0:T(128)} %param.15) | copy-start | bytes 1540
  0.0 2.5 %copy-start.1 = (f32[3,35,35]{2,1,0:T(8,128)S(1)}, f32[3,35,35]{2,1,0:T(8,128)}, u32[]{:S(2)}) copy-start(f32[3,35,35]{2,1,0:T(8,128)} %stiffness.3) | copy-start | bytes 44104
  1.0 1.5 %copy-start.3 = (f32[4,15,35]{2,0,1:T(4,128)S(1)}, f32[4,15,35]{2,0,1:T(4,128)}, u32[]{:S(2)}) copy-start(f32[4,15,35]{2,0,1:T(4,128)} %param.21) | copy-start | bytes 25204
  2.5 31.2 %copy-start.2 = (bf16[2,4,9,9,128]{4,1,3,2,0:T(4,128)(2,1)S(1)}, bf16[2,4,9,9,128]{4,1,3,2,0:T(4,128)(2,1)}, u32[]{:S(2)}) copy-start(bf16[2,4,9,9,128]{4,1,3,2,0:T(4,128)(2,1)} %param.14) | copy-start | bytes 497668
  2.5 31.2 %copy-start.4 = (f32[4,35,15]{1,0,2:T(4,128)S(1)}, f32[4,35,15]{1,0,2:T(4,128)}, u32[]{:S(2)}) copy-start(f32[4,35,15]{1,0,2:T(4,128)} %param.22) | copy-start | bytes 25204
  2.6 31.2 %copy-start.5 = (f32[3,15,15]{2,1,0:T(8,128)S(1)}, f32[3,15,15]{2,1,0:T(8,128)}, u32[]{:S(2)}) copy-start(f32[3,15,15]{2,1,0:T(8,128)} %rotations.1) | copy-start | bytes 8104
  4.3 24.7 %collective-permute-start = (f32[8,144]{1,0:T(8,128)S(1)}, f32[8,144]{1,0:T(8,128)S(1)}, u32[]{:S(2)}, u32[]{:S(2)}) collective-permute-start(f32[8,144]{1,0:T(8,128)S(1)} %get-tuple-element.58), channel_id=1, source_target_pairs={{0,508},{508,0},{8,4},{4,8},{16,12},{12,16},{24,20},{20,24},{32,28... | collective-permute-start | bytes 13832 | tf_op jit(solution)/shard_map/ppermute | solution.py:375
  9.3 20.4 %collective-permute-start.1 = (f32[8,144]{1,0:T(8,128)S(1)}, f32[8,144]{1,0:T(8,128)S(1)}, u32[]{:S(2)}, u32[]{:S(2)}) collective-permute-start(f32[8,144]{1,0:T(8,128)S(1)} %get-tuple-element.59), channel_id=1, source_target_pairs={{0,12},{12,0},{8,20},{20,8},{16,28},{28,16},{24,36},{36,24},{32,44... | collective-permute-start | bytes 13832 | tf_op jit(solution)/shard_map/ppermute | solution.py:375
  21.7 13.2 %collective-permute-start.2 = (f32[8,144]{1,0:T(8,128)S(1)}, f32[8,144]{1,0:T(8,128)S(1)}, u32[]{:S(2)}, u32[]{:S(2)}) collective-permute-start(f32[8,144]{1,0:T(8,128)S(1)} %get-tuple-element.60), channel_id=1, source_target_pairs={{0,500},{500,0},{8,508},{508,8},{16,4},{4,16},{24,12},{12,24},{32,... | collective-permute-start | bytes 13832 | tf_op jit(solution)/shard_map/ppermute | solution.py:375
  23.6 11.2 %collective-permute-start.3 = (f32[8,144]{1,0:T(8,128)S(1)}, f32[8,144]{1,0:T(8,128)S(1)}, u32[]{:S(2)}, u32[]{:S(2)}) collective-permute-start(f32[8,144]{1,0:T(8,128)S(1)} %get-tuple-element.61), channel_id=1, source_target_pairs={{0,256},{4,260},{8,264},{12,268},{16,272},{20,276},{24,280},{28,28... | collective-permute-start | bytes 13832 | tf_op jit(solution)/shard_map/ppermute | solution.py:375
  25.9 9.0 %collective-permute-start.4 = (f32[16,144]{1,0:T(8,128)S(1)}, f32[16,144]{1,0:T(8,128)S(1)}, u32[]{:S(2)}, u32[]{:S(2)}) collective-permute-start(f32[16,144]{1,0:T(8,128)S(1)} %get-tuple-element.62), channel_id=1, source_target_pairs={{0,1},{1,0},{2,3},{3,2},{4,5},{5,4},{6,7},{7,6},{8,9},{9,8},{10,11... | collective-permute-start | bytes 27656 | tf_op jit(solution)/shard_map/ppermute | solution.py:381
  29.0 5.9 %collective-permute-start.5 = (f32[16,144]{1,0:T(8,128)S(1)}, f32[16,144]{1,0:T(8,128)S(1)}, u32[]{:S(2)}, u32[]{:S(2)}) collective-permute-start(f32[16,144]{1,0:T(8,128)S(1)} %get-tuple-element.63), channel_id=1, source_target_pairs={{1,2},{2,1},{5,6},{6,5},{9,10},{10,9},{13,14},{14,13},{17,18},{18,... | collective-permute-start | bytes 27656 | tf_op jit(solution)/shard_map/ppermute | solution.py:381
  29.7 5.2 %collective-permute-start.6 = (f32[24,144]{1,0:T(8,128)S(1)}, f32[24,144]{1,0:T(8,128)S(1)}, u32[]{:S(2)}, u32[]{:S(2)}) collective-permute-start(f32[24,144]{1,0:T(8,128)S(1)} %get-tuple-element.64), channel_id=1, source_target_pairs={{0,4},{4,0},{8,12},{12,8},{16,20},{20,16},{24,28},{28,24},{32,36},... | collective-permute-start | bytes 41480 | tf_op jit(solution)/shard_map/ppermute | solution.py:375
  37.4 18.4 %collective-permute-start.7 = (f32[8,144]{1,0:T(8,128)S(1)}, f32[8,144]{1,0:T(8,128)S(1)}, u32[]{:S(2)}, u32[]{:S(2)}) collective-permute-start(f32[8,144]{1,0:T(8,128)S(1)} %get-tuple-element.74), channel_id=1, source_target_pairs={{0,508},{508,0},{8,4},{4,8},{16,12},{12,16},{24,20},{20,24},{32,28... | collective-permute-start | bytes 13832 | tf_op jit(solution)/shard_map/ppermute | solution.py:375
  40.0 16.5 %collective-permute-start.8 = (f32[8,144]{1,0:T(8,128)S(1)}, f32[8,144]{1,0:T(8,128)S(1)}, u32[]{:S(2)}, u32[]{:S(2)}) collective-permute-start(f32[8,144]{1,0:T(8,128)S(1)} %get-tuple-element.75), channel_id=1, source_target_pairs={{0,12},{12,0},{8,20},{20,8},{16,28},{28,16},{24,36},{36,24},{32,44... | collective-permute-start | bytes 13832 | tf_op jit(solution)/shard_map/ppermute | solution.py:375
  44.8 16.5 %collective-permute-start.9 = (f32[8,144]{1,0:T(8,128)S(1)}, f32[8,144]{1,0:T(8,128)S(1)}, u32[]{:S(2)}, u32[]{:S(2)}) collective-permute-start(f32[8,144]{1,0:T(8,128)S(1)} %get-tuple-element.76), channel_id=1, source_target_pairs={{0,500},{500,0},{8,508},{508,8},{16,4},{4,16},{24,12},{12,24},{32,... | collective-permute-start | bytes 13832 | tf_op jit(solution)/shard_map/ppermute | solution.py:375
  47.4 13.9 %collective-permute-start.10 = (f32[8,144]{1,0:T(8,128)S(1)}, f32[8,144]{1,0:T(8,128)S(1)}, u32[]{:S(2)}, u32[]{:S(2)}) collective-permute-start(f32[8,144]{1,0:T(8,128)S(1)} %get-tuple-element.77), channel_id=1, source_target_pairs={{0,256},{4,260},{8,264},{12,268},{16,272},{20,276},{24,280},{28,28... | collective-permute-start | bytes 13832 | tf_op jit(solution)/shard_map/ppermute | solution.py:375
  50.5 10.8 %collective-permute-start.11 = (f32[16,144]{1,0:T(8,128)S(1)}, f32[16,144]{1,0:T(8,128)S(1)}, u32[]{:S(2)}, u32[]{:S(2)}) collective-permute-start(f32[16,144]{1,0:T(8,128)S(1)} %get-tuple-element.78), channel_id=1, source_target_pairs={{0,1},{1,0},{2,3},{3,2},{4,5},{5,4},{6,7},{7,6},{8,9},{9,8},{10,11... | collective-permute-start | bytes 27656 | tf_op jit(solution)/shard_map/ppermute | solution.py:381
  55.8 5.5 %collective-permute-start.12 = (f32[16,144]{1,0:T(8,128)S(1)}, f32[16,144]{1,0:T(8,128)S(1)}, u32[]{:S(2)}, u32[]{:S(2)}) collective-permute-start(f32[16,144]{1,0:T(8,128)S(1)} %get-tuple-element.79), channel_id=1, source_target_pairs={{1,2},{2,1},{5,6},{6,5},{9,10},{10,9},{13,14},{14,13},{17,18},{18,... | collective-permute-start | bytes 27656 | tf_op jit(solution)/shard_map/ppermute | solution.py:381
  56.5 4.8 %collective-permute-start.13 = (f32[24,144]{1,0:T(8,128)S(1)}, f32[24,144]{1,0:T(8,128)S(1)}, u32[]{:S(2)}, u32[]{:S(2)}) collective-permute-start(f32[24,144]{1,0:T(8,128)S(1)} %get-tuple-element.80), channel_id=1, source_target_pairs={{0,4},{4,0},{8,12},{12,8},{16,20},{20,16},{24,28},{28,24},{32,36},... | collective-permute-start | bytes 41480 | tf_op jit(solution)/shard_map/ppermute | solution.py:375
